TPU v7x, 512 devices: a whole 4x4x16 slice. The times are simulated.
512 devices in a mesh: dom: 512 (over z, y, x, core).
Axes of the slice: x: 4, y: 4, z: 16, core: 2. Of those that a mesh axis runs over, the one named last changes fastest.
Arguments:
- dofs: float32 [56, 9, 65536], P(None, None, 'dom'), may hold values from -6 to 6
- star: float32 [3, 9, 9, 65536], P(None, None, None, 'dom'), may hold values from -5 to 5
- flux_self: float32 [4, 9, 9, 65536], P(None, None, None, 'dom'), may hold values from -0.5 to 0.5
- flux_other: float32 [4, 9, 9, 65536], P(None, None, None, 'dom'), may hold values from -0.5 to 0.5
- labels: int32 [65536], P('dom'), may hold values from 0 to 1, as said below
- neighbour_source: int32 [4, 65536], P(None, 'dom'), may hold values from 0 to 607, as said below
- orientation: int32 [4, 65536], P(None, 'dom'), may hold values from 0 to 2
- fine_send: int32 [4, 6144], P(None, 'dom'), may hold values from 0 to 511, as said below
- coarse_send: int32 [4, 6144], P(None, 'dom'), may hold values from 0 to 511, as said below
- stiff_time: float32 [3, 35, 56], replicated, may hold values from -2 to 2
- stiff_vol: float32 [3, 56, 35], replicated, may hold values from -0.109375 to 0.109375
- face_back: float32 [4, 21, 56], replicated, may hold values from -0.75 to 0.75
- face_front: float32 [4, 56, 21], replicated, may hold values from -1.25 to 1.25
- face_turn: float32 [3, 21, 21], replicated, may hold values from -1.25 to 1.25
Outputs:
- new_dofs: float32 [56, 9, 65536], P(None, None, 'dom')
Inputs may be any that keep to these rules, and one draw needn't show every extreme that they name: `labels`: each partition holds 1 to 64 elements of label 1, exactly 64 on some partition. `neighbour_source`: below 512, the value names face value // 128 of local element value % 128; above, a received slot of the source table; every received slot of a partition is named by exactly one of its faces. `fine_send`: each entry is j * 128 + e with e a local element of label 1 and j one of its faces. `coarse_send`: each entry is j * 128 + e with e a local element of label 0 and j one of its faces.
All inputs are finite; a program needn't handle non-finite values.
Results may differ from a plain program's by a relative error of at most 0.0003.
Values sent between devices are 32-bit elements; how exact they have to be, the bound alone decides.
No kernel may reach another device: no remote copies, remote signals or barrier semaphores. Data moves between devices by JAX's collectives and lax.ppermute only.
A program may use at most 128 MiB of HBM per device.

v0:
```python
import functools
import math

import jax
import jax.numpy as jnp
from jax import lax
from jax.experimental import pallas as pl
from jax.experimental.pallas import tpu as pltpu
from jax.sharding import PartitionSpec as P

ORDER = 6
SUBSTEPS = 4
NQ = 9
NB = 56
NLOW = 35
NF = 21
PEERS = 4
SLOTS = 12
LANES = 128
FPAD = 24
VPAD = 40
BOTH = 2 * SLOTS
WIDTH = 256
COLS = NQ * LANES
FACES = 4 * LANES
REM = 12 * FPAD
OWN = 4 * FPAD
DEEP = REM + OWN + 3 * VPAD
LEVELS = [(0, 35, 40, 56), (120, 20, 24, 40), (192, 10, 16, 24), (240, 4, 8, 16), (264, 1, 8, 8)]
BACK = 288
CHAIN_ROWS = BACK + OWN
HIGH = lax.Precision.HIGH
HIGHEST = lax.Precision.HIGHEST
F32 = jnp.float32
BF16 = jnp.bfloat16


def taylor_weights(start, stop):
    return [
        (stop ** (depth + 1) - start ** (depth + 1)) / math.factorial(depth + 1)
        for depth in range(ORDER)
    ]


def lanes(index):
    return slice(index * LANES, (index + 1) * LANES)


def iota(shape, dim):
    return lax.broadcasted_iota(jnp.int32, shape, dim)


def halves(value):
    top = value.astype(BF16)
    return top, (value - top.astype(F32)).astype(BF16)


def pick(value, hot, contract=((1,), (0,))):
    top, rest = halves(value)
    dims = (contract, ((), ()))
    return lax.dot_general(top, hot, dims, preferred_element_type=F32) + lax.dot_general(
        rest, hot, dims, preferred_element_type=F32
    )


def products(blocks, row_of, rows):
    totals = [None] * NQ
    for position, block in enumerate(blocks):
        for q in range(NQ):
            left = block(q)
            for p in range(NQ):
                term = left * row_of(position, q, p)
                totals[p] = term if totals[p] is None else totals[p] + term
    return totals


def chain_weights(stiff_time, face_back, out):
    out[...] = jnp.zeros(out.shape, F32)
    for start, valid, padded, _ in LEVELS:
        for d in range(3):
            out[start + d * padded : start + d * padded + valid, 0:NB] = stiff_time[d, 0:valid, :]
    for j in range(4):
        out[BACK + j * FPAD : BACK + j * FPAD + NF, 0:NB] = face_back[j]


def chain_of(first, star, weights, terms):
    now = first
    chain = [first]
    offset = 0
    for start, _, padded, width in LEVELS:
        terms[0 : 3 * padded, :] = jnp.dot(
            weights[start : start + 3 * padded, 0:width],
            now,
            precision=HIGH,
            preferred_element_type=F32,
        )
        blocks = [
            lambda q, d=d: terms[d * padded : (d + 1) * padded, lanes(q)] for d in range(3)
        ]
        totals = products(blocks, lambda d, q, p: star[d, q, p : p + 1, :], padded)
        now = jnp.concatenate(totals, axis=1)
        chain.append(now)
    return chain


def integral_of(chain, weights):
    pieces = []
    edges = [0, 8, 16, 24, 40, 56]
    for low, high in zip(edges[:-1], edges[1:]):
        total = None
        for depth in range(ORDER):
            if chain[depth].shape[0] < high:
                continue
            term = (weights[depth] * (-1) ** depth) * chain[depth][low:high]
            total = term if total is None else total + term
        pieces.append(total)
    return jnp.concatenate(pieces, axis=0)


def face_table(faces):
    rows = []
    for q in range(NQ):
        rows.append(
            jnp.concatenate(
                [faces[j * FPAD : (j + 1) * FPAD, lanes(q)] for j in range(4)], axis=1
            )
        )
    rows.append(jnp.zeros((WIDTH - NQ * FPAD, FACES), F32))
    return jnp.concatenate(rows, axis=0)


def project_and_send(integral, weights, lists, odd, faces_out, pair_out, far_out):
    faces = jnp.dot(
        weights[BACK : BACK + OWN, 0:NB], integral, precision=HIGH, preferred_element_type=F32
    )
    faces_out[...] = faces
    top, rest = halves(face_table(faces))
    hot = jnp.where(lists[...] == iota((PEERS * BOTH, FACES), 1), 1.0, 0.0).astype(BF16)
    dims = (((1,), (1,)), ((), ()))
    sent = lax.dot_general(hot, top, dims, preferred_element_type=F32) + lax.dot_general(
        hot, rest, dims, preferred_element_type=F32
    )
    first, second = sent[0:BOTH], sent[BOTH : 2 * BOTH]
    pair_out[0:BOTH, :] = jnp.where(odd, second, first)
    pair_out[BOTH : 2 * BOTH, :] = jnp.where(odd, first, second)
    far_out[...] = sent[2 * BOTH : 4 * BOTH]


def first_kernel(
    place, dofs, star, stiff_time, face_back, lists,
    state_out, low_out, coarse_out, faces_out, pair_out, far_out, weights_out, terms,
):
    odd = lax.rem(place[0], 2) == 1
    chain_weights(stiff_time, face_back, weights_out)
    state = jnp.concatenate([dofs[:, q, :] for q in range(NQ)], axis=1)
    state_out[...] = state
    chain = chain_of(state, star, weights_out, terms)
    integral = integral_of(chain, taylor_weights(0.0, 1.0 / SUBSTEPS))
    low_out[...] = integral[0:VPAD]
    project_and_send(integral, weights_out, lists, odd, faces_out, pair_out, far_out)
    for step in range(1, SUBSTEPS):
        coarse_out[step - 1] = integral_of(
            chain, taylor_weights(step / SUBSTEPS, (step + 1) / SUBSTEPS)
        )


def prepare_kernel(
    source, orientation, flux_other, face_front, face_turn, stiff_vol,
    slot_flux_out, slot_code_out, slot_hot_out, lift_out, table,
):
    row = iota((LANES, LANES), 0)
    peer = (row >= BOTH).astype(jnp.int32) + (row >= 2 * BOTH).astype(jnp.int32)
    peer = peer + (row >= 3 * BOTH).astype(jnp.int32)
    inner = row - BOTH * peer
    kind = (inner >= SLOTS).astype(jnp.int32)
    wanted = kind * (PEERS * SLOTS - SLOTS) + peer * SLOTS + inner + FACES
    wanted = jnp.where(row < PEERS * BOTH, wanted, -1)
    blocks = [jnp.where(source[i : i + 1, :] == wanted, 1.0, 0.0) for i in range(4)]
    slot_hot_out[...] = blocks[0] + blocks[1] + blocks[2] + blocks[3]
    hot = jnp.concatenate(blocks, axis=1).astype(BF16)
    codes = jnp.concatenate(
        [
            jnp.where(iota((16, LANES), 0) - 3 * i == orientation[i : i + 1, :], 1.0, 0.0)
            for i in range(4)
        ],
        axis=1,
    ).astype(BF16)
    dims = (((1,), (1,)), ((), ()))
    slot_code_out[...] = lax.dot_general(codes, hot, dims, preferred_element_type=F32)
    table[...] = jnp.zeros(table.shape, F32)
    for i in range(4):
        for q in range(NQ):
            table[16 * q : 16 * q + NQ, lanes(i)] = flux_other[i, q]
    slot_flux_out[...] = pick(table[...], hot, ((1,), (1,)))

    def placed(rows, offset):
        return jnp.where(
            iota((rows, DEEP), 1) == iota((rows, DEEP), 0) + offset, 1.0, 0.0
        )

    total = jnp.zeros((NB, DEEP), F32)
    for i in range(4):
        spread = placed(NF, REM + FPAD * i)
        for code in range(3):
            spread = spread + jnp.dot(
                face_turn[code], placed(NF, FPAD * (3 * i + code)),
                precision=HIGHEST, preferred_element_type=F32,
            )
        total = total - jnp.dot(
            face_front[i], spread, precision=HIGHEST, preferred_element_type=F32
        )
    for d in range(3):
        total = total + jnp.dot(
            stiff_vol[d], placed(NLOW, REM + OWN + VPAD * d),
            precision=HIGHEST, preferred_element_type=F32,
        )
    lift_out[...] = total


def local_kernel(
    state, low, faces, star, flux_self, flux_other, source, orientation, lift, out, stack,
):
    column = iota((FACES, LANES), 0)
    hot = jnp.concatenate(
        [
            jnp.where(column == source[i : i + 1, :], 1.0, 0.0).astype(BF16)
            for i in range(4)
        ],
        axis=1,
    )
    found = pick(face_table(faces[...]), hot)
    for d in range(3):
        totals = products(
            [lambda q: low[:, lanes(q)]], lambda _, q, p: star[d, q, p : p + 1, :], VPAD
        )
        base = REM + OWN + VPAD * d
        for p in range(NQ):
            stack[base : base + VPAD, lanes(p)] = totals[p]
    for i in range(4):
        totals = products(
            [lambda q: faces[i * FPAD : (i + 1) * FPAD, lanes(q)]],
            lambda _, q, p: flux_self[i, q, p : p + 1, :],
            FPAD,
        )
        for p in range(NQ):
            stack[REM + FPAD * i : REM + FPAD * (i + 1), lanes(p)] = totals[p]
    for i in range(4):
        totals = products(
            [lambda q: found[q * FPAD : (q + 1) * FPAD, lanes(i)]],
            lambda _, q, p: flux_other[i, q, p : p + 1, :],
            FPAD,
        )
        for code in range(3):
            mask = jnp.where(orientation[i : i + 1, :] == code, 1.0, 0.0)
            base = FPAD * (3 * i + code)
            for p in range(NQ):
                stack[base : base + FPAD, lanes(p)] = totals[p] * mask
    out[...] = state[...] + jnp.dot(
        lift[...], stack[...], precision=HIGH, preferred_element_type=F32
    )


def remote_part(position, near, upper, lower, slot_flux, slot_code, slot_hot, lift, stack):
    odd = lax.rem(position, 2) == 1
    behind_up = lax.rem(position, 4) < 2
    up, down = upper[...], lower[...]
    behind = jnp.where(behind_up, up, down)
    ahead = jnp.where(behind_up, down, up)
    here = near[0:BOTH, :]
    relayed = slice(2 * BOTH, 3 * BOTH)
    rows = jnp.concatenate(
        [
            jnp.where(odd, here, behind[relayed]),
            jnp.where(odd, ahead[relayed], here),
            behind[0:BOTH],
            ahead[BOTH : 2 * BOTH],
            jnp.zeros((LANES - PEERS * BOTH, WIDTH), F32),
        ],
        axis=0,
    )
    received = jnp.transpose(rows)
    totals = products(
        [lambda q: received[q * FPAD : (q + 1) * FPAD]],
        lambda _, q, p: slot_flux[16 * q + p : 16 * q + p + 1, :],
        FPAD,
    )
    for code in range(12):
        mask = slot_code[code : code + 1, :]
        for p in range(NQ):
            stack[FPAD * code : FPAD * (code + 1), lanes(p)] = totals[p] * mask
    lifted = jnp.dot(
        lift[:, 0:REM], stack[...], precision=HIGH, preferred_element_type=F32
    )
    by_slot = jnp.concatenate([lifted[:, lanes(p)] for p in range(NQ)], axis=0)
    by_element = pick(by_slot, slot_hot[...].astype(BF16))
    return jnp.concatenate([by_element[p * NB : (p + 1) * NB] for p in range(NQ)], axis=1)


def next_kernel(
    place, state, near, upper, lower, slot_flux, slot_code, slot_hot, lift,
    star, coarse, labels, weights, lists,
    state_out, low_out, faces_out, pair_out, far_out, stack, terms, *, step,
):
    position = place[0]
    odd = lax.rem(position, 2) == 1
    now = state[...] + remote_part(
        position, near, upper, lower, slot_flux, slot_code, slot_hot, lift, stack
    )
    state_out[...] = now
    chain = chain_of(now, star, weights, terms)
    fine = integral_of(chain, taylor_weights(0.0, 1.0 / SUBSTEPS))
    mask = labels[...] == 1
    integral = jnp.concatenate(
        [jnp.where(mask, fine[:, lanes(q)], coarse[step - 1, :, lanes(q)]) for q in range(NQ)],
        axis=1,
    )
    low_out[...] = integral[0:VPAD]
    project_and_send(integral, weights, lists, odd, faces_out, pair_out, far_out)


def last_kernel(
    place, state, near, upper, lower, slot_flux, slot_code, slot_hot, lift, out, stack
):
    total = state[...] + remote_part(
        place[0], near, upper, lower, slot_flux, slot_code, slot_hot, lift, stack
    )
    for q in range(NQ):
        out[:, q, :] = total[:, lanes(q)]


def floats(*shape):
    return jax.ShapeDtypeStruct(shape, F32)


def call(kernel, args, outs, scratch, scalars=0, flops=2.0e7):
    smem = pl.BlockSpec(memory_space=pltpu.SMEM)
    vmem = pl.BlockSpec(memory_space=pltpu.VMEM)
    moved = 4 * sum(math.prod(item.shape) for item in list(args) + list(outs))
    return pl.pallas_call(
        kernel,
        in_specs=[smem] * scalars + [vmem] * (len(args) - scalars),
        out_specs=[vmem] * len(outs),
        out_shape=outs,
        scratch_shapes=[pltpu.VMEM(shape, F32) for shape in scratch],
        compiler_params=pltpu.CompilerParams(vmem_limit_bytes=40 * 2**20),
        cost_estimate=pl.CostEstimate(flops=int(flops), bytes_accessed=moved, transcendentals=0),
    )(*args)


def swaps(count, first):
    pairs = []
    for low in range(count - 2):
        if low % 4 in (first, first + 1):
            pairs += [(low, low + 2), (low + 2, low)]
    return pairs


def local(
    dofs, star, flux_self, flux_other, labels, neighbour_source, orientation,
    fine_send, coarse_send, stiff_time, stiff_vol, face_back, face_front, face_turn,
):
    count = lax.axis_size("dom")
    partners = [(source, source ^ 1) for source in range(count)]
    place = lax.axis_index("dom").astype(jnp.int32).reshape(1)
    lists = jnp.concatenate([fine_send, coarse_send], axis=1).reshape(PEERS * BOTH, 1)
    labels = labels.reshape(1, LANES)
    sent_shapes = [floats(OWN, COLS), floats(2 * BOTH, WIDTH), floats(2 * BOTH, WIDTH)]
    state, low, coarse, faces, pair, far, weights = call(
        first_kernel,
        (place, dofs, star, stiff_time, face_back, lists),
        [floats(NB, COLS), floats(VPAD, COLS), floats(SUBSTEPS - 1, NB, COLS)]
        + sent_shapes
        + [floats(CHAIN_ROWS, LANES)],
        [(120, COLS)],
        scalars=1,
    )
    slot_flux, slot_code, slot_hot, lift = call(
        prepare_kernel,
        (neighbour_source, orientation, flux_other, face_front, face_turn, stiff_vol),
        [floats(16 * NQ, LANES), floats(16, LANES), floats(LANES, LANES), floats(NB, DEEP)],
        [(16 * NQ, FACES)],
    )
    for step in range(SUBSTEPS):
        near = lax.ppermute(pair, "dom", partners)
        message = jnp.concatenate([far, near[BOTH:]], axis=0)
        upper = lax.ppermute(message, "dom", swaps(count, 2))
        lower = lax.ppermute(message, "dom", swaps(count, 0))
        (state,) = call(
            local_kernel,
            (state, low, faces, star, flux_self, flux_other, neighbour_source, orientation, lift),
            [floats(NB, COLS)],
            [(DEEP, COLS)],
        )
        received = (place, state, near, upper, lower, slot_flux, slot_code, slot_hot, lift)
        if step + 1 < SUBSTEPS:
            state, low, faces, pair, far = call(
                functools.partial(next_kernel, step=step + 1),
                received + (star, coarse, labels, weights, lists),
                [floats(NB, COLS), floats(VPAD, COLS)] + sent_shapes,
                [(REM, COLS), (120, COLS)],
                scalars=1,
            )
    (result,) = call(
        last_kernel, received, [floats(NB, NQ, LANES)], [(REM, COLS)], scalars=1
    )
    return result


def solution(mesh):
    split = P(None, None, "dom")
    face = P(None, None, None, "dom")
    row = P(None, "dom")
    in_specs = (split, face, face, face, P("dom"), row, row, row, row, P(), P(), P(), P(), P())
    return jax.shard_map(local, mesh=mesh, in_specs=in_specs, out_specs=split, check_vma=False)
```

profile of v0, /device:TPU:384, one launch (start us, length us, event | category | flops | bytes accessed | tf_op | source)
XLA Modules:
  0.0 83.2 jit_solution(14002624479588775707)
XLA Ops:
  0.0 0.0 copy-start.5
  0.0 0.0 copy-start.12
  0.0 1.0 %copy.16.star = f32[3,9,9,128]{3,2,1,0:T(8,128)S(1)} copy(f32[3,9,9,128]{3,0,2,1:T(4,128)} %param.15) | data formatting | bytes 248832 | tf_op args[1]
  1.0 0.0 copy-start.11
  1.0 0.0 copy-done.12
  1.0 0.7 copy-done.11
  1.7 0.1 pad_add_fusion
  1.8 0.1 reshape.12.lists
  1.9 0.0 copy-done.5
  1.9 0.0 copy-start.9
  1.9 0.1 copy.15.dofs
  2.0 0.7 copy-done.9
  2.7 0.0 copy-start
  2.7 0.8 copy-done
  3.5 2.6 %shard_map.136 = (f32[56,1152]{1,0:T(8,128)S(1)}, f32[40,1152]{1,0:T(8,128)S(1)}, f32[3,56,1152]{2,1,0:T(8,128)S(1)}, f32[96,1152]{1,0:T(8,128)S(1)}, f32[48,256...) custom-call(s32[1]{0:T(128)} %bitcast.place, f32[56,9,128]{2,1,0:T(8,128)S(1)} %copy.15.dofs, ...), custom_call_target="tpu_custom_call" | custom-call | flops 20000000 | bytes 2378980 | tf_op jit(solution)/shard_map/pallas_call | solution.py:339
  6.1 0.0 copy-start.6
  6.1 2.1 %collective-permute-start = (f32[48,256]{1,0:T(8,128)S(1)}, f32[48,256]{1,0:T(8,128)S(1)}, u32[]{:S(2)}, u32[]{:S(2)}) collective-permute-start(f32[48,256]{1,0:T(8,128)S(1)} %get-tuple-element.35), channel_id=1, source_target_pairs={{0,1},{1,0},{2,3},{3,2},{4,5},{5,4},{6,7},{7,6},{8,9},{9,8},{10,11... | collective-permute-start | bytes 147464 | tf_op jit(solution)/shard_map/ppermute | solution.py:384
  8.2 1.2 %collective-permute-done.near = f32[48,256]{1,0:T(8,128)S(1)} collective-permute-done((f32[48,256]{1,0:T(8,128)S(1)}, f32[48,256]{1,0:T(8,128)S(1)}, u32[]{:S(2)}, u32[]{:S(2)}) %collective-permute-start) | collective-permute-done | bytes 49184 | tf_op jit(solution)/shard_map/ppermute | solution.py:384
  9.4 0.0 copy-start.10
  9.4 8.8 %collective-permute-start.1 = (f32[72,256]{1,0:T(8,128)S(1)}, f32[72,256]{1,0:T(8,128)S(1)}, u32[]{:S(2)}, u32[]{:S(2)}) collective-permute-start(f32[72,256]{1,0:T(8,128)S(1)} %pad_maximum_fusion), channel_id=1, source_target_pairs={{2,4},{4,2},{3,5},{5,3},{6,8},{8,6},{7,9},{9,7},{10,12},{12,10},{1... | collective-permute-start | bytes 221192 | tf_op jit(solution)/shard_map/ppermute | solution.py:386
  18.2 1.9 %collective-permute-start.2 = (f32[72,256]{1,0:T(8,128)S(1)}, f32[72,256]{1,0:T(8,128)S(1)}, u32[]{:S(2)}, u32[]{:S(2)}) collective-permute-start(f32[72,256]{1,0:T(8,128)S(1)} %pad_maximum_fusion), channel_id=1, source_target_pairs={{0,2},{2,0},{1,3},{3,1},{4,6},{6,4},{5,7},{7,5},{8,10},{10,8},{9,1... | collective-permute-start | bytes 221192 | tf_op jit(solution)/shard_map/ppermute | solution.py:387
  20.1 0.0 copy-done.6
  20.1 0.0 copy-start.8
  20.2 0.0 copy-done.10
  20.2 0.0 copy-start.7
  20.2 0.1 copy.20.face_front
  20.3 0.6 copy-done.8
  20.9 0.1 copy.21.stiff_vol
  21.0 0.1 copy-done.7
  21.1 0.6 copy-done.1
  21.8 0.0 copy-done.2
  21.8 0.1 copy-done.3
  21.9 2.2 %shard_map.137 = (f32[144,128]{1,0:T(8,128)S(1)}, f32[16,128]{1,0:T(8,128)S(1)}, f32[128,128]{1,0:T(8,128)S(1)}, f32[56,504]{1,0:T(8,128)S(1)}) custom-call(s32[4,128]{1,0:T(4,128)S(1)} %copy-done.1, s32[4,128]{1,0:T(4,128)S(1)} %copy-done.2, f32[4,9,9,128]{3,2,1,0:T(8,128)S(1)} %copy.24.flux_other, f32[4,56,21]{2,1,0:T(8,128)S(1)} %copy.20.face_front, ...), custom_call_target="tpu_custom_call" | custom-call | flops 20000000 | bytes 477964 | tf_op jit(solution)/shard_map/pallas_call | solution.py:339
  24.1 2.0 %shard_map.138.state = f32[56,1152]{1,0:T(8,128)S(1)} custom-call(f32[56,1152]{1,0:T(8,128)S(1)} %get-tuple-element.31.state, f32[40,1152]{1,0:T(8,128)S(1)} %get-tuple-element.32.low, f32[96,1152]{1,0:T(8,128)S(1)} %get-tuple-element.33.faces, f32[3,9,9,128]{3,2,1,0:T(8,128)S(1)} %copy.16.star, f32[4,9,9,128]{3,2,1,0:T(8,128)S(1)} %copy.23.flux_self, ...), custom_call_target="tpu_custom_call" | custom-call | flops 20000000 | bytes 1715968 | tf_op jit(solution)/shard_map/pallas_call | solution.py:339
  26.2 0.0 collective-permute-done.1.upper
  26.2 0.0 collective-permute-done.2.lower
  26.2 0.0 copy-start.4
  26.2 0.6 copy-done.4
  26.8 3.3 %shard_map.139 = (f32[56,1152]{1,0:T(8,128)S(1)}, f32[40,1152]{1,0:T(8,128)S(1)}, f32[96,1152]{1,0:T(8,128)S(1)}, f32[48,256]{1,0:T(8,128)S(1)}, f32[48,256]{1,0:T(8,128)S(1)}) custom-call(s32[1]{0:T(128)} %bitcast.place, f32[56,1152]{1,0:T(8,128)S(1)} %shard_map.138.state, f32[48,256]{1,0:T(8,128)S(1)} %collective-permute-done.near, ...), custom_call_target="tpu_custom_call" | custom-call | flops 20000000 | bytes 2794116 | tf_op jit(solution)/shard_map/pallas_call | solution.py:339
  30.1 1.9 %collective-permute-start.3 = (f32[48,256]{1,0:T(8,128)S(1)}, f32[48,256]{1,0:T(8,128)S(1)}, u32[]{:S(2)}, u32[]{:S(2)}) collective-permute-start(f32[48,256]{1,0:T(8,128)S(1)} %get-tuple-element.45), channel_id=1, source_target_pairs={{0,1},{1,0},{2,3},{3,2},{4,5},{5,4},{6,7},{7,6},{8,9},{9,8},{10,11... | collective-permute-start | bytes 147464 | tf_op jit(solution)/shard_map/ppermute | solution.py:384
  32.0 1.2 %collective-permute-done.3.near = f32[48,256]{1,0:T(8,128)S(1)} collective-permute-done((f32[48,256]{1,0:T(8,128)S(1)}, f32[48,256]{1,0:T(8,128)S(1)}, u32[]{:S(2)}, u32[]{:S(2)}) %collective-permute-start.3) | collective-permute-done | bytes 49184 | tf_op jit(solution)/shard_map/ppermute | solution.py:384
  33.2 3.7 %collective-permute-start.4 = (f32[72,256]{1,0:T(8,128)S(1)}, f32[72,256]{1,0:T(8,128)S(1)}, u32[]{:S(2)}, u32[]{:S(2)}) collective-permute-start(f32[72,256]{1,0:T(8,128)S(1)} %pad_maximum_fusion.1), channel_id=1, source_target_pairs={{2,4},{4,2},{3,5},{5,3},{6,8},{8,6},{7,9},{9,7},{10,12},{12,10},{1... | collective-permute-start | bytes 221192 | tf_op jit(solution)/shard_map/ppermute | solution.py:386
  36.9 2.4 %collective-permute-start.5 = (f32[72,256]{1,0:T(8,128)S(1)}, f32[72,256]{1,0:T(8,128)S(1)}, u32[]{:S(2)}, u32[]{:S(2)}) collective-permute-start(f32[72,256]{1,0:T(8,128)S(1)} %pad_maximum_fusion.1), channel_id=1, source_target_pairs={{0,2},{2,0},{1,3},{3,1},{4,6},{6,4},{5,7},{7,5},{8,10},{10,8},{9,1... | collective-permute-start | bytes 221192 | tf_op jit(solution)/shard_map/ppermute | solution.py:387
  39.3 2.0 %shard_map.140.state = f32[56,1152]{1,0:T(8,128)S(1)} custom-call(f32[56,1152]{1,0:T(8,128)S(1)} %get-tuple-element.42.state, f32[40,1152]{1,0:T(8,128)S(1)} %get-tuple-element.43.low, f32[96,1152]{1,0:T(8,128)S(1)} %get-tuple-element.44.faces, f32[3,9,9,128]{3,2,1,0:T(8,128)S(1)} %copy.16.star, f32[4,9,9,128]{3,2,1,0:T(8,128)S(1)} %copy.23.flux_self, ...), custom_call_target="tpu_custom_call" | custom-call | flops 20000000 | bytes 1715968 | tf_op jit(solution)/shard_map/pallas_call | solution.py:339
  41.3 3.6 %collective-permute-done.4.upper = f32[72,256]{1,0:T(8,128)S(1)} collective-permute-done((f32[72,256]{1,0:T(8,128)S(1)}, f32[72,256]{1,0:T(8,128)S(1)}, u32[]{:S(2)}, u32[]{:S(2)}) %collective-permute-start.4) | collective-permute-done | bytes 73760 | tf_op jit(solution)/shard_map/ppermute | solution.py:386
  44.9 0.0 collective-permute-done.5.lower
  44.9 3.3 %shard_map.141 = (f32[56,1152]{1,0:T(8,128)S(1)}, f32[40,1152]{1,0:T(8,128)S(1)}, f32[96,1152]{1,0:T(8,128)S(1)}, f32[48,256]{1,0:T(8,128)S(1)}, f32[48,256]{1,0:T(8,128)S(1)}) custom-call(s32[1]{0:T(128)} %bitcast.place, f32[56,1152]{1,0:T(8,128)S(1)} %shard_map.140.state, f32[48,256]{1,0:T(8,128)S(1)} %collective-permute-done.3.near, ...), custom_call_target="tpu_custom_call" | custom-call | flops 20000000 | bytes 2794116 | tf_op jit(solution)/shard_map/pallas_call | solution.py:339
  48.2 1.9 %collective-permute-start.6 = (f32[48,256]{1,0:T(8,128)S(1)}, f32[48,256]{1,0:T(8,128)S(1)}, u32[]{:S(2)}, u32[]{:S(2)}) collective-permute-start(f32[48,256]{1,0:T(8,128)S(1)} %get-tuple-element.50), channel_id=1, source_target_pairs={{0,1},{1,0},{2,3},{3,2},{4,5},{5,4},{6,7},{7,6},{8,9},{9,8},{10,11... | collective-permute-start | bytes 147464 | tf_op jit(solution)/shard_map/ppermute | solution.py:384
  50.1 1.2 %collective-permute-done.6.near = f32[48,256]{1,0:T(8,128)S(1)} collective-permute-done((f32[48,256]{1,0:T(8,128)S(1)}, f32[48,256]{1,0:T(8,128)S(1)}, u32[]{:S(2)}, u32[]{:S(2)}) %collective-permute-start.6) | collective-permute-done | bytes 49184 | tf_op jit(solution)/shard_map/ppermute | solution.py:384
  51.3 5.8 %collective-permute-start.7 = (f32[72,256]{1,0:T(8,128)S(1)}, f32[72,256]{1,0:T(8,128)S(1)}, u32[]{:S(2)}, u32[]{:S(2)}) collective-permute-start(f32[72,256]{1,0:T(8,128)S(1)} %pad_maximum_fusion.2), channel_id=1, source_target_pairs={{2,4},{4,2},{3,5},{5,3},{6,8},{8,6},{7,9},{9,7},{10,12},{12,10},{1... | collective-permute-start | bytes 221192 | tf_op jit(solution)/shard_map/ppermute | solution.py:386
  57.2 1.9 %collective-permute-start.8 = (f32[72,256]{1,0:T(8,128)S(1)}, f32[72,256]{1,0:T(8,128)S(1)}, u32[]{:S(2)}, u32[]{:S(2)}) collective-permute-start(f32[72,256]{1,0:T(8,128)S(1)} %pad_maximum_fusion.2), channel_id=1, source_target_pairs={{0,2},{2,0},{1,3},{3,1},{4,6},{6,4},{5,7},{7,5},{8,10},{10,8},{9,1... | collective-permute-start | bytes 221192 | tf_op jit(solution)/shard_map/ppermute | solution.py:387
  59.1 2.0 %shard_map.142.state = f32[56,1152]{1,0:T(8,128)S(1)} custom-call(f32[56,1152]{1,0:T(8,128)S(1)} %get-tuple-element.47.state, f32[40,1152]{1,0:T(8,128)S(1)} %get-tuple-element.48.low, f32[96,1152]{1,0:T(8,128)S(1)} %get-tuple-element.49.faces, f32[3,9,9,128]{3,2,1,0:T(8,128)S(1)} %copy.16.star, f32[4,9,9,128]{3,2,1,0:T(8,128)S(1)} %copy.23.flux_self, ...), custom_call_target="tpu_custom_call" | custom-call | flops 20000000 | bytes 1715968 | tf_op jit(solution)/shard_map/pallas_call | solution.py:339
  61.1 1.9 %collective-permute-done.7.upper = f32[72,256]{1,0:T(8,128)S(1)} collective-permute-done((f32[72,256]{1,0:T(8,128)S(1)}, f32[72,256]{1,0:T(8,128)S(1)}, u32[]{:S(2)}, u32[]{:S(2)}) %collective-permute-start.7) | collective-permute-done | bytes 73760 | tf_op jit(solution)/shard_map/ppermute | solution.py:386
  63.0 0.4 collective-permute-done.8.lower
  63.4 3.3 %shard_map.143 = (f32[56,1152]{1,0:T(8,128)S(1)}, f32[40,1152]{1,0:T(8,128)S(1)}, f32[96,1152]{1,0:T(8,128)S(1)}, f32[48,256]{1,0:T(8,128)S(1)}, f32[48,256]{1,0:T(8,128)S(1)}) custom-call(s32[1]{0:T(128)} %bitcast.place, f32[56,1152]{1,0:T(8,128)S(1)} %shard_map.142.state, f32[48,256]{1,0:T(8,128)S(1)} %collective-permute-done.6.near, ...), custom_call_target="tpu_custom_call" | custom-call | flops 20000000 | bytes 2794116 | tf_op jit(solution)/shard_map/pallas_call | solution.py:339
  66.7 1.9 %collective-permute-start.9 = (f32[48,256]{1,0:T(8,128)S(1)}, f32[48,256]{1,0:T(8,128)S(1)}, u32[]{:S(2)}, u32[]{:S(2)}) collective-permute-start(f32[48,256]{1,0:T(8,128)S(1)} %get-tuple-element.55), channel_id=1, source_target_pairs={{0,1},{1,0},{2,3},{3,2},{4,5},{5,4},{6,7},{7,6},{8,9},{9,8},{10,11... | collective-permute-start | bytes 147464 | tf_op jit(solution)/shard_map/ppermute | solution.py:384
  68.6 1.2 %collective-permute-done.9.near = f32[48,256]{1,0:T(8,128)S(1)} collective-permute-done((f32[48,256]{1,0:T(8,128)S(1)}, f32[48,256]{1,0:T(8,128)S(1)}, u32[]{:S(2)}, u32[]{:S(2)}) %collective-permute-start.9) | collective-permute-done | bytes 49184 | tf_op jit(solution)/shard_map/ppermute | solution.py:384
  69.8 5.4 %collective-permute-start.10 = (f32[72,256]{1,0:T(8,128)S(1)}, f32[72,256]{1,0:T(8,128)S(1)}, u32[]{:S(2)}, u32[]{:S(2)}) collective-permute-start(f32[72,256]{1,0:T(8,128)S(1)} %pad_maximum_fusion.3), channel_id=1, source_target_pairs={{2,4},{4,2},{3,5},{5,3},{6,8},{8,6},{7,9},{9,7},{10,12},{12,10},{1... | collective-permute-start | bytes 221192 | tf_op jit(solution)/shard_map/ppermute | solution.py:386
  75.3 1.9 %collective-permute-start.11 = (f32[72,256]{1,0:T(8,128)S(1)}, f32[72,256]{1,0:T(8,128)S(1)}, u32[]{:S(2)}, u32[]{:S(2)}) collective-permute-start(f32[72,256]{1,0:T(8,128)S(1)} %pad_maximum_fusion.3), channel_id=1, source_target_pairs={{0,2},{2,0},{1,3},{3,1},{4,6},{6,4},{5,7},{7,5},{8,10},{10,8},{9,1... | collective-permute-start | bytes 221192 | tf_op jit(solution)/shard_map/ppermute | solution.py:387
  77.2 2.0 %shard_map.144.state = f32[56,1152]{1,0:T(8,128)S(1)} custom-call(f32[56,1152]{1,0:T(8,128)S(1)} %get-tuple-element.52.state, f32[40,1152]{1,0:T(8,128)S(1)} %get-tuple-element.53.low, f32[96,1152]{1,0:T(8,128)S(1)} %get-tuple-element.54.faces, f32[3,9,9,128]{3,2,1,0:T(8,128)S(1)} %copy.16.star, f32[4,9,9,128]{3,2,1,0:T(8,128)S(1)} %copy.23.flux_self, ...), custom_call_target="tpu_custom_call" | custom-call | flops 20000000 | bytes 1715968 | tf_op jit(solution)/shard_map/pallas_call | solution.py:339
  79.2 2.3 %collective-permute-done.10.upper = f32[72,256]{1,0:T(8,128)S(1)} collective-permute-done((f32[72,256]{1,0:T(8,128)S(1)}, f32[72,256]{1,0:T(8,128)S(1)}, u32[]{:S(2)}, u32[]{:S(2)}) %collective-permute-start.10) | collective-permute-done | bytes 73760 | tf_op jit(solution)/shard_map/ppermute | solution.py:386
  81.5 0.0 collective-permute-done.11.lower
  81.5 0.9 %shard_map.145 = f32[56,9,128]{2,1,0:T(8,128)S(1)} custom-call(s32[1]{0:T(128)} %bitcast.place, f32[56,1152]{1,0:T(8,128)S(1)} %shard_map.144.state, f32[48,256]{1,0:T(8,128)S(1)} %collective-permute-done.9.near, f32[72,256]{1,0:T(8,128)S(1)} %collective-permute-done.10.upper, f32[72,256]{1,0:T(8,128)S(1)} %collective-permute-done.11.lower, ...), custom_call_target="tpu_custom_call" | custom-call | flops 20000000 | bytes 973060 | tf_op jit(solution)/shard_map/pallas_call | solution.py:339
  82.4 0.8 copy.40
  (14 shorter events, 0.1 us)
Async XLA Ops:
  0.0 1.9 %copy-start.5 = (f32[56,9,128]{2,0,1:T(8,128)S(1)}, f32[56,9,128]{2,0,1:T(8,128)}, u32[]{:S(2)}) copy-start(f32[56,9,128]{2,0,1:T(8,128)} %param.14) | copy-start | bytes 774148
  0.0 1.0 %copy-start.12 = (s32[4,12]{1,0:T(4,128)S(1)}, s32[4,12]{1,0:T(4,128)}, u32[]{:S(2)}) copy-start(s32[4,12]{1,0:T(4,128)} %param.21) | copy-start | bytes 580
  1.0 0.7 copy-start.11
  1.9 0.8 copy-start.9
  2.7 0.8 copy-start
  6.1 14.0 %copy-start.6 = (f32[4,9,9,128]{3,0,2,1:T(4,128)S(1)}, f32[4,9,9,128]{3,0,2,1:T(4,128)}, u32[]{:S(2)}) copy-start(f32[4,9,9,128]{3,0,2,1:T(4,128)} %param.17) | copy-start | bytes 497668
  6.1 3.3 %collective-permute-start = (f32[48,256]{1,0:T(8,128)S(1)}, f32[48,256]{1,0:T(8,128)S(1)}, u32[]{:S(2)}, u32[]{:S(2)}) collective-permute-start(f32[48,256]{1,0:T(8,128)S(1)} %get-tuple-element.35), channel_id=1, source_target_pairs={{0,1},{1,0},{2,3},{3,2},{4,5},{5,4},{6,7},{7,6},{8,9},{9,8},{10,11... | collective-permute-start | bytes 147464 | tf_op jit(solution)/shard_map/ppermute | solution.py:384
  9.4 10.8 %copy-start.10 = (f32[4,56,21]{1,0,2:T(4,128)S(1)}, f32[4,56,21]{1,0,2:T(4,128)}, u32[]{:S(2)}) copy-start(f32[4,56,21]{1,0,2:T(4,128)} %param.26) | copy-start | bytes 56452
  9.4 16.8 %collective-permute-start.1 = (f32[72,256]{1,0:T(8,128)S(1)}, f32[72,256]{1,0:T(8,128)S(1)}, u32[]{:S(2)}, u32[]{:S(2)}) collective-permute-start(f32[72,256]{1,0:T(8,128)S(1)} %pad_maximum_fusion), channel_id=1, source_target_pairs={{2,4},{4,2},{3,5},{5,3},{6,8},{8,6},{7,9},{9,7},{10,12},{12,10},{1... | collective-permute-start | bytes 221192 | tf_op jit(solution)/shard_map/ppermute | solution.py:386
  18.2 8.0 %collective-permute-start.2 = (f32[72,256]{1,0:T(8,128)S(1)}, f32[72,256]{1,0:T(8,128)S(1)}, u32[]{:S(2)}, u32[]{:S(2)}) collective-permute-start(f32[72,256]{1,0:T(8,128)S(1)} %pad_maximum_fusion), channel_id=1, source_target_pairs={{0,2},{2,0},{1,3},{3,1},{4,6},{6,4},{5,7},{7,5},{8,10},{10,8},{9,1... | collective-permute-start | bytes 221192 | tf_op jit(solution)/shard_map/ppermute | solution.py:387
  20.1 0.8 %copy-start.8 = (f32[3,56,35]{1,2,0:T(8,128)S(1)}, f32[3,56,35]{1,2,0:T(8,128)}, u32[]{:S(2)}) copy-start(f32[3,56,35]{1,2,0:T(8,128)} %param.24) | copy-start | bytes 70564
  20.2 0.9 %copy-start.7 = (f32[4,9,9,128]{3,0,2,1:T(4,128)S(1)}, f32[4,9,9,128]{3,0,2,1:T(4,128)}, u32[]{:S(2)}) copy-start(f32[4,9,9,128]{3,0,2,1:T(4,128)} %param.16) | copy-start | bytes 497668
  21.1 0.7 copy-start.1
  21.1 0.7 copy-start.2
  21.1 0.8 copy-start.3
  26.2 0.7 copy-start.4
  30.1 3.1 %collective-permute-start.3 = (f32[48,256]{1,0:T(8,128)S(1)}, f32[48,256]{1,0:T(8,128)S(1)}, u32[]{:S(2)}, u32[]{:S(2)}) collective-permute-start(f32[48,256]{1,0:T(8,128)S(1)} %get-tuple-element.45), channel_id=1, source_target_pairs={{0,1},{1,0},{2,3},{3,2},{4,5},{5,4},{6,7},{7,6},{8,9},{9,8},{10,11... | collective-permute-start | bytes 147464 | tf_op jit(solution)/shard_map/ppermute | solution.py:384
  33.2 11.7 %collective-permute-start.4 = (f32[72,256]{1,0:T(8,128)S(1)}, f32[72,256]{1,0:T(8,128)S(1)}, u32[]{:S(2)}, u32[]{:S(2)}) collective-permute-start(f32[72,256]{1,0:T(8,128)S(1)} %pad_maximum_fusion.1), channel_id=1, source_target_pairs={{2,4},{4,2},{3,5},{5,3},{6,8},{8,6},{7,9},{9,7},{10,12},{12,10},{1... | collective-permute-start | bytes 221192 | tf_op jit(solution)/shard_map/ppermute | solution.py:386
  36.9 8.0 %collective-permute-start.5 = (f32[72,256]{1,0:T(8,128)S(1)}, f32[72,256]{1,0:T(8,128)S(1)}, u32[]{:S(2)}, u32[]{:S(2)}) collective-permute-start(f32[72,256]{1,0:T(8,128)S(1)} %pad_maximum_fusion.1), channel_id=1, source_target_pairs={{0,2},{2,0},{1,3},{3,1},{4,6},{6,4},{5,7},{7,5},{8,10},{10,8},{9,1... | collective-permute-start | bytes 221192 | tf_op jit(solution)/shard_map/ppermute | solution.py:387
  48.2 3.1 %collective-permute-start.6 = (f32[48,256]{1,0:T(8,128)S(1)}, f32[48,256]{1,0:T(8,128)S(1)}, u32[]{:S(2)}, u32[]{:S(2)}) collective-permute-start(f32[48,256]{1,0:T(8,128)S(1)} %get-tuple-element.50), channel_id=1, source_target_pairs={{0,1},{1,0},{2,3},{3,2},{4,5},{5,4},{6,7},{7,6},{8,9},{9,8},{10,11... | collective-permute-start | bytes 147464 | tf_op jit(solution)/shard_map/ppermute | solution.py:384
  51.3 11.7 %collective-permute-start.7 = (f32[72,256]{1,0:T(8,128)S(1)}, f32[72,256]{1,0:T(8,128)S(1)}, u32[]{:S(2)}, u32[]{:S(2)}) collective-permute-start(f32[72,256]{1,0:T(8,128)S(1)} %pad_maximum_fusion.2), channel_id=1, source_target_pairs={{2,4},{4,2},{3,5},{5,3},{6,8},{8,6},{7,9},{9,7},{10,12},{12,10},{1... | collective-permute-start | bytes 221192 | tf_op jit(solution)/shard_map/ppermute | solution.py:386
  57.2 6.2 %collective-permute-start.8 = (f32[72,256]{1,0:T(8,128)S(1)}, f32[72,256]{1,0:T(8,128)S(1)}, u32[]{:S(2)}, u32[]{:S(2)}) collective-permute-start(f32[72,256]{1,0:T(8,128)S(1)} %pad_maximum_fusion.2), channel_id=1, source_target_pairs={{0,2},{2,0},{1,3},{3,1},{4,6},{6,4},{5,7},{7,5},{8,10},{10,8},{9,1... | collective-permute-start | bytes 221192 | tf_op jit(solution)/shard_map/ppermute | solution.py:387
  66.7 3.1 %collective-permute-start.9 = (f32[48,256]{1,0:T(8,128)S(1)}, f32[48,256]{1,0:T(8,128)S(1)}, u32[]{:S(2)}, u32[]{:S(2)}) collective-permute-start(f32[48,256]{1,0:T(8,128)S(1)} %get-tuple-element.55), channel_id=1, source_target_pairs={{0,1},{1,0},{2,3},{3,2},{4,5},{5,4},{6,7},{7,6},{8,9},{9,8},{10,11... | collective-permute-start | bytes 147464 | tf_op jit(solution)/shard_map/ppermute | solution.py:384
  69.8 11.7 %collective-permute-start.10 = (f32[72,256]{1,0:T(8,128)S(1)}, f32[72,256]{1,0:T(8,128)S(1)}, u32[]{:S(2)}, u32[]{:S(2)}) collective-permute-start(f32[72,256]{1,0:T(8,128)S(1)} %pad_maximum_fusion.3), channel_id=1, source_target_pairs={{2,4},{4,2},{3,5},{5,3},{6,8},{8,6},{7,9},{9,7},{10,12},{12,10},{1... | collective-permute-start | bytes 221192 | tf_op jit(solution)/shard_map/ppermute | solution.py:386
  75.3 6.2 %collective-permute-start.11 = (f32[72,256]{1,0:T(8,128)S(1)}, f32[72,256]{1,0:T(8,128)S(1)}, u32[]{:S(2)}, u32[]{:S(2)}) collective-permute-start(f32[72,256]{1,0:T(8,128)S(1)} %pad_maximum_fusion.3), channel_id=1, source_target_pairs={{0,2},{2,0},{1,3},{3,1},{4,6},{6,4},{5,7},{7,5},{8,10},{10,8},{9,1... | collective-permute-start | bytes 221192 | tf_op jit(solution)/shard_map/ppermute | solution.py:387
where the time goes:
time: 83.9 us; the launch traced here: 83.2 us
  starting transfers between devices  39.6 us (47%)
  Pallas kernels  23.4 us (28%)
  waiting for transfers between devices  13.1 us (16%)
  local copies, waits for them, and re-layouts  6.56 us (8%)
    ppermute x4, starting transfers between devices, local(): upper = lax.ppermute(message, 'dom', swaps(count, 2))  23.7 us
    pallas_call x10, Pallas kernels, call(): pl.pallas_call(kernel, in_specs=[smem] * scalars + [vmem] * (len(args) -...  23.4 us
    ppermute x4, starting transfers between devices, local(): lower = lax.ppermute(message, 'dom', swaps(count, 0))  8.11 us
    ppermute x4, waiting for transfers between devices, local(): upper = lax.ppermute(message, 'dom', swaps(count, 2))  7.92 us
    ppermute x4, starting transfers between devices, local(): near = lax.ppermute(pair, 'dom', partners)  7.81 us
    unnamed x33, local copies, waits for them, and re-layouts  5.67 us
    ppermute x4, waiting for transfers between devices, local(): near = lax.ppermute(pair, 'dom', partners)  4.79 us
  transfers between devices with their start and end apart: 12, of which 8 were waited for; matrix products, arithmetic and copies ran while one was open for 0% of the time, Pallas kernels for 12%

commit v1 on v0

--- a/solution.py
+++ b/solution.py
@@ -26,6 +26,7 @@
 REM = 12 * FPAD
 OWN = 4 * FPAD
 DEEP = REM + OWN + 3 * VPAD
+DEEP_PAD = 512
 LEVELS = [(0, 35, 40, 56), (120, 20, 24, 40), (192, 10, 16, 24), (240, 4, 8, 16), (264, 1, 8, 8)]
 BACK = 288
 CHAIN_ROWS = BACK + OWN
@@ -80,7 +81,7 @@
         for d in range(3):
             out[start + d * padded : start + d * padded + valid, 0:NB] = stiff_time[d, 0:valid, :]
     for j in range(4):
-        out[BACK + j * FPAD : BACK + j * FPAD + NF, 0:NB] = face_back[j]
+        out[BACK + j * FPAD : BACK + j * FPAD + NF, 0:NB] = face_back[:, j, :]
 
 
 def chain_of(first, star, weights, terms):
@@ -97,7 +98,7 @@
         blocks = [
             lambda q, d=d: terms[d * padded : (d + 1) * padded, lanes(q)] for d in range(3)
         ]
-        totals = products(blocks, lambda d, q, p: star[d, q, p : p + 1, :], padded)
+        totals = products(blocks, lambda d, q, p: star[q, p, d : d + 1, :], padded)
         now = jnp.concatenate(totals, axis=1)
         chain.append(now)
     return chain
@@ -129,44 +130,104 @@
     return jnp.concatenate(rows, axis=0)
 
 
-def project_and_send(integral, weights, lists, odd, faces_out, pair_out, far_out):
+def project_and_send(integral, weights, lists, position, faces_out, pair_out, up_out, down_out):
     faces = jnp.dot(
         weights[BACK : BACK + OWN, 0:NB], integral, precision=HIGH, preferred_element_type=F32
     )
     faces_out[...] = faces
     top, rest = halves(face_table(faces))
-    hot = jnp.where(lists[...] == iota((PEERS * BOTH, FACES), 1), 1.0, 0.0).astype(BF16)
+    hot = jnp.concatenate(
+        [
+            jnp.where(lists[...] == iota((PEERS * BOTH, LANES), 1) + LANES * j, 1.0, 0.0)
+            for j in range(4)
+        ],
+        axis=1,
+    ).astype(BF16)
     dims = (((1,), (1,)), ((), ()))
     sent = lax.dot_general(hot, top, dims, preferred_element_type=F32) + lax.dot_general(
         hot, rest, dims, preferred_element_type=F32
     )
+    odd = lax.rem(position, 2) == 1
     first, second = sent[0:BOTH], sent[BOTH : 2 * BOTH]
     pair_out[0:BOTH, :] = jnp.where(odd, second, first)
     pair_out[BOTH : 2 * BOTH, :] = jnp.where(odd, first, second)
-    far_out[...] = sent[2 * BOTH : 4 * BOTH]
+    behind_up = lax.rem(position, 4) < 2
+    ahead, behind = sent[2 * BOTH : 3 * BOTH], sent[3 * BOTH : 4 * BOTH]
+    up_out[...] = jnp.where(behind_up, behind, ahead)
+    down_out[...] = jnp.where(behind_up, ahead, behind)
+
+
+def list_column(fine, coarse):
+    row = iota((PEERS * BOTH, LANES), 0)
+    peer = (row >= BOTH).astype(jnp.int32) + (row >= 2 * BOTH).astype(jnp.int32)
+    peer = peer + (row >= 3 * BOTH).astype(jnp.int32)
+    inner = row - BOTH * peer
+    total = jnp.zeros((PEERS * BOTH, LANES), F32)
+    for kind, entries in enumerate((fine, coarse)):
+        here = iota((PEERS * BOTH, LANES), 1) == inner - kind * SLOTS
+        for k in range(PEERS):
+            total = total + jnp.where(here & (peer == k), entries[k : k + 1, :], 0.0)
+    column = jnp.sum(total, axis=1, keepdims=True)
+    return jnp.broadcast_to(column, (PEERS * BOTH, LANES)).astype(jnp.int32)
 
 
 def first_kernel(
-    place, dofs, star, stiff_time, face_back, lists,
-    state_out, low_out, coarse_out, faces_out, pair_out, far_out, weights_out, terms,
+    place, dofs, star, stiff_time, face_back, fine_send, coarse_send, labels, *rest
 ):
-    odd = lax.rem(place[0], 2) == 1
-    chain_weights(stiff_time, face_back, weights_out)
-    state = jnp.concatenate([dofs[:, q, :] for q in range(NQ)], axis=1)
-    state_out[...] = state
-    chain = chain_of(state, star, weights_out, terms)
+    later = rest[:7]
+    (
+        state_out, low_out, coarse_out, faces_out, pair_out, up_out, down_out,
+        weights_out, star_out, labels_out, lists_out,
+    ) = rest[7:18]
+    later_out = rest[18:25]
+    terms, time_here, back_here, wide, fine_here, coarse_here, ready = rest[25:]
+    position = place[0]
+    moves = [
+        (stiff_time, time_here),
+        (face_back, back_here),
+        (star, star_out),
+        (fine_send, fine_here),
+        (coarse_send, coarse_here),
+        (labels, labels_out),
+    ]
+    moves += [(dofs.at[q], state_out.at[:, lanes(q)]) for q in range(NQ)]
+    moves += list(zip(later, later_out))
+    copies = [
+        pltpu.make_async_copy(source, target, ready.at[number])
+        for number, (source, target) in enumerate(moves)
+    ]
+    for copy in copies:
+        copy.start()
+    copies[0].wait()
+    copies[1].wait()
+    chain_weights(time_here, back_here, weights_out)
+    for copy in copies[6 : 6 + NQ]:
+        copy.wait()
+    copies[2].wait()
+    state = state_out[...]
+    chain = chain_of(state, star_out, weights_out, terms)
     integral = integral_of(chain, taylor_weights(0.0, 1.0 / SUBSTEPS))
     low_out[...] = integral[0:VPAD]
-    project_and_send(integral, weights_out, lists, odd, faces_out, pair_out, far_out)
+    for copy in copies[3:6]:
+        copy.wait()
+    wide[...] = jnp.zeros(wide.shape, F32)
+    wide[0:PEERS, 0:SLOTS] = fine_here[...].astype(F32)
+    wide[8 : 8 + PEERS, 0:SLOTS] = coarse_here[...].astype(F32)
+    lists_out[...] = list_column(wide[0:PEERS], wide[8 : 8 + PEERS])
+    project_and_send(
+        integral, weights_out, lists_out, position, faces_out, pair_out, up_out, down_out
+    )
     for step in range(1, SUBSTEPS):
         coarse_out[step - 1] = integral_of(
             chain, taylor_weights(step / SUBSTEPS, (step + 1) / SUBSTEPS)
         )
+    for copy in copies[6 + NQ :]:
+        copy.wait()
 
 
 def prepare_kernel(
     source, orientation, flux_other, face_front, face_turn, stiff_vol,
-    slot_flux_out, slot_code_out, slot_hot_out, lift_out, table,
+    slot_flux_out, slot_code_out, slot_hot_out, lift_out, table, fronts, tall,
 ):
     row = iota((LANES, LANES), 0)
     peer = (row >= BOTH).astype(jnp.int32) + (row >= 2 * BOTH).astype(jnp.int32)
@@ -190,31 +251,28 @@
     table[...] = jnp.zeros(table.shape, F32)
     for i in range(4):
         for q in range(NQ):
-            table[16 * q : 16 * q + NQ, lanes(i)] = flux_other[i, q]
+            table[16 * q : 16 * q + NQ, lanes(i)] = flux_other[q, :, i, :]
     slot_flux_out[...] = pick(table[...], hot, ((1,), (1,)))
 
-    def placed(rows, offset):
-        return jnp.where(
-            iota((rows, DEEP), 1) == iota((rows, DEEP), 0) + offset, 1.0, 0.0
-        )
-
-    total = jnp.zeros((NB, DEEP), F32)
+    fronts[...] = jnp.zeros(fronts.shape, F32)
+    tall[...] = jnp.zeros(tall.shape, F32)
     for i in range(4):
-        spread = placed(NF, REM + FPAD * i)
-        for code in range(3):
-            spread = spread + jnp.dot(
-                face_turn[code], placed(NF, FPAD * (3 * i + code)),
-                precision=HIGHEST, preferred_element_type=F32,
-            )
-        total = total - jnp.dot(
-            face_front[i], spread, precision=HIGHEST, preferred_element_type=F32
-        )
+        fronts[0:NF, i * LANES : i * LANES + NB] = face_front[:, i, :]
+    for code in range(3):
+        turned = lax.dot_general(
+            face_turn[code], fronts[0:NF, :], (((0,), (0,)), ((), ())),
+            precision=HIGHEST, preferred_element_type=F32,
+        )
+        for i in range(4):
+            start = FPAD * (3 * i + code)
+            tall[start : start + NF, :] = -turned[:, lanes(i)]
+    for i in range(4):
+        start = REM + FPAD * i
+        tall[start : start + NF, :] = -fronts[0:NF, lanes(i)]
     for d in range(3):
-        total = total + jnp.dot(
-            stiff_vol[d], placed(NLOW, REM + OWN + VPAD * d),
-            precision=HIGHEST, preferred_element_type=F32,
-        )
-    lift_out[...] = total
+        start = REM + OWN + VPAD * d
+        tall[start : start + NLOW, 0:NB] = stiff_vol[d]
+    lift_out[...] = jnp.transpose(tall[...])[0:NB]
 
 
 def local_kernel(
@@ -231,7 +289,7 @@
     found = pick(face_table(faces[...]), hot)
     for d in range(3):
         totals = products(
-            [lambda q: low[:, lanes(q)]], lambda _, q, p: star[d, q, p : p + 1, :], VPAD
+            [lambda q: low[:, lanes(q)]], lambda _, q, p: star[q, p, d : d + 1, :], VPAD
         )
         base = REM + OWN + VPAD * d
         for p in range(NQ):
@@ -239,7 +297,7 @@
     for i in range(4):
         totals = products(
             [lambda q: faces[i * FPAD : (i + 1) * FPAD, lanes(q)]],
-            lambda _, q, p: flux_self[i, q, p : p + 1, :],
+            lambda _, q, p: flux_self[q, p, i : i + 1, :],
             FPAD,
         )
         for p in range(NQ):
@@ -247,7 +305,7 @@
     for i in range(4):
         totals = products(
             [lambda q: found[q * FPAD : (q + 1) * FPAD, lanes(i)]],
-            lambda _, q, p: flux_other[i, q, p : p + 1, :],
+            lambda _, q, p: flux_other[q, p, i : i + 1, :],
             FPAD,
         )
         for code in range(3):
@@ -256,7 +314,7 @@
             for p in range(NQ):
                 stack[base : base + FPAD, lanes(p)] = totals[p] * mask
     out[...] = state[...] + jnp.dot(
-        lift[...], stack[...], precision=HIGH, preferred_element_type=F32
+        lift[:, 0:DEEP], stack[...], precision=HIGH, preferred_element_type=F32
     )
 
 
@@ -267,13 +325,13 @@
     behind = jnp.where(behind_up, up, down)
     ahead = jnp.where(behind_up, down, up)
     here = near[0:BOTH, :]
-    relayed = slice(2 * BOTH, 3 * BOTH)
+    relayed = slice(BOTH, 2 * BOTH)
     rows = jnp.concatenate(
         [
             jnp.where(odd, here, behind[relayed]),
             jnp.where(odd, ahead[relayed], here),
             behind[0:BOTH],
-            ahead[BOTH : 2 * BOTH],
+            ahead[0:BOTH],
             jnp.zeros((LANES - PEERS * BOTH, WIDTH), F32),
         ],
         axis=0,
@@ -299,10 +357,9 @@
 def next_kernel(
     place, state, near, upper, lower, slot_flux, slot_code, slot_hot, lift,
     star, coarse, labels, weights, lists,
-    state_out, low_out, faces_out, pair_out, far_out, stack, terms, *, step,
+    state_out, low_out, faces_out, pair_out, up_out, down_out, stack, terms, *, step,
 ):
     position = place[0]
-    odd = lax.rem(position, 2) == 1
     now = state[...] + remote_part(
         position, near, upper, lower, slot_flux, slot_code, slot_hot, lift, stack
     )
@@ -315,7 +372,9 @@
         axis=1,
     )
     low_out[...] = integral[0:VPAD]
-    project_and_send(integral, weights, lists, odd, faces_out, pair_out, far_out)
+    project_and_send(
+        integral, weights, lists, position, faces_out, pair_out, up_out, down_out
+    )
 
 
 def last_kernel(
@@ -325,23 +384,30 @@
         place[0], near, upper, lower, slot_flux, slot_code, slot_hot, lift, stack
     )
     for q in range(NQ):
-        out[:, q, :] = total[:, lanes(q)]
+        out[q] = total[:, lanes(q)]
 
 
 def floats(*shape):
     return jax.ShapeDtypeStruct(shape, F32)
 
 
-def call(kernel, args, outs, scratch, scalars=0, flops=2.0e7):
+def call(kernel, args, outs, scratch, scalars=0, inside=False, flops=2.0e7):
     smem = pl.BlockSpec(memory_space=pltpu.SMEM)
     vmem = pl.BlockSpec(memory_space=pltpu.VMEM)
+    given = pl.BlockSpec(memory_space=pl.ANY) if inside else vmem
+    if inside:
+        args = args[:scalars] + tuple(
+            pltpu.with_memory_space_constraint(item, pltpu.HBM) for item in args[scalars:]
+        )
     moved = 4 * sum(math.prod(item.shape) for item in list(args) + list(outs))
     return pl.pallas_call(
         kernel,
-        in_specs=[smem] * scalars + [vmem] * (len(args) - scalars),
+        in_specs=[smem] * scalars + [given] * (len(args) - scalars),
         out_specs=[vmem] * len(outs),
         out_shape=outs,
-        scratch_shapes=[pltpu.VMEM(shape, F32) for shape in scratch],
+        scratch_shapes=[
+            pltpu.VMEM(item, F32) if isinstance(item, tuple) else item for item in scratch
+        ],
         compiler_params=pltpu.CompilerParams(vmem_limit_bytes=40 * 2**20),
         cost_estimate=pl.CostEstimate(flops=int(flops), bytes_accessed=moved, transcendentals=0),
     )(*args)
@@ -362,38 +428,59 @@
     count = lax.axis_size("dom")
     partners = [(source, source ^ 1) for source in range(count)]
     place = lax.axis_index("dom").astype(jnp.int32).reshape(1)
-    lists = jnp.concatenate([fine_send, coarse_send], axis=1).reshape(PEERS * BOTH, 1)
     labels = labels.reshape(1, LANES)
-    sent_shapes = [floats(OWN, COLS), floats(2 * BOTH, WIDTH), floats(2 * BOTH, WIDTH)]
-    state, low, coarse, faces, pair, far, weights = call(
+    later = (
+        flux_self.transpose(1, 2, 0, 3),
+        flux_other.transpose(1, 2, 0, 3),
+        neighbour_source,
+        orientation,
+        face_front.transpose(2, 0, 1),
+        face_turn,
+        stiff_vol.transpose(0, 2, 1),
+    )
+    star = star.transpose(1, 2, 0, 3)
+    back = face_back.transpose(1, 0, 2)
+    message = floats(BOTH, WIDTH)
+    sent_shapes = [floats(OWN, COLS), floats(2 * BOTH, WIDTH), message, message]
+    like = lambda item: jax.ShapeDtypeStruct(item.shape, item.dtype)
+    found = call(
         first_kernel,
-        (place, dofs, star, stiff_time, face_back, lists),
+        (place, dofs.transpose(1, 0, 2), star, stiff_time, back, fine_send, coarse_send, labels)
+        + later,
         [floats(NB, COLS), floats(VPAD, COLS), floats(SUBSTEPS - 1, NB, COLS)]
         + sent_shapes
-        + [floats(CHAIN_ROWS, LANES)],
-        [(120, COLS)],
+        + [floats(CHAIN_ROWS, LANES), like(star), like(labels)]
+        + [jax.ShapeDtypeStruct((PEERS * BOTH, LANES), jnp.int32)]
+        + [like(item) for item in later],
+        [(120, COLS), stiff_time.shape, back.shape, (16, LANES)]
+        + [pltpu.VMEM(item.shape, jnp.int32) for item in (fine_send, coarse_send)]
+        + [pltpu.SemaphoreType.DMA((6 + NQ + len(later),))],
         scalars=1,
-    )
+        inside=True,
+    )
+    state, low, coarse, faces, pair, up, down, weights, star, labels, lists = found[:11]
+    flux_self, flux_other, source, orientation, front, turn, vol = found[11:]
     slot_flux, slot_code, slot_hot, lift = call(
         prepare_kernel,
-        (neighbour_source, orientation, flux_other, face_front, face_turn, stiff_vol),
-        [floats(16 * NQ, LANES), floats(16, LANES), floats(LANES, LANES), floats(NB, DEEP)],
-        [(16 * NQ, FACES)],
+        (source, orientation, flux_other, front, turn, vol),
+        [floats(16 * NQ, LANES), floats(16, LANES), floats(LANES, LANES), floats(NB, DEEP_PAD)],
+        [(16 * NQ, FACES), (FPAD, FACES), (DEEP_PAD, LANES)],
     )
     for step in range(SUBSTEPS):
         near = lax.ppermute(pair, "dom", partners)
-        message = jnp.concatenate([far, near[BOTH:]], axis=0)
-        upper = lax.ppermute(message, "dom", swaps(count, 2))
-        lower = lax.ppermute(message, "dom", swaps(count, 0))
+        if step == 0:
+            up, down, lift = lax.optimization_barrier((up, down, lift))
+        upper = lax.ppermute(jnp.concatenate([up, near[BOTH:]], axis=0), "dom", swaps(count, 2))
+        lower = lax.ppermute(jnp.concatenate([down, near[BOTH:]], axis=0), "dom", swaps(count, 0))
         (state,) = call(
             local_kernel,
-            (state, low, faces, star, flux_self, flux_other, neighbour_source, orientation, lift),
+            (state, low, faces, star, flux_self, flux_other, source, orientation, lift),
             [floats(NB, COLS)],
             [(DEEP, COLS)],
         )
         received = (place, state, near, upper, lower, slot_flux, slot_code, slot_hot, lift)
         if step + 1 < SUBSTEPS:
-            state, low, faces, pair, far = call(
+            state, low, faces, pair, up, down = call(
                 functools.partial(next_kernel, step=step + 1),
                 received + (star, coarse, labels, weights, lists),
                 [floats(NB, COLS), floats(VPAD, COLS)] + sent_shapes,
@@ -401,9 +488,9 @@
                 scalars=1,
             )
     (result,) = call(
-        last_kernel, received, [floats(NB, NQ, LANES)], [(REM, COLS)], scalars=1
-    )
-    return result
+        last_kernel, received, [floats(NQ, NB, LANES)], [(REM, COLS)], scalars=1
+    )
+    return result.transpose(1, 0, 2)
 
 
 def solution(mesh):

time: 83.9 us -> 83.1 us (level)
  starting transfers between devices: 39.6 us -> 49.5 us
  local copies, waits for them, and re-layouts: 6.56 us -> 0.01 us
  waiting for transfers between devices: 13.1 us -> 8.92 us
    ppermute x8, starting transfers between devices: 31.8 us -> 41.8 us  [the longest x4 32.6 us: local(): lax.ppermute(jnp.concatenate([up, near[BOTH:]], axis=0), 'dom', swaps(cou...]
    unnamed x33 -> x0, local copies, waits for them, and re-layouts: 5.67 us -> none
    ppermute x8, waiting for transfers between devices: 8.36 us -> 4.78 us  [the longest x4 4.77 us: local(): lax.ppermute(jnp.concatenate([up, near[BOTH:]], axis=0), 'dom', swaps(cou...]
  transfers between devices with their start and end apart: 12 -> 12, of which waited for: 8 -> 8; matrix products, arithmetic and copies ran while one was open for 0% -> 0% of each run, Pallas kernels for 12% -> 11%
where the time goes in v1:
time: 83.1 us; the launch traced here: 82.7 us
  starting transfers between devices  49.5 us (60%)
  Pallas kernels  24.1 us (29%)
  waiting for transfers between devices  8.92 us (11%)
    ppermute x4, starting transfers between devices, local(): lax.ppermute(jnp.concatenate([up, near[BOTH:]], axis=0), 'dom', swaps(cou...  32.6 us
    pallas_call x10, Pallas kernels, call(): pl.pallas_call(kernel, in_specs=[smem] * scalars + [given] * (len(args) -...  24.1 us
    ppermute x4, starting transfers between devices, local(): lax.ppermute(jnp.concatenate([down, near[BOTH:]], axis=0), 'dom', swaps(c...  9.15 us
    ppermute x4, starting transfers between devices, local(): near = lax.ppermute(pair, 'dom', partners)  7.68 us
    ppermute x4, waiting for transfers between devices, local(): lax.ppermute(jnp.concatenate([up, near[BOTH:]], axis=0), 'dom', swaps(cou...  4.77 us
    ppermute x4, waiting for transfers between devices, local(): near = lax.ppermute(pair, 'dom', partners)  4.14 us
  transfers between devices with their start and end apart: 12, of which 8 were waited for; matrix products, arithmetic and copies ran while one was open for 0% of the time, Pallas kernels for 11%

profile of v1, /device:TPU:384, one launch (start us, length us, event | category | flops | bytes accessed | tf_op | source)
XLA Modules:
  0.0 82.7 jit_solution(11051728265276690846)
XLA Ops:
  0.0 3.8 %shard_map.136 = (f32[56,1152]{1,0:T(8,128)S(1)}, f32[40,1152]{1,0:T(8,128)S(1)}, f32[3,56,1152]{2,1,0:T(8,128)S(1)}, f32[96,1152]{1,0:T(8,128)S(1)}, f32[48,256...) custom-call(s32[1]{0:T(128)} %bitcast.place, ...), custom_call_target="tpu_custom_call" | custom-call | flops 20000000 | bytes 3320572 | tf_op jit(solution)/shard_map/pallas_call | solution.py:403
  3.8 1.9 %collective-permute-start = (f32[48,256]{1,0:T(8,128)S(1)}, f32[48,256]{1,0:T(8,128)S(1)}, u32[]{:S(2)}, u32[]{:S(2)}) collective-permute-start(f32[48,256]{1,0:T(8,128)S(1)} %get-tuple-element.63), channel_id=1, source_target_pairs={{0,1},{1,0},{2,3},{3,2},{4,5},{5,4},{6,7},{7,6},{8,9},{9,8},{10,11... | collective-permute-start | bytes 147464 | tf_op jit(solution)/shard_map/ppermute | solution.py:470
  5.7 0.6 shard_map.137
  6.4 0.5 collective-permute-done.near
  6.9 3.4 %collective-permute-start.2 = (f32[48,256]{1,0:T(8,128)S(1)}, f32[48,256]{1,0:T(8,128)S(1)}, u32[]{:S(2)}, u32[]{:S(2)}) collective-permute-start(f32[48,256]{1,0:T(8,128)S(1)} %get-tuple-element.97), channel_id=1, source_target_pairs={{0,2},{2,0},{1,3},{3,1},{4,6},{6,4},{5,7},{7,5},{8,10},{10,8},{9,1... | collective-permute-start | bytes 147464 | tf_op jit(solution)/shard_map/ppermute | solution.py:474
  10.3 8.1 %collective-permute-start.1 = (f32[48,256]{1,0:T(8,128)S(1)}, f32[48,256]{1,0:T(8,128)S(1)}, u32[]{:S(2)}, u32[]{:S(2)}) collective-permute-start(f32[48,256]{1,0:T(8,128)S(1)} %get-tuple-element.98), channel_id=1, source_target_pairs={{2,4},{4,2},{3,5},{5,3},{6,8},{8,6},{7,9},{9,7},{10,12},{12,10},{1... | collective-permute-start | bytes 147464 | tf_op jit(solution)/shard_map/ppermute | solution.py:473
  18.4 2.0 %shard_map.138.state = f32[56,1152]{1,0:T(8,128)S(1)} custom-call(f32[56,1152]{1,0:T(8,128)S(1)} %get-tuple-element.48.state, f32[40,1152]{1,0:T(8,128)S(1)} %get-tuple-element.49.low, f32[96,1152]{1,0:T(8,128)S(1)} %get-tuple-element.50.faces, f32[9,9,3,128]{3,2,1,0:T(4,128)S(1)} %get-tuple-element.51.star, ...), custom_call_target="tpu_custom_call" | custom-call | flops 20000000 | bytes 1717760 | tf_op jit(solution)/shard_map/pallas_call | solution.py:403
  20.5 0.0 collective-permute-done.2.lower
  20.5 1.2 %collective-permute-done.1.upper = f32[48,256]{1,0:T(8,128)S(1)} collective-permute-done((f32[48,256]{1,0:T(8,128)S(1)}, f32[48,256]{1,0:T(8,128)S(1)}, u32[]{:S(2)}, u32[]{:S(2)}) %collective-permute-start.1) | collective-permute-done | bytes 49184 | tf_op jit(solution)/shard_map/ppermute | solution.py:473
  21.7 3.3 %shard_map.139 = (f32[56,1152]{1,0:T(8,128)S(1)}, f32[40,1152]{1,0:T(8,128)S(1)}, f32[96,1152]{1,0:T(8,128)S(1)}, f32[48,256]{1,0:T(8,128)S(1)}, f32[24,256]{1,0:T(8,128)S(1)}, /*index=5*/f32[24,256]{1,0:T(8,128)S(1)}) custom-call(s32[1]{0:T(128)} %bitcast.place, f32[56,1152]{1,0:T(8,128)S(1)} %shard_map.138.state, f32[48,256]{1,0:T(8,128)S(1)} %collective-permute-done.near, ...), custom_call_target="tpu_custom_call" | custom-call | flops 20000000 | bytes 2795524 | tf_op jit(solution)/shard_map/pallas_call | solution.py:403
  25.1 1.9 %collective-permute-start.3 = (f32[48,256]{1,0:T(8,128)S(1)}, f32[48,256]{1,0:T(8,128)S(1)}, u32[]{:S(2)}, u32[]{:S(2)}) collective-permute-start(f32[48,256]{1,0:T(8,128)S(1)} %get-tuple-element.76), channel_id=1, source_target_pairs={{0,1},{1,0},{2,3},{3,2},{4,5},{5,4},{6,7},{7,6},{8,9},{9,8},{10,11... | collective-permute-start | bytes 147464 | tf_op jit(solution)/shard_map/ppermute | solution.py:470
  27.0 1.2 %collective-permute-done.3.near = f32[48,256]{1,0:T(8,128)S(1)} collective-permute-done((f32[48,256]{1,0:T(8,128)S(1)}, f32[48,256]{1,0:T(8,128)S(1)}, u32[]{:S(2)}, u32[]{:S(2)}) %collective-permute-start.3) | collective-permute-done | bytes 49184 | tf_op jit(solution)/shard_map/ppermute | solution.py:470
  28.2 1.9 %collective-permute-start.5 = (f32[48,256]{1,0:T(8,128)S(1)}, f32[48,256]{1,0:T(8,128)S(1)}, u32[]{:S(2)}, u32[]{:S(2)}) collective-permute-start(f32[48,256]{1,0:T(8,128)S(1)} %get-tuple-element.95), channel_id=1, source_target_pairs={{0,2},{2,0},{1,3},{3,1},{4,6},{6,4},{5,7},{7,5},{8,10},{10,8},{9,1... | collective-permute-start | bytes 147464 | tf_op jit(solution)/shard_map/ppermute | solution.py:474
  30.1 8.1 %collective-permute-start.4 = (f32[48,256]{1,0:T(8,128)S(1)}, f32[48,256]{1,0:T(8,128)S(1)}, u32[]{:S(2)}, u32[]{:S(2)}) collective-permute-start(f32[48,256]{1,0:T(8,128)S(1)} %get-tuple-element.96), channel_id=1, source_target_pairs={{2,4},{4,2},{3,5},{5,3},{6,8},{8,6},{7,9},{9,7},{10,12},{12,10},{1... | collective-permute-start | bytes 147464 | tf_op jit(solution)/shard_map/ppermute | solution.py:473
  38.3 2.0 %shard_map.140.state = f32[56,1152]{1,0:T(8,128)S(1)} custom-call(f32[56,1152]{1,0:T(8,128)S(1)} %get-tuple-element.73.state, f32[40,1152]{1,0:T(8,128)S(1)} %get-tuple-element.74.low, f32[96,1152]{1,0:T(8,128)S(1)} %get-tuple-element.75.faces, f32[9,9,3,128]{3,2,1,0:T(4,128)S(1)} %get-tuple-element.51.star, ...), custom_call_target="tpu_custom_call" | custom-call | flops 20000000 | bytes 1717760 | tf_op jit(solution)/shard_map/pallas_call | solution.py:403
  40.3 0.0 collective-permute-done.5.lower
  40.3 1.3 %collective-permute-done.4.upper = f32[48,256]{1,0:T(8,128)S(1)} collective-permute-done((f32[48,256]{1,0:T(8,128)S(1)}, f32[48,256]{1,0:T(8,128)S(1)}, u32[]{:S(2)}, u32[]{:S(2)}) %collective-permute-start.4) | collective-permute-done | bytes 49184 | tf_op jit(solution)/shard_map/ppermute | solution.py:473
  41.6 3.3 %shard_map.141 = (f32[56,1152]{1,0:T(8,128)S(1)}, f32[40,1152]{1,0:T(8,128)S(1)}, f32[96,1152]{1,0:T(8,128)S(1)}, f32[48,256]{1,0:T(8,128)S(1)}, f32[24,256]{1,0:T(8,128)S(1)}, /*index=5*/f32[24,256]{1,0:T(8,128)S(1)}) custom-call(s32[1]{0:T(128)} %bitcast.place, f32[56,1152]{1,0:T(8,128)S(1)} %shard_map.140.state, ...), custom_call_target="tpu_custom_call" | custom-call | flops 20000000 | bytes 2795524 | tf_op jit(solution)/shard_map/pallas_call | solution.py:403
  44.9 1.9 %collective-permute-start.6 = (f32[48,256]{1,0:T(8,128)S(1)}, f32[48,256]{1,0:T(8,128)S(1)}, u32[]{:S(2)}, u32[]{:S(2)}) collective-permute-start(f32[48,256]{1,0:T(8,128)S(1)} %get-tuple-element.82), channel_id=1, source_target_pairs={{0,1},{1,0},{2,3},{3,2},{4,5},{5,4},{6,7},{7,6},{8,9},{9,8},{10,11... | collective-permute-start | bytes 147464 | tf_op jit(solution)/shard_map/ppermute | solution.py:470
  46.8 1.2 %collective-permute-done.6.near = f32[48,256]{1,0:T(8,128)S(1)} collective-permute-done((f32[48,256]{1,0:T(8,128)S(1)}, f32[48,256]{1,0:T(8,128)S(1)}, u32[]{:S(2)}, u32[]{:S(2)}) %collective-permute-start.6) | collective-permute-done | bytes 49184 | tf_op jit(solution)/shard_map/ppermute | solution.py:470
  48.0 1.9 %collective-permute-start.8 = (f32[48,256]{1,0:T(8,128)S(1)}, f32[48,256]{1,0:T(8,128)S(1)}, u32[]{:S(2)}, u32[]{:S(2)}) collective-permute-start(f32[48,256]{1,0:T(8,128)S(1)} %get-tuple-element.93), channel_id=1, source_target_pairs={{0,2},{2,0},{1,3},{3,1},{4,6},{6,4},{5,7},{7,5},{8,10},{10,8},{9,1... | collective-permute-start | bytes 147464 | tf_op jit(solution)/shard_map/ppermute | solution.py:474
  49.9 8.3 %collective-permute-start.7 = (f32[48,256]{1,0:T(8,128)S(1)}, f32[48,256]{1,0:T(8,128)S(1)}, u32[]{:S(2)}, u32[]{:S(2)}) collective-permute-start(f32[48,256]{1,0:T(8,128)S(1)} %get-tuple-element.94), channel_id=1, source_target_pairs={{2,4},{4,2},{3,5},{5,3},{6,8},{8,6},{7,9},{9,7},{10,12},{12,10},{1... | collective-permute-start | bytes 147464 | tf_op jit(solution)/shard_map/ppermute | solution.py:473
  58.2 2.0 %shard_map.142.state = f32[56,1152]{1,0:T(8,128)S(1)} custom-call(f32[56,1152]{1,0:T(8,128)S(1)} %get-tuple-element.79.state, f32[40,1152]{1,0:T(8,128)S(1)} %get-tuple-element.80.low, f32[96,1152]{1,0:T(8,128)S(1)} %get-tuple-element.81.faces, f32[9,9,3,128]{3,2,1,0:T(4,128)S(1)} %get-tuple-element.51.star, ...), custom_call_target="tpu_custom_call" | custom-call | flops 20000000 | bytes 1717760 | tf_op jit(solution)/shard_map/pallas_call | solution.py:403
  60.3 0.0 collective-permute-done.8.lower
  60.3 1.1 %collective-permute-done.7.upper = f32[48,256]{1,0:T(8,128)S(1)} collective-permute-done((f32[48,256]{1,0:T(8,128)S(1)}, f32[48,256]{1,0:T(8,128)S(1)}, u32[]{:S(2)}, u32[]{:S(2)}) %collective-permute-start.7) | collective-permute-done | bytes 49184 | tf_op jit(solution)/shard_map/ppermute | solution.py:473
  61.4 3.3 %shard_map.143 = (f32[56,1152]{1,0:T(8,128)S(1)}, f32[40,1152]{1,0:T(8,128)S(1)}, f32[96,1152]{1,0:T(8,128)S(1)}, f32[48,256]{1,0:T(8,128)S(1)}, f32[24,256]{1,0:T(8,128)S(1)}, /*index=5*/f32[24,256]{1,0:T(8,128)S(1)}) custom-call(s32[1]{0:T(128)} %bitcast.place, f32[56,1152]{1,0:T(8,128)S(1)} %shard_map.142.state, ...), custom_call_target="tpu_custom_call" | custom-call | flops 20000000 | bytes 2795524 | tf_op jit(solution)/shard_map/pallas_call | solution.py:403
  64.7 1.9 %collective-permute-start.9 = (f32[48,256]{1,0:T(8,128)S(1)}, f32[48,256]{1,0:T(8,128)S(1)}, u32[]{:S(2)}, u32[]{:S(2)}) collective-permute-start(f32[48,256]{1,0:T(8,128)S(1)} %get-tuple-element.88), channel_id=1, source_target_pairs={{0,1},{1,0},{2,3},{3,2},{4,5},{5,4},{6,7},{7,6},{8,9},{9,8},{10,11... | collective-permute-start | bytes 147464 | tf_op jit(solution)/shard_map/ppermute | solution.py:470
  66.6 1.2 %collective-permute-done.9.near = f32[48,256]{1,0:T(8,128)S(1)} collective-permute-done((f32[48,256]{1,0:T(8,128)S(1)}, f32[48,256]{1,0:T(8,128)S(1)}, u32[]{:S(2)}, u32[]{:S(2)}) %collective-permute-start.9) | collective-permute-done | bytes 49184 | tf_op jit(solution)/shard_map/ppermute | solution.py:470
  67.8 1.9 %collective-permute-start.11 = (f32[48,256]{1,0:T(8,128)S(1)}, f32[48,256]{1,0:T(8,128)S(1)}, u32[]{:S(2)}, u32[]{:S(2)}) collective-permute-start(f32[48,256]{1,0:T(8,128)S(1)} %get-tuple-element.91), channel_id=1, source_target_pairs={{0,2},{2,0},{1,3},{3,1},{4,6},{6,4},{5,7},{7,5},{8,10},{10,8},{9,1... | collective-permute-start | bytes 147464 | tf_op jit(solution)/shard_map/ppermute | solution.py:474
  69.7 8.1 %collective-permute-start.10 = (f32[48,256]{1,0:T(8,128)S(1)}, f32[48,256]{1,0:T(8,128)S(1)}, u32[]{:S(2)}, u32[]{:S(2)}) collective-permute-start(f32[48,256]{1,0:T(8,128)S(1)} %get-tuple-element.92), channel_id=1, source_target_pairs={{2,4},{4,2},{3,5},{5,3},{6,8},{8,6},{7,9},{9,7},{10,12},{12,10},{1... | collective-permute-start | bytes 147464 | tf_op jit(solution)/shard_map/ppermute | solution.py:473
  77.9 2.0 %shard_map.144.state = f32[56,1152]{1,0:T(8,128)S(1)} custom-call(f32[56,1152]{1,0:T(8,128)S(1)} %get-tuple-element.85.state, f32[40,1152]{1,0:T(8,128)S(1)} %get-tuple-element.86.low, f32[96,1152]{1,0:T(8,128)S(1)} %get-tuple-element.87.faces, f32[9,9,3,128]{3,2,1,0:T(4,128)S(1)} %get-tuple-element.51.star, ...), custom_call_target="tpu_custom_call" | custom-call | flops 20000000 | bytes 1717760 | tf_op jit(solution)/shard_map/pallas_call | solution.py:403
  79.9 0.0 collective-permute-done.11.lower
  79.9 1.2 %collective-permute-done.10.upper = f32[48,256]{1,0:T(8,128)S(1)} collective-permute-done((f32[48,256]{1,0:T(8,128)S(1)}, f32[48,256]{1,0:T(8,128)S(1)}, u32[]{:S(2)}, u32[]{:S(2)}) %collective-permute-start.10) | collective-permute-done | bytes 49184 | tf_op jit(solution)/shard_map/ppermute | solution.py:473
  81.2 1.5 %shard_map.145 = f32[9,56,128]{2,1,0:T(8,128)} custom-call(s32[1]{0:T(128)} %bitcast.place, f32[56,1152]{1,0:T(8,128)S(1)} %shard_map.144.state, f32[48,256]{1,0:T(8,128)S(1)} %collective-permute-done.9.near, f32[48,256]{1,0:T(8,128)S(1)} %collective-permute-done.10.upper, f32[48,256]{1,0:T(8,128)S(1)} %collective-permute-done.11.lower, ...), custom_call_target="tpu_custom_call" | custom-call | flops 20000000 | bytes 925700 | tf_op jit(solution)/shard_map/pallas_call | solution.py:403
  (8 shorter events, 0.0 us)
Async XLA Ops:
  3.8 3.1 %collective-permute-start = (f32[48,256]{1,0:T(8,128)S(1)}, f32[48,256]{1,0:T(8,128)S(1)}, u32[]{:S(2)}, u32[]{:S(2)}) collective-permute-start(f32[48,256]{1,0:T(8,128)S(1)} %get-tuple-element.63), channel_id=1, source_target_pairs={{0,1},{1,0},{2,3},{3,2},{4,5},{5,4},{6,7},{7,6},{8,9},{9,8},{10,11... | collective-permute-start | bytes 147464 | tf_op jit(solution)/shard_map/ppermute | solution.py:470
  6.9 13.6 %collective-permute-start.2 = (f32[48,256]{1,0:T(8,128)S(1)}, f32[48,256]{1,0:T(8,128)S(1)}, u32[]{:S(2)}, u32[]{:S(2)}) collective-permute-start(f32[48,256]{1,0:T(8,128)S(1)} %get-tuple-element.97), channel_id=1, source_target_pairs={{0,2},{2,0},{1,3},{3,1},{4,6},{6,4},{5,7},{7,5},{8,10},{10,8},{9,1... | collective-permute-start | bytes 147464 | tf_op jit(solution)/shard_map/ppermute | solution.py:474
  10.3 11.4 %collective-permute-start.1 = (f32[48,256]{1,0:T(8,128)S(1)}, f32[48,256]{1,0:T(8,128)S(1)}, u32[]{:S(2)}, u32[]{:S(2)}) collective-permute-start(f32[48,256]{1,0:T(8,128)S(1)} %get-tuple-element.98), channel_id=1, source_target_pairs={{2,4},{4,2},{3,5},{5,3},{6,8},{8,6},{7,9},{9,7},{10,12},{12,10},{1... | collective-permute-start | bytes 147464 | tf_op jit(solution)/shard_map/ppermute | solution.py:473
  25.1 3.1 %collective-permute-start.3 = (f32[48,256]{1,0:T(8,128)S(1)}, f32[48,256]{1,0:T(8,128)S(1)}, u32[]{:S(2)}, u32[]{:S(2)}) collective-permute-start(f32[48,256]{1,0:T(8,128)S(1)} %get-tuple-element.76), channel_id=1, source_target_pairs={{0,1},{1,0},{2,3},{3,2},{4,5},{5,4},{6,7},{7,6},{8,9},{9,8},{10,11... | collective-permute-start | bytes 147464 | tf_op jit(solution)/shard_map/ppermute | solution.py:470
  28.2 12.1 %collective-permute-start.5 = (f32[48,256]{1,0:T(8,128)S(1)}, f32[48,256]{1,0:T(8,128)S(1)}, u32[]{:S(2)}, u32[]{:S(2)}) collective-permute-start(f32[48,256]{1,0:T(8,128)S(1)} %get-tuple-element.95), channel_id=1, source_target_pairs={{0,2},{2,0},{1,3},{3,1},{4,6},{6,4},{5,7},{7,5},{8,10},{10,8},{9,1... | collective-permute-start | bytes 147464 | tf_op jit(solution)/shard_map/ppermute | solution.py:474
  30.1 11.4 %collective-permute-start.4 = (f32[48,256]{1,0:T(8,128)S(1)}, f32[48,256]{1,0:T(8,128)S(1)}, u32[]{:S(2)}, u32[]{:S(2)}) collective-permute-start(f32[48,256]{1,0:T(8,128)S(1)} %get-tuple-element.96), channel_id=1, source_target_pairs={{2,4},{4,2},{3,5},{5,3},{6,8},{8,6},{7,9},{9,7},{10,12},{12,10},{1... | collective-permute-start | bytes 147464 | tf_op jit(solution)/shard_map/ppermute | solution.py:473
  44.9 3.1 %collective-permute-start.6 = (f32[48,256]{1,0:T(8,128)S(1)}, f32[48,256]{1,0:T(8,128)S(1)}, u32[]{:S(2)}, u32[]{:S(2)}) collective-permute-start(f32[48,256]{1,0:T(8,128)S(1)} %get-tuple-element.82), channel_id=1, source_target_pairs={{0,1},{1,0},{2,3},{3,2},{4,5},{5,4},{6,7},{7,6},{8,9},{9,8},{10,11... | collective-permute-start | bytes 147464 | tf_op jit(solution)/shard_map/ppermute | solution.py:470
  48.0 12.3 %collective-permute-start.8 = (f32[48,256]{1,0:T(8,128)S(1)}, f32[48,256]{1,0:T(8,128)S(1)}, u32[]{:S(2)}, u32[]{:S(2)}) collective-permute-start(f32[48,256]{1,0:T(8,128)S(1)} %get-tuple-element.93), channel_id=1, source_target_pairs={{0,2},{2,0},{1,3},{3,1},{4,6},{6,4},{5,7},{7,5},{8,10},{10,8},{9,1... | collective-permute-start | bytes 147464 | tf_op jit(solution)/shard_map/ppermute | solution.py:474
  49.9 11.4 %collective-permute-start.7 = (f32[48,256]{1,0:T(8,128)S(1)}, f32[48,256]{1,0:T(8,128)S(1)}, u32[]{:S(2)}, u32[]{:S(2)}) collective-permute-start(f32[48,256]{1,0:T(8,128)S(1)} %get-tuple-element.94), channel_id=1, source_target_pairs={{2,4},{4,2},{3,5},{5,3},{6,8},{8,6},{7,9},{9,7},{10,12},{12,10},{1... | collective-permute-start | bytes 147464 | tf_op jit(solution)/shard_map/ppermute | solution.py:473
  64.7 3.1 %collective-permute-start.9 = (f32[48,256]{1,0:T(8,128)S(1)}, f32[48,256]{1,0:T(8,128)S(1)}, u32[]{:S(2)}, u32[]{:S(2)}) collective-permute-start(f32[48,256]{1,0:T(8,128)S(1)} %get-tuple-element.88), channel_id=1, source_target_pairs={{0,1},{1,0},{2,3},{3,2},{4,5},{5,4},{6,7},{7,6},{8,9},{9,8},{10,11... | collective-permute-start | bytes 147464 | tf_op jit(solution)/shard_map/ppermute | solution.py:470
  67.8 12.1 %collective-permute-start.11 = (f32[48,256]{1,0:T(8,128)S(1)}, f32[48,256]{1,0:T(8,128)S(1)}, u32[]{:S(2)}, u32[]{:S(2)}) collective-permute-start(f32[48,256]{1,0:T(8,128)S(1)} %get-tuple-element.91), channel_id=1, source_target_pairs={{0,2},{2,0},{1,3},{3,1},{4,6},{6,4},{5,7},{7,5},{8,10},{10,8},{9,1... | collective-permute-start | bytes 147464 | tf_op jit(solution)/shard_map/ppermute | solution.py:474
  69.7 11.4 %collective-permute-start.10 = (f32[48,256]{1,0:T(8,128)S(1)}, f32[48,256]{1,0:T(8,128)S(1)}, u32[]{:S(2)}, u32[]{:S(2)}) collective-permute-start(f32[48,256]{1,0:T(8,128)S(1)} %get-tuple-element.92), channel_id=1, source_target_pairs={{2,4},{4,2},{3,5},{5,3},{6,8},{8,6},{7,9},{9,7},{10,12},{12,10},{1... | collective-permute-start | bytes 147464 | tf_op jit(solution)/shard_map/ppermute | solution.py:473

commit v2 on v1

--- a/solution.py
+++ b/solution.py
@@ -470,8 +470,11 @@
         near = lax.ppermute(pair, "dom", partners)
         if step == 0:
             up, down, lift = lax.optimization_barrier((up, down, lift))
-        upper = lax.ppermute(jnp.concatenate([up, near[BOTH:]], axis=0), "dom", swaps(count, 2))
-        lower = lax.ppermute(jnp.concatenate([down, near[BOTH:]], axis=0), "dom", swaps(count, 0))
+        lower = jnp.concatenate([down, near[BOTH:]], axis=0)
+        lower, up, relayed = lax.optimization_barrier((lower, up, near[BOTH:]))
+        upper = jnp.concatenate([up, relayed], axis=0)
+        upper = lax.ppermute(upper, "dom", swaps(count, 2))
+        lower = lax.ppermute(lower, "dom", swaps(count, 0))
         (state,) = call(
             local_kernel,
             (state, low, faces, star, flux_self, flux_other, source, orientation, lift),

time: 83.1 us -> 77.8 us (0.936)
  starting transfers between devices: 49.5 us -> 41 us
  waiting for transfers between devices: 8.92 us -> 12 us
    ppermute x8, starting transfers between devices: 41.8 us -> 33.3 us  [the longest x4 25.5 us: local(): upper = lax.ppermute(upper, 'dom', swaps(count, 2))]
    ppermute x8, waiting for transfers between devices: 4.78 us -> 7.88 us  [the longest x4 5.44 us: local(): upper = lax.ppermute(upper, 'dom', swaps(count, 2))]
  transfers between devices with their start and end apart: 12 -> 12, of which waited for: 8 -> 9; matrix products, arithmetic and copies ran while one was open for 0% -> 0% of each run, Pallas kernels for 11% -> 11%
where the time goes in v2:
time: 77.8 us; the launch traced here: 77.3 us
  starting transfers between devices  41 us (53%)
  Pallas kernels  24 us (31%)
  waiting for transfers between devices  12 us (15%)
    ppermute x4, starting transfers between devices, local(): upper = lax.ppermute(upper, 'dom', swaps(count, 2))  25.5 us
    pallas_call x10, Pallas kernels, call(): pl.pallas_call(kernel, in_specs=[smem] * scalars + [given] * (len(args) -...  24 us
    ppermute x4, starting transfers between devices, local(): lower = lax.ppermute(lower, 'dom', swaps(count, 0))  7.86 us
    ppermute x4, starting transfers between devices, local(): near = lax.ppermute(pair, 'dom', partners)  7.68 us
    ppermute x4, waiting for transfers between devices, local(): upper = lax.ppermute(upper, 'dom', swaps(count, 2))  5.44 us
    ppermute x4, waiting for transfers between devices, local(): near = lax.ppermute(pair, 'dom', partners)  4.14 us
    ppermute x4, waiting for transfers between devices, local(): lower = lax.ppermute(lower, 'dom', swaps(count, 0))  2.44 us
  transfers between devices with their start and end apart: 12, of which 9 were waited for; matrix products, arithmetic and copies ran while one was open for 0% of the time, Pallas kernels for 11%

profile of v2, /device:TPU:384, one launch (start us, length us, event | category | flops | bytes accessed | tf_op | source)
XLA Modules:
  0.0 77.3 jit_solution(1827741462303994507)
XLA Ops:
  0.0 3.8 %shard_map.136 = (f32[56,1152]{1,0:T(8,128)S(1)}, f32[40,1152]{1,0:T(8,128)S(1)}, f32[3,56,1152]{2,1,0:T(8,128)S(1)}, f32[96,1152]{1,0:T(8,128)S(1)}, f32[48,256...) custom-call(s32[1]{0:T(128)} %bitcast.place, ...), custom_call_target="tpu_custom_call" | custom-call | flops 20000000 | bytes 3320572 | tf_op jit(solution)/shard_map/pallas_call | solution.py:403
  3.8 1.9 %collective-permute-start = (f32[48,256]{1,0:T(8,128)S(1)}, f32[48,256]{1,0:T(8,128)S(1)}, u32[]{:S(2)}, u32[]{:S(2)}) collective-permute-start(f32[48,256]{1,0:T(8,128)S(1)} %get-tuple-element.75), channel_id=1, source_target_pairs={{0,1},{1,0},{2,3},{3,2},{4,5},{5,4},{6,7},{7,6},{8,9},{9,8},{10,11... | collective-permute-start | bytes 147464 | tf_op jit(solution)/shard_map/ppermute | solution.py:470
  5.7 0.6 shard_map.137
  6.4 0.5 collective-permute-done.near
  6.9 8.8 %collective-permute-start.1 = (f32[48,256]{1,0:T(8,128)S(1)}, f32[48,256]{1,0:T(8,128)S(1)}, u32[]{:S(2)}, u32[]{:S(2)}) collective-permute-start(f32[48,256]{1,0:T(8,128)S(1)} %pad_maximum_fusion.1), channel_id=1, source_target_pairs={{2,4},{4,2},{3,5},{5,3},{6,8},{8,6},{7,9},{9,7},{10,12},{12,10},{1... | collective-permute-start | bytes 147464 | tf_op jit(solution)/shard_map/ppermute | solution.py:476
  15.7 1.9 %collective-permute-start.2 = (f32[48,256]{1,0:T(8,128)S(1)}, f32[48,256]{1,0:T(8,128)S(1)}, u32[]{:S(2)}, u32[]{:S(2)}) collective-permute-start(f32[48,256]{1,0:T(8,128)S(1)} %pad_maximum_fusion), channel_id=1, source_target_pairs={{0,2},{2,0},{1,3},{3,1},{4,6},{6,4},{5,7},{7,5},{8,10},{10,8},{9,1... | collective-permute-start | bytes 147464 | tf_op jit(solution)/shard_map/ppermute | solution.py:477
  17.6 2.0 %shard_map.138.state = f32[56,1152]{1,0:T(8,128)S(1)} custom-call(f32[56,1152]{1,0:T(8,128)S(1)} %get-tuple-element.60.state, f32[40,1152]{1,0:T(8,128)S(1)} %get-tuple-element.61.low, f32[96,1152]{1,0:T(8,128)S(1)} %get-tuple-element.62.faces, f32[9,9,3,128]{3,2,1,0:T(4,128)S(1)} %get-tuple-element.63.star, ...), custom_call_target="tpu_custom_call" | custom-call | flops 20000000 | bytes 1717760 | tf_op jit(solution)/shard_map/pallas_call | solution.py:403
  19.7 0.0 collective-permute-done.1.upper
  19.7 2.0 %collective-permute-done.2.lower = f32[48,256]{1,0:T(8,128)S(1)} collective-permute-done((f32[48,256]{1,0:T(8,128)S(1)}, f32[48,256]{1,0:T(8,128)S(1)}, u32[]{:S(2)}, u32[]{:S(2)}) %collective-permute-start.2) | collective-permute-done | bytes 49184 | tf_op jit(solution)/shard_map/ppermute | solution.py:477
  21.7 3.3 %shard_map.139 = (f32[56,1152]{1,0:T(8,128)S(1)}, f32[40,1152]{1,0:T(8,128)S(1)}, f32[96,1152]{1,0:T(8,128)S(1)}, f32[48,256]{1,0:T(8,128)S(1)}, f32[24,256]{1,0:T(8,128)S(1)}, /*index=5*/f32[24,256]{1,0:T(8,128)S(1)}) custom-call(s32[1]{0:T(128)} %bitcast.place, f32[56,1152]{1,0:T(8,128)S(1)} %shard_map.138.state, f32[48,256]{1,0:T(8,128)S(1)} %collective-permute-done.near, ...), custom_call_target="tpu_custom_call" | custom-call | flops 20000000 | bytes 2795524 | tf_op jit(solution)/shard_map/pallas_call | solution.py:403
  25.0 1.9 %collective-permute-start.3 = (f32[48,256]{1,0:T(8,128)S(1)}, f32[48,256]{1,0:T(8,128)S(1)}, u32[]{:S(2)}, u32[]{:S(2)}) collective-permute-start(f32[48,256]{1,0:T(8,128)S(1)} %get-tuple-element.91), channel_id=1, source_target_pairs={{0,1},{1,0},{2,3},{3,2},{4,5},{5,4},{6,7},{7,6},{8,9},{9,8},{10,11... | collective-permute-start | bytes 147464 | tf_op jit(solution)/shard_map/ppermute | solution.py:470
  27.0 1.2 %collective-permute-done.3.near = f32[48,256]{1,0:T(8,128)S(1)} collective-permute-done((f32[48,256]{1,0:T(8,128)S(1)}, f32[48,256]{1,0:T(8,128)S(1)}, u32[]{:S(2)}, u32[]{:S(2)}) %collective-permute-start.3) | collective-permute-done | bytes 49184 | tf_op jit(solution)/shard_map/ppermute | solution.py:470
  28.2 5.4 %collective-permute-start.4 = (f32[48,256]{1,0:T(8,128)S(1)}, f32[48,256]{1,0:T(8,128)S(1)}, u32[]{:S(2)}, u32[]{:S(2)}) collective-permute-start(f32[48,256]{1,0:T(8,128)S(1)} %pad_maximum_fusion.3), channel_id=1, source_target_pairs={{2,4},{4,2},{3,5},{5,3},{6,8},{8,6},{7,9},{9,7},{10,12},{12,10},{1... | collective-permute-start | bytes 147464 | tf_op jit(solution)/shard_map/ppermute | solution.py:476
  33.6 1.9 %collective-permute-start.5 = (f32[48,256]{1,0:T(8,128)S(1)}, f32[48,256]{1,0:T(8,128)S(1)}, u32[]{:S(2)}, u32[]{:S(2)}) collective-permute-start(f32[48,256]{1,0:T(8,128)S(1)} %pad_maximum_fusion.2), channel_id=1, source_target_pairs={{0,2},{2,0},{1,3},{3,1},{4,6},{6,4},{5,7},{7,5},{8,10},{10,8},{9,1... | collective-permute-start | bytes 147464 | tf_op jit(solution)/shard_map/ppermute | solution.py:477
  35.5 2.0 %shard_map.140.state = f32[56,1152]{1,0:T(8,128)S(1)} custom-call(f32[56,1152]{1,0:T(8,128)S(1)} %get-tuple-element.88.state, f32[40,1152]{1,0:T(8,128)S(1)} %get-tuple-element.89.low, f32[96,1152]{1,0:T(8,128)S(1)} %get-tuple-element.90.faces, f32[9,9,3,128]{3,2,1,0:T(4,128)S(1)} %get-tuple-element.63.star, ...), custom_call_target="tpu_custom_call" | custom-call | flops 20000000 | bytes 1717760 | tf_op jit(solution)/shard_map/pallas_call | solution.py:403
  37.6 2.0 %collective-permute-done.4.upper = f32[48,256]{1,0:T(8,128)S(1)} collective-permute-done((f32[48,256]{1,0:T(8,128)S(1)}, f32[48,256]{1,0:T(8,128)S(1)}, u32[]{:S(2)}, u32[]{:S(2)}) %collective-permute-start.4) | collective-permute-done | bytes 49184 | tf_op jit(solution)/shard_map/ppermute | solution.py:476
  39.6 0.0 collective-permute-done.5.lower
  39.6 3.3 %shard_map.141 = (f32[56,1152]{1,0:T(8,128)S(1)}, f32[40,1152]{1,0:T(8,128)S(1)}, f32[96,1152]{1,0:T(8,128)S(1)}, f32[48,256]{1,0:T(8,128)S(1)}, f32[24,256]{1,0:T(8,128)S(1)}, /*index=5*/f32[24,256]{1,0:T(8,128)S(1)}) custom-call(s32[1]{0:T(128)} %bitcast.place, f32[56,1152]{1,0:T(8,128)S(1)} %shard_map.140.state, ...), custom_call_target="tpu_custom_call" | custom-call | flops 20000000 | bytes 2795524 | tf_op jit(solution)/shard_map/pallas_call | solution.py:403
  42.9 1.9 %collective-permute-start.6 = (f32[48,256]{1,0:T(8,128)S(1)}, f32[48,256]{1,0:T(8,128)S(1)}, u32[]{:S(2)}, u32[]{:S(2)}) collective-permute-start(f32[48,256]{1,0:T(8,128)S(1)} %get-tuple-element.100), channel_id=1, source_target_pairs={{0,1},{1,0},{2,3},{3,2},{4,5},{5,4},{6,7},{7,6},{8,9},{9,8},{10,11... | collective-permute-start | bytes 147464 | tf_op jit(solution)/shard_map/ppermute | solution.py:470
  44.8 1.2 %collective-permute-done.6.near = f32[48,256]{1,0:T(8,128)S(1)} collective-permute-done((f32[48,256]{1,0:T(8,128)S(1)}, f32[48,256]{1,0:T(8,128)S(1)}, u32[]{:S(2)}, u32[]{:S(2)}) %collective-permute-start.6) | collective-permute-done | bytes 49184 | tf_op jit(solution)/shard_map/ppermute | solution.py:470
  46.1 5.8 %collective-permute-start.7 = (f32[48,256]{1,0:T(8,128)S(1)}, f32[48,256]{1,0:T(8,128)S(1)}, u32[]{:S(2)}, u32[]{:S(2)}) collective-permute-start(f32[48,256]{1,0:T(8,128)S(1)} %pad_maximum_fusion.5), channel_id=1, source_target_pairs={{2,4},{4,2},{3,5},{5,3},{6,8},{8,6},{7,9},{9,7},{10,12},{12,10},{1... | collective-permute-start | bytes 147464 | tf_op jit(solution)/shard_map/ppermute | solution.py:476
  51.9 2.1 %collective-permute-start.8 = (f32[48,256]{1,0:T(8,128)S(1)}, f32[48,256]{1,0:T(8,128)S(1)}, u32[]{:S(2)}, u32[]{:S(2)}) collective-permute-start(f32[48,256]{1,0:T(8,128)S(1)} %pad_maximum_fusion.4), channel_id=1, source_target_pairs={{0,2},{2,0},{1,3},{3,1},{4,6},{6,4},{5,7},{7,5},{8,10},{10,8},{9,1... | collective-permute-start | bytes 147464 | tf_op jit(solution)/shard_map/ppermute | solution.py:477
  54.0 2.0 %shard_map.142.state = f32[56,1152]{1,0:T(8,128)S(1)} custom-call(f32[56,1152]{1,0:T(8,128)S(1)} %get-tuple-element.97.state, f32[40,1152]{1,0:T(8,128)S(1)} %get-tuple-element.98.low, f32[96,1152]{1,0:T(8,128)S(1)} %get-tuple-element.99.faces, f32[9,9,3,128]{3,2,1,0:T(4,128)S(1)} %get-tuple-element.63.star, ...), custom_call_target="tpu_custom_call" | custom-call | flops 20000000 | bytes 1717760 | tf_op jit(solution)/shard_map/pallas_call | solution.py:403
  56.0 1.4 %collective-permute-done.7.upper = f32[48,256]{1,0:T(8,128)S(1)} collective-permute-done((f32[48,256]{1,0:T(8,128)S(1)}, f32[48,256]{1,0:T(8,128)S(1)}, u32[]{:S(2)}, u32[]{:S(2)}) %collective-permute-start.7) | collective-permute-done | bytes 49184 | tf_op jit(solution)/shard_map/ppermute | solution.py:476
  57.5 0.4 collective-permute-done.8.lower
  57.9 3.3 %shard_map.143 = (f32[56,1152]{1,0:T(8,128)S(1)}, f32[40,1152]{1,0:T(8,128)S(1)}, f32[96,1152]{1,0:T(8,128)S(1)}, f32[48,256]{1,0:T(8,128)S(1)}, f32[24,256]{1,0:T(8,128)S(1)}, /*index=5*/f32[24,256]{1,0:T(8,128)S(1)}) custom-call(s32[1]{0:T(128)} %bitcast.place, f32[56,1152]{1,0:T(8,128)S(1)} %shard_map.142.state, ...), custom_call_target="tpu_custom_call" | custom-call | flops 20000000 | bytes 2795524 | tf_op jit(solution)/shard_map/pallas_call | solution.py:403
  61.2 1.9 %collective-permute-start.9 = (f32[48,256]{1,0:T(8,128)S(1)}, f32[48,256]{1,0:T(8,128)S(1)}, u32[]{:S(2)}, u32[]{:S(2)}) collective-permute-start(f32[48,256]{1,0:T(8,128)S(1)} %get-tuple-element.109), channel_id=1, source_target_pairs={{0,1},{1,0},{2,3},{3,2},{4,5},{5,4},{6,7},{7,6},{8,9},{9,8},{10,11... | collective-permute-start | bytes 147464 | tf_op jit(solution)/shard_map/ppermute | solution.py:470
  63.1 1.2 %collective-permute-done.9.near = f32[48,256]{1,0:T(8,128)S(1)} collective-permute-done((f32[48,256]{1,0:T(8,128)S(1)}, f32[48,256]{1,0:T(8,128)S(1)}, u32[]{:S(2)}, u32[]{:S(2)}) %collective-permute-start.9) | collective-permute-done | bytes 49184 | tf_op jit(solution)/shard_map/ppermute | solution.py:470
  64.4 5.4 %collective-permute-start.10 = (f32[48,256]{1,0:T(8,128)S(1)}, f32[48,256]{1,0:T(8,128)S(1)}, u32[]{:S(2)}, u32[]{:S(2)}) collective-permute-start(f32[48,256]{1,0:T(8,128)S(1)} %pad_maximum_fusion.7), channel_id=1, source_target_pairs={{2,4},{4,2},{3,5},{5,3},{6,8},{8,6},{7,9},{9,7},{10,12},{12,10},{1... | collective-permute-start | bytes 147464 | tf_op jit(solution)/shard_map/ppermute | solution.py:476
  69.8 1.9 %collective-permute-start.11 = (f32[48,256]{1,0:T(8,128)S(1)}, f32[48,256]{1,0:T(8,128)S(1)}, u32[]{:S(2)}, u32[]{:S(2)}) collective-permute-start(f32[48,256]{1,0:T(8,128)S(1)} %pad_maximum_fusion.6), channel_id=1, source_target_pairs={{0,2},{2,0},{1,3},{3,1},{4,6},{6,4},{5,7},{7,5},{8,10},{10,8},{9,1... | collective-permute-start | bytes 147464 | tf_op jit(solution)/shard_map/ppermute | solution.py:477
  71.7 2.0 %shard_map.144.state = f32[56,1152]{1,0:T(8,128)S(1)} custom-call(f32[56,1152]{1,0:T(8,128)S(1)} %get-tuple-element.106.state, f32[40,1152]{1,0:T(8,128)S(1)} %get-tuple-element.107.low, f32[96,1152]{1,0:T(8,128)S(1)} %get-tuple-element.108.faces, f32[9,9,3,128]{3,2,1,0:T(4,128)S(1)} %get-tuple-element.63.star, ...), custom_call_target="tpu_custom_call" | custom-call | flops 20000000 | bytes 1717760 | tf_op jit(solution)/shard_map/pallas_call | solution.py:403
  73.8 2.0 %collective-permute-done.10.upper = f32[48,256]{1,0:T(8,128)S(1)} collective-permute-done((f32[48,256]{1,0:T(8,128)S(1)}, f32[48,256]{1,0:T(8,128)S(1)}, u32[]{:S(2)}, u32[]{:S(2)}) %collective-permute-start.10) | collective-permute-done | bytes 49184 | tf_op jit(solution)/shard_map/ppermute | solution.py:476
  75.8 0.0 collective-permute-done.11.lower
  75.8 1.5 %shard_map.145 = f32[9,56,128]{2,1,0:T(8,128)} custom-call(s32[1]{0:T(128)} %bitcast.place, f32[56,1152]{1,0:T(8,128)S(1)} %shard_map.144.state, f32[48,256]{1,0:T(8,128)S(1)} %collective-permute-done.9.near, f32[48,256]{1,0:T(8,128)S(1)} %collective-permute-done.10.upper, f32[48,256]{1,0:T(8,128)S(1)} %collective-permute-done.11.lower, ...), custom_call_target="tpu_custom_call" | custom-call | flops 20000000 | bytes 925700 | tf_op jit(solution)/shard_map/pallas_call | solution.py:403
  (12 shorter events, 0.1 us)
Async XLA Ops:
  3.8 3.1 %collective-permute-start = (f32[48,256]{1,0:T(8,128)S(1)}, f32[48,256]{1,0:T(8,128)S(1)}, u32[]{:S(2)}, u32[]{:S(2)}) collective-permute-start(f32[48,256]{1,0:T(8,128)S(1)} %get-tuple-element.75), channel_id=1, source_target_pairs={{0,1},{1,0},{2,3},{3,2},{4,5},{5,4},{6,7},{7,6},{8,9},{9,8},{10,11... | collective-permute-start | bytes 147464 | tf_op jit(solution)/shard_map/ppermute | solution.py:470
  6.9 12.7 %collective-permute-start.1 = (f32[48,256]{1,0:T(8,128)S(1)}, f32[48,256]{1,0:T(8,128)S(1)}, u32[]{:S(2)}, u32[]{:S(2)}) collective-permute-start(f32[48,256]{1,0:T(8,128)S(1)} %pad_maximum_fusion.1), channel_id=1, source_target_pairs={{2,4},{4,2},{3,5},{5,3},{6,8},{8,6},{7,9},{9,7},{10,12},{12,10},{1... | collective-permute-start | bytes 147464 | tf_op jit(solution)/shard_map/ppermute | solution.py:476
  15.7 6.0 %collective-permute-start.2 = (f32[48,256]{1,0:T(8,128)S(1)}, f32[48,256]{1,0:T(8,128)S(1)}, u32[]{:S(2)}, u32[]{:S(2)}) collective-permute-start(f32[48,256]{1,0:T(8,128)S(1)} %pad_maximum_fusion), channel_id=1, source_target_pairs={{0,2},{2,0},{1,3},{3,1},{4,6},{6,4},{5,7},{7,5},{8,10},{10,8},{9,1... | collective-permute-start | bytes 147464 | tf_op jit(solution)/shard_map/ppermute | solution.py:477
  25.0 3.1 %collective-permute-start.3 = (f32[48,256]{1,0:T(8,128)S(1)}, f32[48,256]{1,0:T(8,128)S(1)}, u32[]{:S(2)}, u32[]{:S(2)}) collective-permute-start(f32[48,256]{1,0:T(8,128)S(1)} %get-tuple-element.91), channel_id=1, source_target_pairs={{0,1},{1,0},{2,3},{3,2},{4,5},{5,4},{6,7},{7,6},{8,9},{9,8},{10,11... | collective-permute-start | bytes 147464 | tf_op jit(solution)/shard_map/ppermute | solution.py:470
  28.2 11.4 %collective-permute-start.4 = (f32[48,256]{1,0:T(8,128)S(1)}, f32[48,256]{1,0:T(8,128)S(1)}, u32[]{:S(2)}, u32[]{:S(2)}) collective-permute-start(f32[48,256]{1,0:T(8,128)S(1)} %pad_maximum_fusion.3), channel_id=1, source_target_pairs={{2,4},{4,2},{3,5},{5,3},{6,8},{8,6},{7,9},{9,7},{10,12},{12,10},{1... | collective-permute-start | bytes 147464 | tf_op jit(solution)/shard_map/ppermute | solution.py:476
  33.6 6.0 %collective-permute-start.5 = (f32[48,256]{1,0:T(8,128)S(1)}, f32[48,256]{1,0:T(8,128)S(1)}, u32[]{:S(2)}, u32[]{:S(2)}) collective-permute-start(f32[48,256]{1,0:T(8,128)S(1)} %pad_maximum_fusion.2), channel_id=1, source_target_pairs={{0,2},{2,0},{1,3},{3,1},{4,6},{6,4},{5,7},{7,5},{8,10},{10,8},{9,1... | collective-permute-start | bytes 147464 | tf_op jit(solution)/shard_map/ppermute | solution.py:477
  42.9 3.1 %collective-permute-start.6 = (f32[48,256]{1,0:T(8,128)S(1)}, f32[48,256]{1,0:T(8,128)S(1)}, u32[]{:S(2)}, u32[]{:S(2)}) collective-permute-start(f32[48,256]{1,0:T(8,128)S(1)} %get-tuple-element.100), channel_id=1, source_target_pairs={{0,1},{1,0},{2,3},{3,2},{4,5},{5,4},{6,7},{7,6},{8,9},{9,8},{10,11... | collective-permute-start | bytes 147464 | tf_op jit(solution)/shard_map/ppermute | solution.py:470
  46.1 11.4 %collective-permute-start.7 = (f32[48,256]{1,0:T(8,128)S(1)}, f32[48,256]{1,0:T(8,128)S(1)}, u32[]{:S(2)}, u32[]{:S(2)}) collective-permute-start(f32[48,256]{1,0:T(8,128)S(1)} %pad_maximum_fusion.5), channel_id=1, source_target_pairs={{2,4},{4,2},{3,5},{5,3},{6,8},{8,6},{7,9},{9,7},{10,12},{12,10},{1... | collective-permute-start | bytes 147464 | tf_op jit(solution)/shard_map/ppermute | solution.py:476
  51.9 6.0 %collective-permute-start.8 = (f32[48,256]{1,0:T(8,128)S(1)}, f32[48,256]{1,0:T(8,128)S(1)}, u32[]{:S(2)}, u32[]{:S(2)}) collective-permute-start(f32[48,256]{1,0:T(8,128)S(1)} %pad_maximum_fusion.4), channel_id=1, source_target_pairs={{0,2},{2,0},{1,3},{3,1},{4,6},{6,4},{5,7},{7,5},{8,10},{10,8},{9,1... | collective-permute-start | bytes 147464 | tf_op jit(solution)/shard_map/ppermute | solution.py:477
  61.2 3.1 %collective-permute-start.9 = (f32[48,256]{1,0:T(8,128)S(1)}, f32[48,256]{1,0:T(8,128)S(1)}, u32[]{:S(2)}, u32[]{:S(2)}) collective-permute-start(f32[48,256]{1,0:T(8,128)S(1)} %get-tuple-element.109), channel_id=1, source_target_pairs={{0,1},{1,0},{2,3},{3,2},{4,5},{5,4},{6,7},{7,6},{8,9},{9,8},{10,11... | collective-permute-start | bytes 147464 | tf_op jit(solution)/shard_map/ppermute | solution.py:470
  64.4 11.4 %collective-permute-start.10 = (f32[48,256]{1,0:T(8,128)S(1)}, f32[48,256]{1,0:T(8,128)S(1)}, u32[]{:S(2)}, u32[]{:S(2)}) collective-permute-start(f32[48,256]{1,0:T(8,128)S(1)} %pad_maximum_fusion.7), channel_id=1, source_target_pairs={{2,4},{4,2},{3,5},{5,3},{6,8},{8,6},{7,9},{9,7},{10,12},{12,10},{1... | collective-permute-start | bytes 147464 | tf_op jit(solution)/shard_map/ppermute | solution.py:476
  69.8 6.0 %collective-permute-start.11 = (f32[48,256]{1,0:T(8,128)S(1)}, f32[48,256]{1,0:T(8,128)S(1)}, u32[]{:S(2)}, u32[]{:S(2)}) collective-permute-start(f32[48,256]{1,0:T(8,128)S(1)} %pad_maximum_fusion.6), channel_id=1, source_target_pairs={{0,2},{2,0},{1,3},{3,1},{4,6},{6,4},{5,7},{7,5},{8,10},{10,8},{9,1... | collective-permute-start | bytes 147464 | tf_op jit(solution)/shard_map/ppermute | solution.py:477

commit v3 on v2

--- a/solution.py
+++ b/solution.py
@@ -24,12 +24,16 @@
 COLS = NQ * LANES
 FACES = 4 * LANES
 REM = 12 * FPAD
+SLOT_PAD = 32
+SLOT_REM = 12 * SLOT_PAD
 OWN = 4 * FPAD
 DEEP = REM + OWN + 3 * VPAD
 DEEP_PAD = 512
-LEVELS = [(0, 35, 40, 56), (120, 20, 24, 40), (192, 10, 16, 24), (240, 4, 8, 16), (264, 1, 8, 8)]
-BACK = 288
+LEVELS = [(0, 35, 40, 128), (128, 20, 24, 80), (208, 10, 16, 48), (256, 4, 8, 32), (288, 1, 8, 32)]
+BACK = 320
 CHAIN_ROWS = BACK + OWN
+TAIL = 96
+PART = 64
 HIGH = lax.Precision.HIGH
 HIGHEST = lax.Precision.HIGHEST
 F32 = jnp.float32
@@ -56,18 +60,44 @@
     return top, (value - top.astype(F32)).astype(BF16)
 
 
-def pick(value, hot, contract=((1,), (0,))):
-    top, rest = halves(value)
-    dims = (contract, ((), ()))
-    return lax.dot_general(top, hot, dims, preferred_element_type=F32) + lax.dot_general(
-        rest, hot, dims, preferred_element_type=F32
-    )
+def pick(value, hot):
+    return jnp.dot(
+        jnp.concatenate(halves(value), axis=1),
+        jnp.concatenate([hot, hot], axis=0),
+        preferred_element_type=F32,
+    )
+
+
+def pick_rows(hot, value):
+    return lax.dot_general(
+        jnp.concatenate([hot, hot], axis=1),
+        jnp.concatenate(halves(value), axis=1),
+        (((1,), (1,)), ((), ())),
+        preferred_element_type=F32,
+    )
+
+
+def pick_across(value, hot):
+    return lax.dot_general(
+        jnp.concatenate(halves(value), axis=1),
+        jnp.concatenate([hot, hot], axis=1),
+        (((1,), (1,)), ((), ())),
+        preferred_element_type=F32,
+    )
+
+
+def stacked(value):
+    top = value.astype(BF16).astype(F32)
+    rest = value - top
+    fill = PART - value.shape[0]
+    gap = [jnp.zeros((fill, value.shape[1]), F32)] if fill else []
+    return jnp.concatenate([top] + gap + [rest] + gap + [top] + gap, axis=0).astype(BF16)
 
 
 def products(blocks, row_of, rows):
     totals = [None] * NQ
-    for position, block in enumerate(blocks):
-        for q in range(NQ):
+    for q in range(NQ):
+        for position, block in enumerate(blocks):
             left = block(q)
             for p in range(NQ):
                 term = left * row_of(position, q, p)
@@ -75,28 +105,32 @@
     return totals
 
 
-def chain_weights(stiff_time, face_back, out):
-    out[...] = jnp.zeros(out.shape, F32)
+def chain_weights(stiff_time, face_back, out, raw):
+    raw[...] = jnp.zeros(raw.shape, F32)
     for start, valid, padded, _ in LEVELS:
         for d in range(3):
-            out[start + d * padded : start + d * padded + valid, 0:NB] = stiff_time[d, 0:valid, :]
+            raw[start + d * padded : start + d * padded + valid, 0:NB] = stiff_time[d, 0:valid, :]
     for j in range(4):
-        out[BACK + j * FPAD : BACK + j * FPAD + NF, 0:NB] = face_back[:, j, :]
-
-
-def chain_of(first, star, weights, terms):
+        raw[BACK + j * FPAD : BACK + j * FPAD + NF, 0:NB] = face_back[:, j, :]
+    once = raw[...]
+    top = once.astype(BF16).astype(F32)
+    out[:, 0:LANES] = (top + pltpu.roll(top, PART, 1)).astype(BF16)
+    out[:, LANES : 2 * LANES] = (once - top).astype(BF16)
+
+
+def weigh(weights, start, rows, value):
+    return jnp.dot(
+        weights[start : start + rows, 0 : 3 * PART], stacked(value), preferred_element_type=F32
+    )
+
+
+def chain_of(first, star, weights):
     now = first
     chain = [first]
-    offset = 0
-    for start, _, padded, width in LEVELS:
-        terms[0 : 3 * padded, :] = jnp.dot(
-            weights[start : start + 3 * padded, 0:width],
-            now,
-            precision=HIGH,
-            preferred_element_type=F32,
-        )
+    for start, _, padded, rows in LEVELS:
+        found = weigh(weights, start, rows, now)
         blocks = [
-            lambda q, d=d: terms[d * padded : (d + 1) * padded, lanes(q)] for d in range(3)
+            lambda q, d=d: found[d * padded : (d + 1) * padded, lanes(q)] for d in range(3)
         ]
         totals = products(blocks, lambda d, q, p: star[q, p, d : d + 1, :], padded)
         now = jnp.concatenate(totals, axis=1)
@@ -131,11 +165,8 @@
 
 
 def project_and_send(integral, weights, lists, position, faces_out, pair_out, up_out, down_out):
-    faces = jnp.dot(
-        weights[BACK : BACK + OWN, 0:NB], integral, precision=HIGH, preferred_element_type=F32
-    )
+    faces = weigh(weights, BACK, OWN, integral)
     faces_out[...] = faces
-    top, rest = halves(face_table(faces))
     hot = jnp.concatenate(
         [
             jnp.where(lists[...] == iota((PEERS * BOTH, LANES), 1) + LANES * j, 1.0, 0.0)
@@ -143,10 +174,7 @@
         ],
         axis=1,
     ).astype(BF16)
-    dims = (((1,), (1,)), ((), ()))
-    sent = lax.dot_general(hot, top, dims, preferred_element_type=F32) + lax.dot_general(
-        hot, rest, dims, preferred_element_type=F32
-    )
+    sent = pick_rows(hot, face_table(faces))
     odd = lax.rem(position, 2) == 1
     first, second = sent[0:BOTH], sent[BOTH : 2 * BOTH]
     pair_out[0:BOTH, :] = jnp.where(odd, second, first)
@@ -176,13 +204,14 @@
 ):
     later = rest[:7]
     (
-        state_out, low_out, coarse_out, faces_out, pair_out, up_out, down_out,
+        state_out, low_out, tail_out, faces_out, pair_out, up_out, down_out,
         weights_out, star_out, labels_out, lists_out,
     ) = rest[7:18]
     later_out = rest[18:25]
-    terms, time_here, back_here, wide, fine_here, coarse_here, ready = rest[25:]
+    raw, dofs_here, time_here, back_here, wide, fine_here, coarse_here, ready = rest[25:]
     position = place[0]
     moves = [
+        (dofs, dofs_here),
         (stiff_time, time_here),
         (face_back, back_here),
         (star, star_out),
@@ -190,7 +219,7 @@
         (coarse_send, coarse_here),
         (labels, labels_out),
     ]
-    moves += [(dofs.at[q], state_out.at[:, lanes(q)]) for q in range(NQ)]
+    first = len(moves)
     moves += list(zip(later, later_out))
     copies = [
         pltpu.make_async_copy(source, target, ready.at[number])
@@ -198,17 +227,17 @@
     ]
     for copy in copies:
         copy.start()
+    for copy in copies[1:3]:
+        copy.wait()
+    chain_weights(time_here, back_here, weights_out, raw)
     copies[0].wait()
-    copies[1].wait()
-    chain_weights(time_here, back_here, weights_out)
-    for copy in copies[6 : 6 + NQ]:
-        copy.wait()
-    copies[2].wait()
-    state = state_out[...]
-    chain = chain_of(state, star_out, weights_out, terms)
+    state = jnp.concatenate([dofs_here[q] for q in range(NQ)], axis=1)
+    state_out[...] = state
+    copies[3].wait()
+    chain = chain_of(state, star_out, weights_out)
     integral = integral_of(chain, taylor_weights(0.0, 1.0 / SUBSTEPS))
     low_out[...] = integral[0:VPAD]
-    for copy in copies[3:6]:
+    for copy in copies[4:first]:
         copy.wait()
     wide[...] = jnp.zeros(wide.shape, F32)
     wide[0:PEERS, 0:SLOTS] = fine_here[...].astype(F32)
@@ -217,18 +246,25 @@
     project_and_send(
         integral, weights_out, lists_out, position, faces_out, pair_out, up_out, down_out
     )
+    tail_out[...] = jnp.concatenate(chain[1:], axis=0)
+    for copy in copies[first:]:
+        copy.wait()
+
+
+def prepare_kernel(
+    state, tail, source, orientation, flux_other, face_front, face_turn, stiff_vol,
+    coarse_out, slot_flux_out, slot_code_out, slot_hot_out, lift_out, slot_lift_out,
+    table, fronts, tall, slot_tall,
+):
+    chain = [state[...]]
+    start = 0
+    for _, _, padded, _ in LEVELS:
+        chain.append(tail[start : start + padded, :])
+        start += padded
     for step in range(1, SUBSTEPS):
         coarse_out[step - 1] = integral_of(
             chain, taylor_weights(step / SUBSTEPS, (step + 1) / SUBSTEPS)
         )
-    for copy in copies[6 + NQ :]:
-        copy.wait()
-
-
-def prepare_kernel(
-    source, orientation, flux_other, face_front, face_turn, stiff_vol,
-    slot_flux_out, slot_code_out, slot_hot_out, lift_out, table, fronts, tall,
-):
     row = iota((LANES, LANES), 0)
     peer = (row >= BOTH).astype(jnp.int32) + (row >= 2 * BOTH).astype(jnp.int32)
     peer = peer + (row >= 3 * BOTH).astype(jnp.int32)
@@ -252,10 +288,11 @@
     for i in range(4):
         for q in range(NQ):
             table[16 * q : 16 * q + NQ, lanes(i)] = flux_other[q, :, i, :]
-    slot_flux_out[...] = pick(table[...], hot, ((1,), (1,)))
+    slot_flux_out[...] = pick_across(table[...], hot)
 
     fronts[...] = jnp.zeros(fronts.shape, F32)
     tall[...] = jnp.zeros(tall.shape, F32)
+    slot_tall[...] = jnp.zeros(slot_tall.shape, F32)
     for i in range(4):
         fronts[0:NF, i * LANES : i * LANES + NB] = face_front[:, i, :]
     for code in range(3):
@@ -266,6 +303,8 @@
         for i in range(4):
             start = FPAD * (3 * i + code)
             tall[start : start + NF, :] = -turned[:, lanes(i)]
+            start = SLOT_PAD * (3 * i + code)
+            slot_tall[start : start + NF, :] = -turned[:, lanes(i)]
     for i in range(4):
         start = REM + FPAD * i
         tall[start : start + NF, :] = -fronts[0:NF, lanes(i)]
@@ -273,6 +312,12 @@
         start = REM + OWN + VPAD * d
         tall[start : start + NLOW, 0:NB] = stiff_vol[d]
     lift_out[...] = jnp.transpose(tall[...])[0:NB]
+    whole = jnp.transpose(slot_tall[...])[0:PART]
+    top = whole.astype(BF16)
+    slot_lift_out[0:PART, 0:SLOT_REM] = top
+    slot_lift_out[0:PART, SLOT_REM:] = top
+    slot_lift_out[PART:, 0:SLOT_REM] = (whole - top.astype(F32)).astype(BF16)
+    slot_lift_out[PART:, SLOT_REM:] = jnp.zeros((PART, SLOT_REM), BF16)
 
 
 def local_kernel(
@@ -342,13 +387,18 @@
         lambda _, q, p: slot_flux[16 * q + p : 16 * q + p + 1, :],
         FPAD,
     )
-    for code in range(12):
-        mask = slot_code[code : code + 1, :]
-        for p in range(NQ):
-            stack[FPAD * code : FPAD * (code + 1), lanes(p)] = totals[p] * mask
-    lifted = jnp.dot(
-        lift[:, 0:REM], stack[...], precision=HIGH, preferred_element_type=F32
-    )
+    codes = [
+        jnp.broadcast_to(slot_code[code : code + 1, :], (SLOT_PAD, LANES)).astype(BF16)
+        for code in range(12)
+    ]
+    gap = jnp.zeros((SLOT_PAD - FPAD, LANES), F32)
+    for p in range(NQ):
+        for half, part in enumerate(halves(jnp.concatenate([totals[p], gap], axis=0))):
+            for code in range(12):
+                start = SLOT_REM * half + SLOT_PAD * code
+                stack[start : start + SLOT_PAD, lanes(p)] = part * codes[code]
+    lifted = jnp.dot(lift[...], stack[...], preferred_element_type=F32)
+    lifted = lifted[0:NB] + lifted[PART : PART + NB]
     by_slot = jnp.concatenate([lifted[:, lanes(p)] for p in range(NQ)], axis=0)
     by_element = pick(by_slot, slot_hot[...].astype(BF16))
     return jnp.concatenate([by_element[p * NB : (p + 1) * NB] for p in range(NQ)], axis=1)
@@ -357,14 +407,14 @@
 def next_kernel(
     place, state, near, upper, lower, slot_flux, slot_code, slot_hot, lift,
     star, coarse, labels, weights, lists,
-    state_out, low_out, faces_out, pair_out, up_out, down_out, stack, terms, *, step,
+    state_out, low_out, faces_out, pair_out, up_out, down_out, stack, *, step,
 ):
     position = place[0]
     now = state[...] + remote_part(
         position, near, upper, lower, slot_flux, slot_code, slot_hot, lift, stack
     )
     state_out[...] = now
-    chain = chain_of(now, star, weights, terms)
+    chain = chain_of(now, star, weights)
     fine = integral_of(chain, taylor_weights(0.0, 1.0 / SUBSTEPS))
     mask = labels[...] == 1
     integral = jnp.concatenate(
@@ -441,30 +491,32 @@
     star = star.transpose(1, 2, 0, 3)
     back = face_back.transpose(1, 0, 2)
     message = floats(BOTH, WIDTH)
+    stack = pltpu.VMEM((2 * SLOT_REM, COLS), BF16)
     sent_shapes = [floats(OWN, COLS), floats(2 * BOTH, WIDTH), message, message]
     like = lambda item: jax.ShapeDtypeStruct(item.shape, item.dtype)
     found = call(
         first_kernel,
         (place, dofs.transpose(1, 0, 2), star, stiff_time, back, fine_send, coarse_send, labels)
         + later,
-        [floats(NB, COLS), floats(VPAD, COLS), floats(SUBSTEPS - 1, NB, COLS)]
+        [floats(NB, COLS), floats(VPAD, COLS), floats(TAIL, COLS)]
         + sent_shapes
-        + [floats(CHAIN_ROWS, LANES), like(star), like(labels)]
+        + [jax.ShapeDtypeStruct((CHAIN_ROWS, 2 * LANES), BF16), like(star), like(labels)]
         + [jax.ShapeDtypeStruct((PEERS * BOTH, LANES), jnp.int32)]
         + [like(item) for item in later],
-        [(120, COLS), stiff_time.shape, back.shape, (16, LANES)]
+        [(CHAIN_ROWS, LANES), (NQ, NB, LANES), stiff_time.shape, back.shape, (16, LANES)]
         + [pltpu.VMEM(item.shape, jnp.int32) for item in (fine_send, coarse_send)]
-        + [pltpu.SemaphoreType.DMA((6 + NQ + len(later),))],
+        + [pltpu.SemaphoreType.DMA((7 + len(later),))],
         scalars=1,
         inside=True,
     )
-    state, low, coarse, faces, pair, up, down, weights, star, labels, lists = found[:11]
+    state, low, tail, faces, pair, up, down, weights, star, labels, lists = found[:11]
     flux_self, flux_other, source, orientation, front, turn, vol = found[11:]
-    slot_flux, slot_code, slot_hot, lift = call(
+    coarse, slot_flux, slot_code, slot_hot, lift, slot_lift = call(
         prepare_kernel,
-        (source, orientation, flux_other, front, turn, vol),
-        [floats(16 * NQ, LANES), floats(16, LANES), floats(LANES, LANES), floats(NB, DEEP_PAD)],
-        [(16 * NQ, FACES), (FPAD, FACES), (DEEP_PAD, LANES)],
+        (state, tail, source, orientation, flux_other, front, turn, vol),
+        [floats(SUBSTEPS - 1, NB, COLS), floats(16 * NQ, LANES), floats(16, LANES), floats(LANES, LANES), floats(NB, DEEP_PAD),
+         jax.ShapeDtypeStruct((2 * PART, 2 * SLOT_REM), BF16)],
+        [(16 * NQ, FACES), (FPAD, FACES), (DEEP_PAD, LANES), (SLOT_REM, LANES)],
     )
     for step in range(SUBSTEPS):
         near = lax.ppermute(pair, "dom", partners)
@@ -481,17 +533,17 @@
             [floats(NB, COLS)],
             [(DEEP, COLS)],
         )
-        received = (place, state, near, upper, lower, slot_flux, slot_code, slot_hot, lift)
+        received = (place, state, near, upper, lower, slot_flux, slot_code, slot_hot, slot_lift)
         if step + 1 < SUBSTEPS:
             state, low, faces, pair, up, down = call(
                 functools.partial(next_kernel, step=step + 1),
                 received + (star, coarse, labels, weights, lists),
                 [floats(NB, COLS), floats(VPAD, COLS)] + sent_shapes,
-                [(REM, COLS), (120, COLS)],
+                [stack],
                 scalars=1,
             )
     (result,) = call(
-        last_kernel, received, [floats(NQ, NB, LANES)], [(REM, COLS)], scalars=1
+        last_kernel, received, [floats(NQ, NB, LANES)], [stack], scalars=1
     )
     return result.transpose(1, 0, 2)
 

time: 77.8 us -> 75.2 us (0.967)
  Pallas kernels: 24 us -> 21.6 us
    pallas_call x10, Pallas kernels: 24 us -> 21.6 us  [call(): pl.pallas_call(kernel, in_specs=[smem] * scalars + [given] * (len(args) -...]
  transfers between devices with their start and end apart: 12 -> 12, of which waited for: 9 -> 9; matrix products, arithmetic and copies ran while one was open for 0% -> 0% of each run, Pallas kernels for 11% -> 12%
where the time goes in v3:
time: 75.2 us; the launch traced here: 74.7 us
  starting transfers between devices  41 us (55%)
  Pallas kernels  21.6 us (29%)
  waiting for transfers between devices  11.9 us (16%)
    ppermute x4, starting transfers between devices, local(): upper = lax.ppermute(upper, 'dom', swaps(count, 2))  25.5 us
    pallas_call x10, Pallas kernels, call(): pl.pallas_call(kernel, in_specs=[smem] * scalars + [given] * (len(args) -...  21.6 us
    ppermute x4, starting transfers between devices, local(): lower = lax.ppermute(lower, 'dom', swaps(count, 0))  7.86 us
    ppermute x4, starting transfers between devices, local(): near = lax.ppermute(pair, 'dom', partners)  7.68 us
    ppermute x4, waiting for transfers between devices, local(): upper = lax.ppermute(upper, 'dom', swaps(count, 2))  5.45 us
    ppermute x4, waiting for transfers between devices, local(): near = lax.ppermute(pair, 'dom', partners)  3.95 us
    ppermute x4, waiting for transfers between devices, local(): lower = lax.ppermute(lower, 'dom', swaps(count, 0))  2.46 us
  transfers between devices with their start and end apart: 12, of which 9 were waited for; matrix products, arithmetic and copies ran while one was open for 0% of the time, Pallas kernels for 12%

profile of v3, /device:TPU:384, one launch (start us, length us, event | category | flops | bytes accessed | tf_op | source)
XLA Modules:
  0.0 74.7 jit_solution(8964936659988704293)
XLA Ops:
  0.0 3.3 %shard_map.136 = (f32[56,1152]{1,0:T(8,128)S(1)}, f32[40,1152]{1,0:T(8,128)S(1)}, f32[96,1152]{1,0:T(8,128)S(1)}, f32[96,1152]{1,0:T(8,128)S(1)}, f32[48,256]{1,...) custom-call(s32[1]{0:T(128)} %bitcast.place, ...), custom_call_target="tpu_custom_call" | custom-call | flops 20000000 | bytes 3218172 | tf_op jit(solution)/shard_map/pallas_call | solution.py:453
  3.3 1.9 %collective-permute-start = (f32[48,256]{1,0:T(8,128)S(1)}, f32[48,256]{1,0:T(8,128)S(1)}, u32[]{:S(2)}, u32[]{:S(2)}) collective-permute-start(f32[48,256]{1,0:T(8,128)S(1)} %get-tuple-element.78), channel_id=1, source_target_pairs={{0,1},{1,0},{2,3},{3,2},{4,5},{5,4},{6,7},{7,6},{8,9},{9,8},{10,11... | collective-permute-start | bytes 147464 | tf_op jit(solution)/shard_map/ppermute | solution.py:522
  5.3 0.8 %shard_map.137 = (f32[3,56,1152]{2,1,0:T(8,128)S(1)}, f32[144,128]{1,0:T(8,128)S(1)}, f32[16,128]{1,0:T(8,128)S(1)}, f32[128,128]{1,0:T(8,128)S(1)}, f32[56,512]...) custom-call(f32[56,1152]{1,0:T(8,128)S(1)} %get-tuple-element.62.state, f32[96,1152]{1,0:T(8,128)S(1)} %get-tuple-element.72.tail, ...), custom_call_target="tpu_custom_call" | custom-call | flops 20000000 | bytes 2347532 | tf_op jit(solution)/shard_map/pallas_call | solution.py:453
  6.1 0.4 collective-permute-done.near
  6.5 8.8 %collective-permute-start.1 = (f32[48,256]{1,0:T(8,128)S(1)}, f32[48,256]{1,0:T(8,128)S(1)}, u32[]{:S(2)}, u32[]{:S(2)}) collective-permute-start(f32[48,256]{1,0:T(8,128)S(1)} %pad_maximum_fusion.1), channel_id=1, source_target_pairs={{2,4},{4,2},{3,5},{5,3},{6,8},{8,6},{7,9},{9,7},{10,12},{12,10},{1... | collective-permute-start | bytes 147464 | tf_op jit(solution)/shard_map/ppermute | solution.py:528
  15.2 1.9 %collective-permute-start.2 = (f32[48,256]{1,0:T(8,128)S(1)}, f32[48,256]{1,0:T(8,128)S(1)}, u32[]{:S(2)}, u32[]{:S(2)}) collective-permute-start(f32[48,256]{1,0:T(8,128)S(1)} %pad_maximum_fusion), channel_id=1, source_target_pairs={{0,2},{2,0},{1,3},{3,1},{4,6},{6,4},{5,7},{7,5},{8,10},{10,8},{9,1... | collective-permute-start | bytes 147464 | tf_op jit(solution)/shard_map/ppermute | solution.py:529
  17.2 2.0 %shard_map.138.state = f32[56,1152]{1,0:T(8,128)S(1)} custom-call(f32[56,1152]{1,0:T(8,128)S(1)} %get-tuple-element.62.state, f32[40,1152]{1,0:T(8,128)S(1)} %get-tuple-element.63.low, f32[96,1152]{1,0:T(8,128)S(1)} %get-tuple-element.64.faces, f32[9,9,3,128]{3,2,1,0:T(4,128)S(1)} %get-tuple-element.65.star, ...), custom_call_target="tpu_custom_call" | custom-call | flops 20000000 | bytes 1717760 | tf_op jit(solution)/shard_map/pallas_call | solution.py:453
  19.2 0.0 collective-permute-done.1.upper
  19.2 2.0 %collective-permute-done.2.lower = f32[48,256]{1,0:T(8,128)S(1)} collective-permute-done((f32[48,256]{1,0:T(8,128)S(1)}, f32[48,256]{1,0:T(8,128)S(1)}, u32[]{:S(2)}, u32[]{:S(2)}) %collective-permute-start.2) | collective-permute-done | bytes 49184 | tf_op jit(solution)/shard_map/ppermute | solution.py:529
  21.2 2.6 %shard_map.139 = (f32[56,1152]{1,0:T(8,128)S(1)}, f32[40,1152]{1,0:T(8,128)S(1)}, f32[96,1152]{1,0:T(8,128)S(1)}, f32[48,256]{1,0:T(8,128)S(1)}, f32[24,256]{1,0:T(8,128)S(1)}, /*index=5*/f32[24,256]{1,0:T(8,128)S(1)}) custom-call(s32[1]{0:T(128)} %bitcast.place, f32[56,1152]{1,0:T(8,128)S(1)} %shard_map.138.state, f32[48,256]{1,0:T(8,128)S(1)} %collective-permute-done.near, ...), custom_call_target="tpu_custom_call" | custom-call | flops 20000000 | bytes 3303428 | tf_op jit(solution)/shard_map/pallas_call | solution.py:453
  23.9 1.9 %collective-permute-start.3 = (f32[48,256]{1,0:T(8,128)S(1)}, f32[48,256]{1,0:T(8,128)S(1)}, u32[]{:S(2)}, u32[]{:S(2)}) collective-permute-start(f32[48,256]{1,0:T(8,128)S(1)} %get-tuple-element.95), channel_id=1, source_target_pairs={{0,1},{1,0},{2,3},{3,2},{4,5},{5,4},{6,7},{7,6},{8,9},{9,8},{10,11... | collective-permute-start | bytes 147464 | tf_op jit(solution)/shard_map/ppermute | solution.py:522
  25.8 1.2 %collective-permute-done.3.near = f32[48,256]{1,0:T(8,128)S(1)} collective-permute-done((f32[48,256]{1,0:T(8,128)S(1)}, f32[48,256]{1,0:T(8,128)S(1)}, u32[]{:S(2)}, u32[]{:S(2)}) %collective-permute-start.3) | collective-permute-done | bytes 49184 | tf_op jit(solution)/shard_map/ppermute | solution.py:522
  27.0 5.4 %collective-permute-start.4 = (f32[48,256]{1,0:T(8,128)S(1)}, f32[48,256]{1,0:T(8,128)S(1)}, u32[]{:S(2)}, u32[]{:S(2)}) collective-permute-start(f32[48,256]{1,0:T(8,128)S(1)} %pad_maximum_fusion.3), channel_id=1, source_target_pairs={{2,4},{4,2},{3,5},{5,3},{6,8},{8,6},{7,9},{9,7},{10,12},{12,10},{1... | collective-permute-start | bytes 147464 | tf_op jit(solution)/shard_map/ppermute | solution.py:528
  32.4 1.9 %collective-permute-start.5 = (f32[48,256]{1,0:T(8,128)S(1)}, f32[48,256]{1,0:T(8,128)S(1)}, u32[]{:S(2)}, u32[]{:S(2)}) collective-permute-start(f32[48,256]{1,0:T(8,128)S(1)} %pad_maximum_fusion.2), channel_id=1, source_target_pairs={{0,2},{2,0},{1,3},{3,1},{4,6},{6,4},{5,7},{7,5},{8,10},{10,8},{9,1... | collective-permute-start | bytes 147464 | tf_op jit(solution)/shard_map/ppermute | solution.py:529
  34.4 2.0 %shard_map.140.state = f32[56,1152]{1,0:T(8,128)S(1)} custom-call(f32[56,1152]{1,0:T(8,128)S(1)} %get-tuple-element.92.state, f32[40,1152]{1,0:T(8,128)S(1)} %get-tuple-element.93.low, f32[96,1152]{1,0:T(8,128)S(1)} %get-tuple-element.94.faces, f32[9,9,3,128]{3,2,1,0:T(4,128)S(1)} %get-tuple-element.65.star, ...), custom_call_target="tpu_custom_call" | custom-call | flops 20000000 | bytes 1717760 | tf_op jit(solution)/shard_map/pallas_call | solution.py:453
  36.4 2.0 %collective-permute-done.4.upper = f32[48,256]{1,0:T(8,128)S(1)} collective-permute-done((f32[48,256]{1,0:T(8,128)S(1)}, f32[48,256]{1,0:T(8,128)S(1)}, u32[]{:S(2)}, u32[]{:S(2)}) %collective-permute-start.4) | collective-permute-done | bytes 49184 | tf_op jit(solution)/shard_map/ppermute | solution.py:528
  38.4 0.0 collective-permute-done.5.lower
  38.4 2.6 %shard_map.141 = (f32[56,1152]{1,0:T(8,128)S(1)}, f32[40,1152]{1,0:T(8,128)S(1)}, f32[96,1152]{1,0:T(8,128)S(1)}, f32[48,256]{1,0:T(8,128)S(1)}, f32[24,256]{1,0:T(8,128)S(1)}, /*index=5*/f32[24,256]{1,0:T(8,128)S(1)}) custom-call(s32[1]{0:T(128)} %bitcast.place, f32[56,1152]{1,0:T(8,128)S(1)} %shard_map.140.state, ...), custom_call_target="tpu_custom_call" | custom-call | flops 20000000 | bytes 3303428 | tf_op jit(solution)/shard_map/pallas_call | solution.py:453
  41.1 1.9 %collective-permute-start.6 = (f32[48,256]{1,0:T(8,128)S(1)}, f32[48,256]{1,0:T(8,128)S(1)}, u32[]{:S(2)}, u32[]{:S(2)}) collective-permute-start(f32[48,256]{1,0:T(8,128)S(1)} %get-tuple-element.104), channel_id=1, source_target_pairs={{0,1},{1,0},{2,3},{3,2},{4,5},{5,4},{6,7},{7,6},{8,9},{9,8},{10,11... | collective-permute-start | bytes 147464 | tf_op jit(solution)/shard_map/ppermute | solution.py:522
  43.0 1.2 %collective-permute-done.6.near = f32[48,256]{1,0:T(8,128)S(1)} collective-permute-done((f32[48,256]{1,0:T(8,128)S(1)}, f32[48,256]{1,0:T(8,128)S(1)}, u32[]{:S(2)}, u32[]{:S(2)}) %collective-permute-start.6) | collective-permute-done | bytes 49184 | tf_op jit(solution)/shard_map/ppermute | solution.py:522
  44.2 5.8 %collective-permute-start.7 = (f32[48,256]{1,0:T(8,128)S(1)}, f32[48,256]{1,0:T(8,128)S(1)}, u32[]{:S(2)}, u32[]{:S(2)}) collective-permute-start(f32[48,256]{1,0:T(8,128)S(1)} %pad_maximum_fusion.5), channel_id=1, source_target_pairs={{2,4},{4,2},{3,5},{5,3},{6,8},{8,6},{7,9},{9,7},{10,12},{12,10},{1... | collective-permute-start | bytes 147464 | tf_op jit(solution)/shard_map/ppermute | solution.py:528
  50.1 2.1 %collective-permute-start.8 = (f32[48,256]{1,0:T(8,128)S(1)}, f32[48,256]{1,0:T(8,128)S(1)}, u32[]{:S(2)}, u32[]{:S(2)}) collective-permute-start(f32[48,256]{1,0:T(8,128)S(1)} %pad_maximum_fusion.4), channel_id=1, source_target_pairs={{0,2},{2,0},{1,3},{3,1},{4,6},{6,4},{5,7},{7,5},{8,10},{10,8},{9,1... | collective-permute-start | bytes 147464 | tf_op jit(solution)/shard_map/ppermute | solution.py:529
  52.2 2.0 %shard_map.142.state = f32[56,1152]{1,0:T(8,128)S(1)} custom-call(f32[56,1152]{1,0:T(8,128)S(1)} %get-tuple-element.101.state, f32[40,1152]{1,0:T(8,128)S(1)} %get-tuple-element.102.low, f32[96,1152]{1,0:T(8,128)S(1)} %get-tuple-element.103.faces, f32[9,9,3,128]{3,2,1,0:T(4,128)S(1)} %get-tuple-element.65.star, ...), custom_call_target="tpu_custom_call" | custom-call | flops 20000000 | bytes 1717760 | tf_op jit(solution)/shard_map/pallas_call | solution.py:453
  54.2 1.4 %collective-permute-done.7.upper = f32[48,256]{1,0:T(8,128)S(1)} collective-permute-done((f32[48,256]{1,0:T(8,128)S(1)}, f32[48,256]{1,0:T(8,128)S(1)}, u32[]{:S(2)}, u32[]{:S(2)}) %collective-permute-start.7) | collective-permute-done | bytes 49184 | tf_op jit(solution)/shard_map/ppermute | solution.py:528
  55.6 0.4 collective-permute-done.8.lower
  56.1 2.6 %shard_map.143 = (f32[56,1152]{1,0:T(8,128)S(1)}, f32[40,1152]{1,0:T(8,128)S(1)}, f32[96,1152]{1,0:T(8,128)S(1)}, f32[48,256]{1,0:T(8,128)S(1)}, f32[24,256]{1,0:T(8,128)S(1)}, /*index=5*/f32[24,256]{1,0:T(8,128)S(1)}) custom-call(s32[1]{0:T(128)} %bitcast.place, f32[56,1152]{1,0:T(8,128)S(1)} %shard_map.142.state, ...), custom_call_target="tpu_custom_call" | custom-call | flops 20000000 | bytes 3303428 | tf_op jit(solution)/shard_map/pallas_call | solution.py:453
  58.7 1.9 %collective-permute-start.9 = (f32[48,256]{1,0:T(8,128)S(1)}, f32[48,256]{1,0:T(8,128)S(1)}, u32[]{:S(2)}, u32[]{:S(2)}) collective-permute-start(f32[48,256]{1,0:T(8,128)S(1)} %get-tuple-element.113), channel_id=1, source_target_pairs={{0,1},{1,0},{2,3},{3,2},{4,5},{5,4},{6,7},{7,6},{8,9},{9,8},{10,11... | collective-permute-start | bytes 147464 | tf_op jit(solution)/shard_map/ppermute | solution.py:522
  60.6 1.2 %collective-permute-done.9.near = f32[48,256]{1,0:T(8,128)S(1)} collective-permute-done((f32[48,256]{1,0:T(8,128)S(1)}, f32[48,256]{1,0:T(8,128)S(1)}, u32[]{:S(2)}, u32[]{:S(2)}) %collective-permute-start.9) | collective-permute-done | bytes 49184 | tf_op jit(solution)/shard_map/ppermute | solution.py:522
  61.8 5.4 %collective-permute-start.10 = (f32[48,256]{1,0:T(8,128)S(1)}, f32[48,256]{1,0:T(8,128)S(1)}, u32[]{:S(2)}, u32[]{:S(2)}) collective-permute-start(f32[48,256]{1,0:T(8,128)S(1)} %pad_maximum_fusion.7), channel_id=1, source_target_pairs={{2,4},{4,2},{3,5},{5,3},{6,8},{8,6},{7,9},{9,7},{10,12},{12,10},{1... | collective-permute-start | bytes 147464 | tf_op jit(solution)/shard_map/ppermute | solution.py:528
  67.3 1.9 %collective-permute-start.11 = (f32[48,256]{1,0:T(8,128)S(1)}, f32[48,256]{1,0:T(8,128)S(1)}, u32[]{:S(2)}, u32[]{:S(2)}) collective-permute-start(f32[48,256]{1,0:T(8,128)S(1)} %pad_maximum_fusion.6), channel_id=1, source_target_pairs={{0,2},{2,0},{1,3},{3,1},{4,6},{6,4},{5,7},{7,5},{8,10},{10,8},{9,1... | collective-permute-start | bytes 147464 | tf_op jit(solution)/shard_map/ppermute | solution.py:529
  69.2 2.0 %shard_map.144.state = f32[56,1152]{1,0:T(8,128)S(1)} custom-call(f32[56,1152]{1,0:T(8,128)S(1)} %get-tuple-element.110.state, f32[40,1152]{1,0:T(8,128)S(1)} %get-tuple-element.111.low, f32[96,1152]{1,0:T(8,128)S(1)} %get-tuple-element.112.faces, f32[9,9,3,128]{3,2,1,0:T(4,128)S(1)} %get-tuple-element.65.star, ...), custom_call_target="tpu_custom_call" | custom-call | flops 20000000 | bytes 1717760 | tf_op jit(solution)/shard_map/pallas_call | solution.py:453
  71.2 2.0 %collective-permute-done.10.upper = f32[48,256]{1,0:T(8,128)S(1)} collective-permute-done((f32[48,256]{1,0:T(8,128)S(1)}, f32[48,256]{1,0:T(8,128)S(1)}, u32[]{:S(2)}, u32[]{:S(2)}) %collective-permute-start.10) | collective-permute-done | bytes 49184 | tf_op jit(solution)/shard_map/ppermute | solution.py:528
  73.2 0.0 collective-permute-done.11.lower
  73.3 1.5 %shard_map.145 = f32[9,56,128]{2,1,0:T(8,128)} custom-call(s32[1]{0:T(128)} %bitcast.place, f32[56,1152]{1,0:T(8,128)S(1)} %shard_map.144.state, f32[48,256]{1,0:T(8,128)S(1)} %collective-permute-done.9.near, f32[48,256]{1,0:T(8,128)S(1)} %collective-permute-done.10.upper, f32[48,256]{1,0:T(8,128)S(1)} %collective-permute-done.11.lower, ...), custom_call_target="tpu_custom_call" | custom-call | flops 20000000 | bytes 1204228 | tf_op jit(solution)/shard_map/pallas_call | solution.py:453
  (12 shorter events, 0.1 us)
Async XLA Ops:
  3.3 3.1 %collective-permute-start = (f32[48,256]{1,0:T(8,128)S(1)}, f32[48,256]{1,0:T(8,128)S(1)}, u32[]{:S(2)}, u32[]{:S(2)}) collective-permute-start(f32[48,256]{1,0:T(8,128)S(1)} %get-tuple-element.78), channel_id=1, source_target_pairs={{0,1},{1,0},{2,3},{3,2},{4,5},{5,4},{6,7},{7,6},{8,9},{9,8},{10,11... | collective-permute-start | bytes 147464 | tf_op jit(solution)/shard_map/ppermute | solution.py:522
  6.5 12.7 %collective-permute-start.1 = (f32[48,256]{1,0:T(8,128)S(1)}, f32[48,256]{1,0:T(8,128)S(1)}, u32[]{:S(2)}, u32[]{:S(2)}) collective-permute-start(f32[48,256]{1,0:T(8,128)S(1)} %pad_maximum_fusion.1), channel_id=1, source_target_pairs={{2,4},{4,2},{3,5},{5,3},{6,8},{8,6},{7,9},{9,7},{10,12},{12,10},{1... | collective-permute-start | bytes 147464 | tf_op jit(solution)/shard_map/ppermute | solution.py:528
  15.2 6.0 %collective-permute-start.2 = (f32[48,256]{1,0:T(8,128)S(1)}, f32[48,256]{1,0:T(8,128)S(1)}, u32[]{:S(2)}, u32[]{:S(2)}) collective-permute-start(f32[48,256]{1,0:T(8,128)S(1)} %pad_maximum_fusion), channel_id=1, source_target_pairs={{0,2},{2,0},{1,3},{3,1},{4,6},{6,4},{5,7},{7,5},{8,10},{10,8},{9,1... | collective-permute-start | bytes 147464 | tf_op jit(solution)/shard_map/ppermute | solution.py:529
  23.9 3.1 %collective-permute-start.3 = (f32[48,256]{1,0:T(8,128)S(1)}, f32[48,256]{1,0:T(8,128)S(1)}, u32[]{:S(2)}, u32[]{:S(2)}) collective-permute-start(f32[48,256]{1,0:T(8,128)S(1)} %get-tuple-element.95), channel_id=1, source_target_pairs={{0,1},{1,0},{2,3},{3,2},{4,5},{5,4},{6,7},{7,6},{8,9},{9,8},{10,11... | collective-permute-start | bytes 147464 | tf_op jit(solution)/shard_map/ppermute | solution.py:522
  27.0 11.4 %collective-permute-start.4 = (f32[48,256]{1,0:T(8,128)S(1)}, f32[48,256]{1,0:T(8,128)S(1)}, u32[]{:S(2)}, u32[]{:S(2)}) collective-permute-start(f32[48,256]{1,0:T(8,128)S(1)} %pad_maximum_fusion.3), channel_id=1, source_target_pairs={{2,4},{4,2},{3,5},{5,3},{6,8},{8,6},{7,9},{9,7},{10,12},{12,10},{1... | collective-permute-start | bytes 147464 | tf_op jit(solution)/shard_map/ppermute | solution.py:528
  32.4 6.0 %collective-permute-start.5 = (f32[48,256]{1,0:T(8,128)S(1)}, f32[48,256]{1,0:T(8,128)S(1)}, u32[]{:S(2)}, u32[]{:S(2)}) collective-permute-start(f32[48,256]{1,0:T(8,128)S(1)} %pad_maximum_fusion.2), channel_id=1, source_target_pairs={{0,2},{2,0},{1,3},{3,1},{4,6},{6,4},{5,7},{7,5},{8,10},{10,8},{9,1... | collective-permute-start | bytes 147464 | tf_op jit(solution)/shard_map/ppermute | solution.py:529
  41.1 3.1 %collective-permute-start.6 = (f32[48,256]{1,0:T(8,128)S(1)}, f32[48,256]{1,0:T(8,128)S(1)}, u32[]{:S(2)}, u32[]{:S(2)}) collective-permute-start(f32[48,256]{1,0:T(8,128)S(1)} %get-tuple-element.104), channel_id=1, source_target_pairs={{0,1},{1,0},{2,3},{3,2},{4,5},{5,4},{6,7},{7,6},{8,9},{9,8},{10,11... | collective-permute-start | bytes 147464 | tf_op jit(solution)/shard_map/ppermute | solution.py:522
  44.2 11.4 %collective-permute-start.7 = (f32[48,256]{1,0:T(8,128)S(1)}, f32[48,256]{1,0:T(8,128)S(1)}, u32[]{:S(2)}, u32[]{:S(2)}) collective-permute-start(f32[48,256]{1,0:T(8,128)S(1)} %pad_maximum_fusion.5), channel_id=1, source_target_pairs={{2,4},{4,2},{3,5},{5,3},{6,8},{8,6},{7,9},{9,7},{10,12},{12,10},{1... | collective-permute-start | bytes 147464 | tf_op jit(solution)/shard_map/ppermute | solution.py:528
  50.1 6.0 %collective-permute-start.8 = (f32[48,256]{1,0:T(8,128)S(1)}, f32[48,256]{1,0:T(8,128)S(1)}, u32[]{:S(2)}, u32[]{:S(2)}) collective-permute-start(f32[48,256]{1,0:T(8,128)S(1)} %pad_maximum_fusion.4), channel_id=1, source_target_pairs={{0,2},{2,0},{1,3},{3,1},{4,6},{6,4},{5,7},{7,5},{8,10},{10,8},{9,1... | collective-permute-start | bytes 147464 | tf_op jit(solution)/shard_map/ppermute | solution.py:529
  58.7 3.1 %collective-permute-start.9 = (f32[48,256]{1,0:T(8,128)S(1)}, f32[48,256]{1,0:T(8,128)S(1)}, u32[]{:S(2)}, u32[]{:S(2)}) collective-permute-start(f32[48,256]{1,0:T(8,128)S(1)} %get-tuple-element.113), channel_id=1, source_target_pairs={{0,1},{1,0},{2,3},{3,2},{4,5},{5,4},{6,7},{7,6},{8,9},{9,8},{10,11... | collective-permute-start | bytes 147464 | tf_op jit(solution)/shard_map/ppermute | solution.py:522
  61.8 11.4 %collective-permute-start.10 = (f32[48,256]{1,0:T(8,128)S(1)}, f32[48,256]{1,0:T(8,128)S(1)}, u32[]{:S(2)}, u32[]{:S(2)}) collective-permute-start(f32[48,256]{1,0:T(8,128)S(1)} %pad_maximum_fusion.7), channel_id=1, source_target_pairs={{2,4},{4,2},{3,5},{5,3},{6,8},{8,6},{7,9},{9,7},{10,12},{12,10},{1... | collective-permute-start | bytes 147464 | tf_op jit(solution)/shard_map/ppermute | solution.py:528
  67.3 6.0 %collective-permute-start.11 = (f32[48,256]{1,0:T(8,128)S(1)}, f32[48,256]{1,0:T(8,128)S(1)}, u32[]{:S(2)}, u32[]{:S(2)}) collective-permute-start(f32[48,256]{1,0:T(8,128)S(1)} %pad_maximum_fusion.6), channel_id=1, source_target_pairs={{0,2},{2,0},{1,3},{3,1},{4,6},{6,4},{5,7},{7,5},{8,10},{10,8},{9,1... | collective-permute-start | bytes 147464 | tf_op jit(solution)/shard_map/ppermute | solution.py:529

commit v4 on v3

--- a/solution.py
+++ b/solution.py
@@ -369,7 +369,7 @@
     up, down = upper[...], lower[...]
     behind = jnp.where(behind_up, up, down)
     ahead = jnp.where(behind_up, down, up)
-    here = near[0:BOTH, :]
+    here = jnp.where(odd, near[0:BOTH, :], near[2 * BOTH : 3 * BOTH, :])
     relayed = slice(BOTH, 2 * BOTH)
     rows = jnp.concatenate(
         [
@@ -476,8 +476,10 @@
     fine_send, coarse_send, stiff_time, stiff_vol, face_back, face_front, face_turn,
 ):
     count = lax.axis_size("dom")
-    partners = [(source, source ^ 1) for source in range(count)]
-    place = lax.axis_index("dom").astype(jnp.int32).reshape(1)
+    pairs = [[low, low + 1] for low in range(0, count, 2)]
+    place = lax.axis_index("dom").astype(jnp.int32)
+    partner_relay = jnp.where(place % 2 == 1, BOTH, 3 * BOTH)
+    place = place.reshape(1)
     labels = labels.reshape(1, LANES)
     later = (
         flux_self.transpose(1, 2, 0, 3),
@@ -519,11 +521,10 @@
         [(16 * NQ, FACES), (FPAD, FACES), (DEEP_PAD, LANES), (SLOT_REM, LANES)],
     )
     for step in range(SUBSTEPS):
-        near = lax.ppermute(pair, "dom", partners)
-        if step == 0:
-            up, down, lift = lax.optimization_barrier((up, down, lift))
-        lower = jnp.concatenate([down, near[BOTH:]], axis=0)
-        lower, up, relayed = lax.optimization_barrier((lower, up, near[BOTH:]))
+        near = lax.all_gather(pair, "dom", axis_index_groups=pairs, tiled=True)
+        relayed = lax.dynamic_slice(near, (partner_relay, 0), (BOTH, WIDTH))
+        lower = jnp.concatenate([down, relayed], axis=0)
+        lower, up, relayed = lax.optimization_barrier((lower, up, relayed))
         upper = jnp.concatenate([up, relayed], axis=0)
         upper = lax.ppermute(upper, "dom", swaps(count, 2))
         lower = lax.ppermute(lower, "dom", swaps(count, 0))

time: 75.2 us -> 69.9 us (0.930)
  starting transfers between devices: 41 us -> 33.3 us
  blocking collectives: 0 us -> 7.51 us
  waiting for transfers between devices: 11.9 us -> 7.09 us
    ppermute x4 -> x0, starting transfers between devices: 7.68 us -> none  [local(): near = lax.ppermute(pair, 'dom', partners)]
    all_gather x0 -> x4, blocking collectives: none -> 7.51 us  [local(): near = lax.all_gather(pair, 'dom', axis_index_groups=pairs, tiled=True)]
    ppermute x4 -> x0, waiting for transfers between devices: 3.95 us -> none  [local(): near = lax.ppermute(pair, 'dom', partners)]
    ppermute x4, waiting for transfers between devices: 2.46 us -> 1.63 us  [local(): lower = lax.ppermute(lower, 'dom', swaps(count, 0))]
  transfers between devices with their start and end apart: 12 -> 8, of which waited for: 9 -> 5; matrix products, arithmetic and copies ran while one was open for 0% -> 0% of each run, Pallas kernels for 12% -> 13%
where the time goes in v4:
time: 69.9 us; the launch traced here: 69.6 us
  starting transfers between devices  33.3 us (48%)
  Pallas kernels  21.4 us (31%)
  blocking collectives  7.51 us (11%)
  waiting for transfers between devices  7.09 us (10%)
    ppermute x4, starting transfers between devices, local(): upper = lax.ppermute(upper, 'dom', swaps(count, 2))  25.5 us
    pallas_call x10, Pallas kernels, call(): pl.pallas_call(kernel, in_specs=[smem] * scalars + [given] * (len(args) -...  21.4 us
    ppermute x4, starting transfers between devices, local(): lower = lax.ppermute(lower, 'dom', swaps(count, 0))  7.86 us
    all_gather x4, blocking collectives, local(): near = lax.all_gather(pair, 'dom', axis_index_groups=pairs, tiled=True)  7.51 us
    ppermute x4, waiting for transfers between devices, local(): upper = lax.ppermute(upper, 'dom', swaps(count, 2))  5.46 us
    ppermute x4, waiting for transfers between devices, local(): lower = lax.ppermute(lower, 'dom', swaps(count, 0))  1.63 us
  transfers between devices with their start and end apart: 8, of which 5 were waited for; matrix products, arithmetic and copies ran while one was open for 0% of the time, Pallas kernels for 13%

profile of v4, /device:TPU:384, one launch (start us, length us, event | category | flops | bytes accessed | tf_op | source)
XLA Modules:
  0.0 69.6 jit_solution(14419850817821517328)
XLA Ops:
  0.0 3.3 %shard_map.136 = (f32[56,1152]{1,0:T(8,128)S(1)}, f32[40,1152]{1,0:T(8,128)S(1)}, f32[96,1152]{1,0:T(8,128)S(1)}, f32[96,1152]{1,0:T(8,128)S(1)}, f32[48,256]{1,...) custom-call(s32[1]{0:T(128)} %bitcast.place, ...), custom_call_target="tpu_custom_call" | custom-call | flops 20000000 | bytes 3218172 | tf_op jit(solution)/shard_map/pallas_call | solution.py:453
  3.3 1.9 %all_gather.12.near = f32[96,256]{1,0:T(8,128)S(1)} all-gather(f32[48,256]{1,0:T(8,128)S(1)} %get-tuple-element.72), channel_id=1, replica_groups={{0,1},{2,3},{4,5},{6,7},{8,9},{10,11},{12,13},{14,15},{16,17},{18,19},{..., dimensions={0}, use_global_device_ids=true | all-gather | bytes 147456 | tf_op jit(solution)/shard_map/all_gather | solution.py:524
  5.2 8.8 %collective-permute-start = (f32[48,256]{1,0:T(8,128)S(1)}, f32[48,256]{1,0:T(8,128)S(1)}, u32[]{:S(2)}, u32[]{:S(2)}) collective-permute-start(f32[48,256]{1,0:T(8,128)S(1)} %pad_maximum_fusion.1), channel_id=1, source_target_pairs={{2,4},{4,2},{3,5},{5,3},{6,8},{8,6},{7,9},{9,7},{10,12},{12,10},{1... | collective-permute-start | bytes 147464 | tf_op jit(solution)/shard_map/ppermute | solution.py:529
  14.0 1.9 %collective-permute-start.1 = (f32[48,256]{1,0:T(8,128)S(1)}, f32[48,256]{1,0:T(8,128)S(1)}, u32[]{:S(2)}, u32[]{:S(2)}) collective-permute-start(f32[48,256]{1,0:T(8,128)S(1)} %pad_maximum_fusion), channel_id=1, source_target_pairs={{0,2},{2,0},{1,3},{3,1},{4,6},{6,4},{5,7},{7,5},{8,10},{10,8},{9,1... | collective-permute-start | bytes 147464 | tf_op jit(solution)/shard_map/ppermute | solution.py:530
  15.9 0.8 %shard_map.137 = (f32[3,56,1152]{2,1,0:T(8,128)S(1)}, f32[144,128]{1,0:T(8,128)S(1)}, f32[16,128]{1,0:T(8,128)S(1)}, f32[128,128]{1,0:T(8,128)S(1)}, f32[56,512]...) custom-call(f32[56,1152]{1,0:T(8,128)S(1)} %get-tuple-element.59.state, f32[96,1152]{1,0:T(8,128)S(1)} %get-tuple-element.67.tail, ...), custom_call_target="tpu_custom_call" | custom-call | flops 20000000 | bytes 2347532 | tf_op jit(solution)/shard_map/pallas_call | solution.py:453
  16.7 2.0 %shard_map.138.state = f32[56,1152]{1,0:T(8,128)S(1)} custom-call(f32[56,1152]{1,0:T(8,128)S(1)} %get-tuple-element.59.state, f32[40,1152]{1,0:T(8,128)S(1)} %get-tuple-element.60.low, f32[96,1152]{1,0:T(8,128)S(1)} %get-tuple-element.61.faces, f32[9,9,3,128]{3,2,1,0:T(4,128)S(1)} %get-tuple-element.62.star, ...), custom_call_target="tpu_custom_call" | custom-call | flops 20000000 | bytes 1717760 | tf_op jit(solution)/shard_map/pallas_call | solution.py:453
  18.7 0.0 collective-permute-done.upper
  18.8 1.2 %collective-permute-done.1.lower = f32[48,256]{1,0:T(8,128)S(1)} collective-permute-done((f32[48,256]{1,0:T(8,128)S(1)}, f32[48,256]{1,0:T(8,128)S(1)}, u32[]{:S(2)}, u32[]{:S(2)}) %collective-permute-start.1) | collective-permute-done | bytes 49184 | tf_op jit(solution)/shard_map/ppermute | solution.py:530
  20.0 2.6 %shard_map.139 = (f32[56,1152]{1,0:T(8,128)S(1)}, f32[40,1152]{1,0:T(8,128)S(1)}, f32[96,1152]{1,0:T(8,128)S(1)}, f32[48,256]{1,0:T(8,128)S(1)}, f32[24,256]{1,0:T(8,128)S(1)}, /*index=5*/f32[24,256]{1,0:T(8,128)S(1)}) custom-call(s32[1]{0:T(128)} %bitcast.place, f32[56,1152]{1,0:T(8,128)S(1)} %shard_map.138.state, f32[96,256]{1,0:T(8,128)S(1)} %all_gather.12.near, ...), custom_call_target="tpu_custom_call" | custom-call | flops 20000000 | bytes 3352580 | tf_op jit(solution)/shard_map/pallas_call | solution.py:453
  22.5 1.9 %all_gather.13.near = f32[96,256]{1,0:T(8,128)S(1)} all-gather(f32[48,256]{1,0:T(8,128)S(1)} %get-tuple-element.89), channel_id=1, replica_groups={{0,1},{2,3},{4,5},{6,7},{8,9},{10,11},{12,13},{14,15},{16,17},{18,19},{..., dimensions={0}, use_global_device_ids=true | all-gather | bytes 147456 | tf_op jit(solution)/shard_map/all_gather | solution.py:524
  24.4 5.4 %collective-permute-start.2 = (f32[48,256]{1,0:T(8,128)S(1)}, f32[48,256]{1,0:T(8,128)S(1)}, u32[]{:S(2)}, u32[]{:S(2)}) collective-permute-start(f32[48,256]{1,0:T(8,128)S(1)} %pad_maximum_fusion.3), channel_id=1, source_target_pairs={{2,4},{4,2},{3,5},{5,3},{6,8},{8,6},{7,9},{9,7},{10,12},{12,10},{1... | collective-permute-start | bytes 147464 | tf_op jit(solution)/shard_map/ppermute | solution.py:529
  29.9 1.9 %collective-permute-start.3 = (f32[48,256]{1,0:T(8,128)S(1)}, f32[48,256]{1,0:T(8,128)S(1)}, u32[]{:S(2)}, u32[]{:S(2)}) collective-permute-start(f32[48,256]{1,0:T(8,128)S(1)} %pad_maximum_fusion.2), channel_id=1, source_target_pairs={{0,2},{2,0},{1,3},{3,1},{4,6},{6,4},{5,7},{7,5},{8,10},{10,8},{9,1... | collective-permute-start | bytes 147464 | tf_op jit(solution)/shard_map/ppermute | solution.py:530
  31.8 2.0 %shard_map.140.state = f32[56,1152]{1,0:T(8,128)S(1)} custom-call(f32[56,1152]{1,0:T(8,128)S(1)} %get-tuple-element.86.state, f32[40,1152]{1,0:T(8,128)S(1)} %get-tuple-element.87.low, f32[96,1152]{1,0:T(8,128)S(1)} %get-tuple-element.88.faces, f32[9,9,3,128]{3,2,1,0:T(4,128)S(1)} %get-tuple-element.62.star, ...), custom_call_target="tpu_custom_call" | custom-call | flops 20000000 | bytes 1717760 | tf_op jit(solution)/shard_map/pallas_call | solution.py:453
  33.8 2.0 %collective-permute-done.2.upper = f32[48,256]{1,0:T(8,128)S(1)} collective-permute-done((f32[48,256]{1,0:T(8,128)S(1)}, f32[48,256]{1,0:T(8,128)S(1)}, u32[]{:S(2)}, u32[]{:S(2)}) %collective-permute-start.2) | collective-permute-done | bytes 49184 | tf_op jit(solution)/shard_map/ppermute | solution.py:529
  35.9 0.0 collective-permute-done.3.lower
  35.9 2.6 %shard_map.141 = (f32[56,1152]{1,0:T(8,128)S(1)}, f32[40,1152]{1,0:T(8,128)S(1)}, f32[96,1152]{1,0:T(8,128)S(1)}, f32[48,256]{1,0:T(8,128)S(1)}, f32[24,256]{1,0:T(8,128)S(1)}, /*index=5*/f32[24,256]{1,0:T(8,128)S(1)}) custom-call(s32[1]{0:T(128)} %bitcast.place, f32[56,1152]{1,0:T(8,128)S(1)} %shard_map.140.state, f32[96,256]{1,0:T(8,128)S(1)} %all_gather.13.near, ...), custom_call_target="tpu_custom_call" | custom-call | flops 20000000 | bytes 3352580 | tf_op jit(solution)/shard_map/pallas_call | solution.py:453
  38.5 1.9 %all_gather.14.near = f32[96,256]{1,0:T(8,128)S(1)} all-gather(f32[48,256]{1,0:T(8,128)S(1)} %get-tuple-element.98), channel_id=1, replica_groups={{0,1},{2,3},{4,5},{6,7},{8,9},{10,11},{12,13},{14,15},{16,17},{18,19},{..., dimensions={0}, use_global_device_ids=true | all-gather | bytes 147456 | tf_op jit(solution)/shard_map/all_gather | solution.py:524
  40.4 5.8 %collective-permute-start.4 = (f32[48,256]{1,0:T(8,128)S(1)}, f32[48,256]{1,0:T(8,128)S(1)}, u32[]{:S(2)}, u32[]{:S(2)}) collective-permute-start(f32[48,256]{1,0:T(8,128)S(1)} %pad_maximum_fusion.5), channel_id=1, source_target_pairs={{2,4},{4,2},{3,5},{5,3},{6,8},{8,6},{7,9},{9,7},{10,12},{12,10},{1... | collective-permute-start | bytes 147464 | tf_op jit(solution)/shard_map/ppermute | solution.py:529
  46.2 2.1 %collective-permute-start.5 = (f32[48,256]{1,0:T(8,128)S(1)}, f32[48,256]{1,0:T(8,128)S(1)}, u32[]{:S(2)}, u32[]{:S(2)}) collective-permute-start(f32[48,256]{1,0:T(8,128)S(1)} %pad_maximum_fusion.4), channel_id=1, source_target_pairs={{0,2},{2,0},{1,3},{3,1},{4,6},{6,4},{5,7},{7,5},{8,10},{10,8},{9,1... | collective-permute-start | bytes 147464 | tf_op jit(solution)/shard_map/ppermute | solution.py:530
  48.3 2.0 %shard_map.142.state = f32[56,1152]{1,0:T(8,128)S(1)} custom-call(f32[56,1152]{1,0:T(8,128)S(1)} %get-tuple-element.95.state, f32[40,1152]{1,0:T(8,128)S(1)} %get-tuple-element.96.low, f32[96,1152]{1,0:T(8,128)S(1)} %get-tuple-element.97.faces, f32[9,9,3,128]{3,2,1,0:T(4,128)S(1)} %get-tuple-element.62.star, ...), custom_call_target="tpu_custom_call" | custom-call | flops 20000000 | bytes 1717760 | tf_op jit(solution)/shard_map/pallas_call | solution.py:453
  50.4 1.4 %collective-permute-done.4.upper = f32[48,256]{1,0:T(8,128)S(1)} collective-permute-done((f32[48,256]{1,0:T(8,128)S(1)}, f32[48,256]{1,0:T(8,128)S(1)}, u32[]{:S(2)}, u32[]{:S(2)}) %collective-permute-start.4) | collective-permute-done | bytes 49184 | tf_op jit(solution)/shard_map/ppermute | solution.py:529
  51.8 0.4 collective-permute-done.5.lower
  52.2 2.6 %shard_map.143 = (f32[56,1152]{1,0:T(8,128)S(1)}, f32[40,1152]{1,0:T(8,128)S(1)}, f32[96,1152]{1,0:T(8,128)S(1)}, f32[48,256]{1,0:T(8,128)S(1)}, f32[24,256]{1,0:T(8,128)S(1)}, /*index=5*/f32[24,256]{1,0:T(8,128)S(1)}) custom-call(s32[1]{0:T(128)} %bitcast.place, f32[56,1152]{1,0:T(8,128)S(1)} %shard_map.142.state, f32[96,256]{1,0:T(8,128)S(1)} %all_gather.14.near, ...), custom_call_target="tpu_custom_call" | custom-call | flops 20000000 | bytes 3352580 | tf_op jit(solution)/shard_map/pallas_call | solution.py:453
  54.8 1.9 %all_gather.15.near = f32[96,256]{1,0:T(8,128)S(1)} all-gather(f32[48,256]{1,0:T(8,128)S(1)} %get-tuple-element.107), channel_id=1, replica_groups={{0,1},{2,3},{4,5},{6,7},{8,9},{10,11},{12,13},{14,15},{16,17},{18,19},{..., dimensions={0}, use_global_device_ids=true | all-gather | bytes 147456 | tf_op jit(solution)/shard_map/all_gather | solution.py:524
  56.7 5.4 %collective-permute-start.6 = (f32[48,256]{1,0:T(8,128)S(1)}, f32[48,256]{1,0:T(8,128)S(1)}, u32[]{:S(2)}, u32[]{:S(2)}) collective-permute-start(f32[48,256]{1,0:T(8,128)S(1)} %pad_maximum_fusion.7), channel_id=1, source_target_pairs={{2,4},{4,2},{3,5},{5,3},{6,8},{8,6},{7,9},{9,7},{10,12},{12,10},{1... | collective-permute-start | bytes 147464 | tf_op jit(solution)/shard_map/ppermute | solution.py:529
  62.1 1.9 %collective-permute-start.7 = (f32[48,256]{1,0:T(8,128)S(1)}, f32[48,256]{1,0:T(8,128)S(1)}, u32[]{:S(2)}, u32[]{:S(2)}) collective-permute-start(f32[48,256]{1,0:T(8,128)S(1)} %pad_maximum_fusion.6), channel_id=1, source_target_pairs={{0,2},{2,0},{1,3},{3,1},{4,6},{6,4},{5,7},{7,5},{8,10},{10,8},{9,1... | collective-permute-start | bytes 147464 | tf_op jit(solution)/shard_map/ppermute | solution.py:530
  64.1 2.0 %shard_map.144.state = f32[56,1152]{1,0:T(8,128)S(1)} custom-call(f32[56,1152]{1,0:T(8,128)S(1)} %get-tuple-element.104.state, f32[40,1152]{1,0:T(8,128)S(1)} %get-tuple-element.105.low, f32[96,1152]{1,0:T(8,128)S(1)} %get-tuple-element.106.faces, f32[9,9,3,128]{3,2,1,0:T(4,128)S(1)} %get-tuple-element.62.star, ...), custom_call_target="tpu_custom_call" | custom-call | flops 20000000 | bytes 1717760 | tf_op jit(solution)/shard_map/pallas_call | solution.py:453
  66.1 2.0 %collective-permute-done.6.upper = f32[48,256]{1,0:T(8,128)S(1)} collective-permute-done((f32[48,256]{1,0:T(8,128)S(1)}, f32[48,256]{1,0:T(8,128)S(1)}, u32[]{:S(2)}, u32[]{:S(2)}) %collective-permute-start.6) | collective-permute-done | bytes 49184 | tf_op jit(solution)/shard_map/ppermute | solution.py:529
  68.1 0.0 collective-permute-done.7.lower
  68.1 1.5 %shard_map.145 = f32[9,56,128]{2,1,0:T(8,128)} custom-call(s32[1]{0:T(128)} %bitcast.place, f32[56,1152]{1,0:T(8,128)S(1)} %shard_map.144.state, f32[96,256]{1,0:T(8,128)S(1)} %all_gather.15.near, f32[48,256]{1,0:T(8,128)S(1)} %collective-permute-done.6.upper, f32[48,256]{1,0:T(8,128)S(1)} %collective-permute-done.7.lower, ...), custom_call_target="tpu_custom_call" | custom-call | flops 20000000 | bytes 1253380 | tf_op jit(solution)/shard_map/pallas_call | solution.py:453
  (12 shorter events, 0.1 us)
Async XLA Ops:
  5.2 13.6 %collective-permute-start = (f32[48,256]{1,0:T(8,128)S(1)}, f32[48,256]{1,0:T(8,128)S(1)}, u32[]{:S(2)}, u32[]{:S(2)}) collective-permute-start(f32[48,256]{1,0:T(8,128)S(1)} %pad_maximum_fusion.1), channel_id=1, source_target_pairs={{2,4},{4,2},{3,5},{5,3},{6,8},{8,6},{7,9},{9,7},{10,12},{12,10},{1... | collective-permute-start | bytes 147464 | tf_op jit(solution)/shard_map/ppermute | solution.py:529
  14.0 6.0 %collective-permute-start.1 = (f32[48,256]{1,0:T(8,128)S(1)}, f32[48,256]{1,0:T(8,128)S(1)}, u32[]{:S(2)}, u32[]{:S(2)}) collective-permute-start(f32[48,256]{1,0:T(8,128)S(1)} %pad_maximum_fusion), channel_id=1, source_target_pairs={{0,2},{2,0},{1,3},{3,1},{4,6},{6,4},{5,7},{7,5},{8,10},{10,8},{9,1... | collective-permute-start | bytes 147464 | tf_op jit(solution)/shard_map/ppermute | solution.py:530
  24.4 11.4 %collective-permute-start.2 = (f32[48,256]{1,0:T(8,128)S(1)}, f32[48,256]{1,0:T(8,128)S(1)}, u32[]{:S(2)}, u32[]{:S(2)}) collective-permute-start(f32[48,256]{1,0:T(8,128)S(1)} %pad_maximum_fusion.3), channel_id=1, source_target_pairs={{2,4},{4,2},{3,5},{5,3},{6,8},{8,6},{7,9},{9,7},{10,12},{12,10},{1... | collective-permute-start | bytes 147464 | tf_op jit(solution)/shard_map/ppermute | solution.py:529
  29.9 6.0 %collective-permute-start.3 = (f32[48,256]{1,0:T(8,128)S(1)}, f32[48,256]{1,0:T(8,128)S(1)}, u32[]{:S(2)}, u32[]{:S(2)}) collective-permute-start(f32[48,256]{1,0:T(8,128)S(1)} %pad_maximum_fusion.2), channel_id=1, source_target_pairs={{0,2},{2,0},{1,3},{3,1},{4,6},{6,4},{5,7},{7,5},{8,10},{10,8},{9,1... | collective-permute-start | bytes 147464 | tf_op jit(solution)/shard_map/ppermute | solution.py:530
  40.4 11.4 %collective-permute-start.4 = (f32[48,256]{1,0:T(8,128)S(1)}, f32[48,256]{1,0:T(8,128)S(1)}, u32[]{:S(2)}, u32[]{:S(2)}) collective-permute-start(f32[48,256]{1,0:T(8,128)S(1)} %pad_maximum_fusion.5), channel_id=1, source_target_pairs={{2,4},{4,2},{3,5},{5,3},{6,8},{8,6},{7,9},{9,7},{10,12},{12,10},{1... | collective-permute-start | bytes 147464 | tf_op jit(solution)/shard_map/ppermute | solution.py:529
  46.2 6.0 %collective-permute-start.5 = (f32[48,256]{1,0:T(8,128)S(1)}, f32[48,256]{1,0:T(8,128)S(1)}, u32[]{:S(2)}, u32[]{:S(2)}) collective-permute-start(f32[48,256]{1,0:T(8,128)S(1)} %pad_maximum_fusion.4), channel_id=1, source_target_pairs={{0,2},{2,0},{1,3},{3,1},{4,6},{6,4},{5,7},{7,5},{8,10},{10,8},{9,1... | collective-permute-start | bytes 147464 | tf_op jit(solution)/shard_map/ppermute | solution.py:530
  56.7 11.4 %collective-permute-start.6 = (f32[48,256]{1,0:T(8,128)S(1)}, f32[48,256]{1,0:T(8,128)S(1)}, u32[]{:S(2)}, u32[]{:S(2)}) collective-permute-start(f32[48,256]{1,0:T(8,128)S(1)} %pad_maximum_fusion.7), channel_id=1, source_target_pairs={{2,4},{4,2},{3,5},{5,3},{6,8},{8,6},{7,9},{9,7},{10,12},{12,10},{1... | collective-permute-start | bytes 147464 | tf_op jit(solution)/shard_map/ppermute | solution.py:529
  62.1 6.0 %collective-permute-start.7 = (f32[48,256]{1,0:T(8,128)S(1)}, f32[48,256]{1,0:T(8,128)S(1)}, u32[]{:S(2)}, u32[]{:S(2)}) collective-permute-start(f32[48,256]{1,0:T(8,128)S(1)} %pad_maximum_fusion.6), channel_id=1, source_target_pairs={{0,2},{2,0},{1,3},{3,1},{4,6},{6,4},{5,7},{7,5},{8,10},{10,8},{9,1... | collective-permute-start | bytes 147464 | tf_op jit(solution)/shard_map/ppermute | solution.py:530

commit v5 on v4

--- a/solution.py
+++ b/solution.py
@@ -34,6 +34,9 @@
 CHAIN_ROWS = BACK + OWN
 TAIL = 96
 PART = 64
+TWOS = 5
+NARROW = TWOS * LANES
+STAR_ROWS = 40
 HIGH = lax.Precision.HIGH
 HIGHEST = lax.Precision.HIGHEST
 F32 = jnp.float32
@@ -86,6 +89,34 @@
     )
 
 
+def gather_exact(value, hot):
+    top, rest = halves(value)
+    middle, low = halves(value - top.astype(F32))
+    return lax.dot_general(
+        jnp.concatenate([top, middle, low], axis=1),
+        jnp.concatenate([hot, hot, hot], axis=1),
+        (((1,), (1,)), ((), ())),
+        preferred_element_type=F32,
+    )
+
+
+def first_half(rows):
+    return iota((rows, LANES), 1) < PART
+
+
+def paired(blocks):
+    rows = blocks[0].shape[0]
+    blocks = list(blocks) + [jnp.zeros_like(blocks[0])]
+    return jnp.concatenate(
+        [jnp.where(first_half(rows), blocks[2 * t], blocks[2 * t + 1]) for t in range(TWOS)],
+        axis=1,
+    )
+
+
+def place_of(q):
+    return LANES * (q % 2) + FPAD * (q // 2)
+
+
 def stacked(value):
     top = value.astype(BF16).astype(F32)
     rest = value - top
@@ -94,9 +125,9 @@
     return jnp.concatenate([top] + gap + [rest] + gap + [top] + gap, axis=0).astype(BF16)
 
 
-def products(blocks, row_of, rows):
+def products(blocks, row_of, count=NQ):
     totals = [None] * NQ
-    for q in range(NQ):
+    for q in range(count):
         for position, block in enumerate(blocks):
             left = block(q)
             for p in range(NQ):
@@ -105,7 +136,7 @@
     return totals
 
 
-def chain_weights(stiff_time, face_back, out, raw):
+def chain_weights(stiff_time, face_back, out, tips, raw):
     raw[...] = jnp.zeros(raw.shape, F32)
     for start, valid, padded, _ in LEVELS:
         for d in range(3):
@@ -116,6 +147,12 @@
     top = once.astype(BF16).astype(F32)
     out[:, 0:LANES] = (top + pltpu.roll(top, PART, 1)).astype(BF16)
     out[:, LANES : 2 * LANES] = (once - top).astype(BF16)
+    start = LEVELS[-1][0]
+    turned = jnp.transpose(once[start : start + LANES])
+    for d in range(3):
+        column = turned[0:8, 8 * d : 8 * d + 1]
+        tips[8 * d : 8 * d + 8, :] = jnp.broadcast_to(column, (8, LANES))
+    tips[24 : 24 + OWN, :] = jnp.broadcast_to(once[BACK : BACK + OWN, 0:1], (OWN, LANES))
 
 
 def weigh(weights, start, rows, value):
@@ -124,18 +161,54 @@
     )
 
 
-def chain_of(first, star, weights):
+def wide_sums(block, star):
+    blocks = [functools.partial(block, d) for d in range(3)]
+    return products(blocks, lambda d, q, p: star[q, p, d : d + 1, :])
+
+
+def narrow_sums(block, star):
+    return products(
+        [functools.partial(block, d) for d in range(3)],
+        lambda d, t, p: star[STAR_ROWS * t + 4 * p + d : STAR_ROWS * t + 4 * p + d + 1, :],
+        TWOS,
+    )
+
+
+def narrow_join(totals):
+    half = first_half(totals[0].shape[0])
+    totals = list(totals) + [jnp.zeros_like(totals[0])]
+    pieces = []
+    for t in range(TWOS):
+        even, odd = totals[2 * t], totals[2 * t + 1]
+        crossed = pltpu.roll(jnp.where(half, odd, even), PART, 1)
+        pieces.append(jnp.where(half, even, odd) + crossed)
+    return jnp.concatenate(pieces, axis=1)
+
+
+def wide_join(totals):
+    return jnp.concatenate(totals, axis=1)
+
+
+def chain_of(first, star, weights, tips, sums, join):
     now = first
     chain = [first]
-    for start, _, padded, rows in LEVELS:
+    for start, _, padded, rows in LEVELS[:-1]:
         found = weigh(weights, start, rows, now)
-        blocks = [
-            lambda q, d=d: found[d * padded : (d + 1) * padded, lanes(q)] for d in range(3)
-        ]
-        totals = products(blocks, lambda d, q, p: star[q, p, d : d + 1, :], padded)
-        now = jnp.concatenate(totals, axis=1)
+        now = join(
+            sums(lambda d, c: found[d * padded : (d + 1) * padded, lanes(c)], star)
+        )
         chain.append(now)
-    return chain
+    totals = sums(lambda d, c: now[:, lanes(c)] * tips[8 * d : 8 * d + 8, :], star)
+    return chain, join([jnp.sum(total, axis=0, keepdims=True) for total in totals])
+
+
+def with_end(integral, faces, end, tips):
+    row = jnp.where(iota((8, end.shape[1]), 0) == 0, end, 0.0)
+    low = jnp.concatenate([integral[0:8] + row, integral[8:VPAD]], axis=0)
+    column = tips[24 : 24 + OWN, :]
+    count = end.shape[1] // LANES
+    faces = [faces[:, lanes(c)] + column * end[:, lanes(c)] for c in range(count)]
+    return low, jnp.concatenate(faces, axis=1)
 
 
 def integral_of(chain, weights):
@@ -143,7 +216,7 @@
     edges = [0, 8, 16, 24, 40, 56]
     for low, high in zip(edges[:-1], edges[1:]):
         total = None
-        for depth in range(ORDER):
+        for depth in range(len(chain)):
             if chain[depth].shape[0] < high:
                 continue
             term = (weights[depth] * (-1) ** depth) * chain[depth][low:high]
@@ -153,28 +226,42 @@
 
 
 def face_table(faces):
-    rows = []
-    for q in range(NQ):
-        rows.append(
-            jnp.concatenate(
-                [faces[j * FPAD : (j + 1) * FPAD, lanes(q)] for j in range(4)], axis=1
-            )
-        )
-    rows.append(jnp.zeros((WIDTH - NQ * FPAD, FACES), F32))
-    return jnp.concatenate(rows, axis=0)
-
-
-def project_and_send(integral, weights, lists, position, faces_out, pair_out, up_out, down_out):
-    faces = weigh(weights, BACK, OWN, integral)
-    faces_out[...] = faces
-    hot = jnp.concatenate(
-        [
-            jnp.where(lists[...] == iota((PEERS * BOTH, LANES), 1) + LANES * j, 1.0, 0.0)
-            for j in range(4)
-        ],
-        axis=1,
-    ).astype(BF16)
-    sent = pick_rows(hot, face_table(faces))
+    def block(q):
+        return jnp.concatenate(
+            [faces[j * FPAD : (j + 1) * FPAD, lanes(q)] for j in range(4)], axis=1
+        )
+
+    even = [block(q) for q in range(0, NQ, 2)]
+    odd = [block(q) for q in range(1, NQ, 2)]
+    return jnp.concatenate(
+        even
+        + [jnp.zeros((LANES - len(even) * FPAD, FACES), F32)]
+        + odd
+        + [jnp.zeros((LANES - len(odd) * FPAD, FACES), F32)],
+        axis=0,
+    )
+
+
+def narrow_table(faces):
+    rows = [
+        jnp.concatenate([faces[j * FPAD : (j + 1) * FPAD, lanes(t)] for j in range(4)], axis=1)
+        for t in range(TWOS)
+    ]
+    return jnp.concatenate(rows + [jnp.zeros((LANES - TWOS * FPAD, FACES), F32)], axis=0)
+
+
+def list_rows():
+    row = iota((PEERS * BOTH, LANES), 0)
+    peer = (row >= BOTH).astype(jnp.int32) + (row >= 2 * BOTH).astype(jnp.int32)
+    peer = peer + (row >= 3 * BOTH).astype(jnp.int32)
+    return peer, row - BOTH * peer
+
+
+def list_hot(lists, face):
+    return lists[...] == iota((PEERS * BOTH, LANES), 1) + LANES * face
+
+
+def deliver(sent, position, pair_out, up_out, down_out):
     odd = lax.rem(position, 2) == 1
     first, second = sent[0:BOTH], sent[BOTH : 2 * BOTH]
     pair_out[0:BOTH, :] = jnp.where(odd, second, first)
@@ -186,10 +273,7 @@
 
 
 def list_column(fine, coarse):
-    row = iota((PEERS * BOTH, LANES), 0)
-    peer = (row >= BOTH).astype(jnp.int32) + (row >= 2 * BOTH).astype(jnp.int32)
-    peer = peer + (row >= 3 * BOTH).astype(jnp.int32)
-    inner = row - BOTH * peer
+    peer, inner = list_rows()
     total = jnp.zeros((PEERS * BOTH, LANES), F32)
     for kind, entries in enumerate((fine, coarse)):
         here = iota((PEERS * BOTH, LANES), 1) == inner - kind * SLOTS
@@ -205,10 +289,10 @@
     later = rest[:7]
     (
         state_out, low_out, tail_out, faces_out, pair_out, up_out, down_out,
-        weights_out, star_out, labels_out, lists_out,
-    ) = rest[7:18]
-    later_out = rest[18:25]
-    raw, dofs_here, time_here, back_here, wide, fine_here, coarse_here, ready = rest[25:]
+        weights_out, tips_out, star_out, labels_out, lists_out,
+    ) = rest[7:19]
+    later_out = rest[19:26]
+    raw, dofs_here, time_here, back_here, wide, fine_here, coarse_here, ready = rest[26:]
     position = place[0]
     moves = [
         (dofs, dofs_here),
@@ -229,33 +313,68 @@
         copy.start()
     for copy in copies[1:3]:
         copy.wait()
-    chain_weights(time_here, back_here, weights_out, raw)
+    chain_weights(time_here, back_here, weights_out, tips_out, raw)
     copies[0].wait()
     state = jnp.concatenate([dofs_here[q] for q in range(NQ)], axis=1)
     state_out[...] = state
     copies[3].wait()
-    chain = chain_of(state, star_out, weights_out)
-    integral = integral_of(chain, taylor_weights(0.0, 1.0 / SUBSTEPS))
-    low_out[...] = integral[0:VPAD]
+    chain, end = chain_of(state, star_out, weights_out, tips_out, wide_sums, wide_join)
+    first_weights = taylor_weights(0.0, 1.0 / SUBSTEPS)
+    integral = integral_of(chain, first_weights)
     for copy in copies[4:first]:
         copy.wait()
     wide[...] = jnp.zeros(wide.shape, F32)
     wide[0:PEERS, 0:SLOTS] = fine_here[...].astype(F32)
     wide[8 : 8 + PEERS, 0:SLOTS] = coarse_here[...].astype(F32)
     lists_out[...] = list_column(wide[0:PEERS], wide[8 : 8 + PEERS])
-    project_and_send(
-        integral, weights_out, lists_out, position, faces_out, pair_out, up_out, down_out
-    )
-    tail_out[...] = jnp.concatenate(chain[1:], axis=0)
+    faces = weigh(weights_out, BACK, OWN, integral)
+    low, faces = with_end(integral, faces, -first_weights[-1] * end, tips_out)
+    low_out[...] = low
+    faces_out[...] = faces
+    hot = jnp.concatenate(
+        [jnp.where(list_hot(lists_out, j), 1.0, 0.0) for j in range(4)], axis=1
+    ).astype(BF16)
+    deliver(pick_rows(hot, face_table(faces)), position, pair_out, up_out, down_out)
+    end = jnp.where(iota((8, COLS), 0) == 0, end, 0.0)
+    tail_out[...] = jnp.concatenate(chain[1:] + [end], axis=0)
     for copy in copies[first:]:
         copy.wait()
 
 
 def prepare_kernel(
     state, tail, source, orientation, flux_other, face_front, face_turn, stiff_vol,
+    star, labels, lists,
     coarse_out, slot_flux_out, slot_code_out, slot_hot_out, lift_out, slot_lift_out,
-    table, fronts, tall, slot_tall,
+    narrow_hot_out, slot_narrow_out, star_out, send_out,
+    table, fronts, tall, slot_tall, flat,
 ):
+    fine = labels[...] == 1
+    before = (iota((LANES, LANES), 0) < iota((LANES, LANES), 1)).astype(F32).astype(BF16)
+    marks = jnp.broadcast_to(jnp.where(fine, 1.0, 0.0), (16, LANES)).astype(BF16)
+    rank = jnp.dot(marks, before, preferred_element_type=F32)[0:1].astype(jnp.int32)
+    rank = jnp.where(fine, rank, -1)
+    lane = iota((LANES, LANES), 0)
+    lane = jnp.where(lane >= PART, lane - PART, lane)
+    narrow_hot = jnp.where(rank == lane, 1.0, 0.0).astype(BF16)
+    narrow_hot_out[...] = narrow_hot
+    flat[...] = jnp.zeros(flat.shape, F32)
+    for q in range(NQ):
+        for p in range(NQ):
+            start = STAR_ROWS * q + 4 * p
+            flat[start : start + 3, :] = star[q, p]
+    gathered = gather_exact(flat[...], narrow_hot)
+    stars = [gathered[STAR_ROWS * q : STAR_ROWS * (q + 1)] for q in range(NQ)]
+    packed = paired(stars)
+    for t in range(TWOS):
+        star_out[STAR_ROWS * t : STAR_ROWS * (t + 1), :] = packed[:, lanes(t)]
+    _, inner = list_rows()
+    half = first_half(PEERS * BOTH)
+    across = (((1,), (1,)), ((), ()))
+    for j in range(4):
+        chosen = jnp.where(list_hot(lists, j) & (inner < SLOTS), 1.0, 0.0).astype(BF16)
+        found = lax.dot_general(chosen, narrow_hot, across, preferred_element_type=F32)
+        send_out[0 : PEERS * BOTH, lanes(j)] = jnp.where(half, found, 0.0).astype(BF16)
+        send_out[PEERS * BOTH :, lanes(j)] = jnp.where(half, 0.0, found).astype(BF16)
     chain = [state[...]]
     start = 0
     for _, _, padded, _ in LEVELS:
@@ -273,7 +392,11 @@
     wanted = kind * (PEERS * SLOTS - SLOTS) + peer * SLOTS + inner + FACES
     wanted = jnp.where(row < PEERS * BOTH, wanted, -1)
     blocks = [jnp.where(source[i : i + 1, :] == wanted, 1.0, 0.0) for i in range(4)]
-    slot_hot_out[...] = blocks[0] + blocks[1] + blocks[2] + blocks[3]
+    slot_hot = (blocks[0] + blocks[1] + blocks[2] + blocks[3]).astype(BF16)
+    slot_hot_out[...] = slot_hot
+    slot_narrow_out[...] = lax.dot_general(
+        slot_hot, narrow_hot, across, preferred_element_type=F32
+    ).astype(BF16)
     hot = jnp.concatenate(blocks, axis=1).astype(BF16)
     codes = jnp.concatenate(
         [
@@ -283,7 +406,11 @@
         axis=1,
     ).astype(BF16)
     dims = (((1,), (1,)), ((), ()))
-    slot_code_out[...] = lax.dot_general(codes, hot, dims, preferred_element_type=F32)
+    found = lax.dot_general(codes, hot, dims, preferred_element_type=F32)
+    for code in range(12):
+        slot_code_out[SLOT_PAD * code : SLOT_PAD * (code + 1), :] = jnp.broadcast_to(
+            found[code : code + 1], (SLOT_PAD, LANES)
+        ).astype(BF16)
     table[...] = jnp.zeros(table.shape, F32)
     for i in range(4):
         for q in range(NQ):
@@ -320,9 +447,49 @@
     slot_lift_out[PART:, SLOT_REM:] = jnp.zeros((PART, SLOT_REM), BF16)
 
 
-def local_kernel(
-    state, low, faces, star, flux_self, flux_other, source, orientation, lift, out, stack,
-):
+def local_kernel(*refs, step):
+    if step == 0:
+        state, low, faces, *rest = refs
+        state, low, faces = state[...], low[...], faces[...]
+    else:
+        state, by_slot, slot_hot, low, faces, coarse_faces, *rest = refs
+    star, flux_self, flux_other, source, orientation, lift, *rest = rest
+    coarse, weights, lists, narrow_hot, labels, *rest = rest
+    out, *rest = rest
+    if step > 0:
+        state = state[...] + by_elements(by_slot[...], slot_hot[...])
+        back = jnp.transpose(narrow_hot[...].astype(F32))
+        half = iota((LANES, LANES), 1) < PART
+        spread = jnp.concatenate(
+            [
+                jnp.transpose(jnp.where(half, back, 0.0)),
+                jnp.transpose(jnp.where(half, 0.0, back)),
+            ],
+            axis=1,
+        ).astype(BF16)
+        both = VPAD + OWN
+        rows = [
+            part[:, lanes(t)] for t in range(TWOS) for part in (low, faces)
+        ]
+        wide = pick(jnp.concatenate(rows, axis=0), spread)
+        wide = [wide[both * t : both * (t + 1)] for t in range(TWOS)]
+        wide = jnp.concatenate(wide, axis=1)[:, 0:COLS]
+        fine = labels[...] == 1
+        fine = jnp.concatenate([fine] * NQ, axis=1)
+        low = jnp.where(fine, wide[0:VPAD], coarse[step - 1, 0:VPAD, :])
+        faces = jnp.where(fine, wide[VPAD:both], coarse_faces[...])
+    if step + 1 < SUBSTEPS:
+        narrow_out, next_faces_out, next_sent_out, stack = rest
+        next_faces = weigh(weights, BACK, OWN, coarse[step])
+        next_faces_out[...] = next_faces
+        _, inner = list_rows()
+        hot = jnp.concatenate(
+            [jnp.where(list_hot(lists, j) & (inner >= SLOTS), 1.0, 0.0) for j in range(4)],
+            axis=1,
+        ).astype(BF16)
+        next_sent_out[...] = pick_rows(hot, face_table(next_faces))
+    else:
+        (stack,) = rest
     column = iota((FACES, LANES), 0)
     hot = jnp.concatenate(
         [
@@ -331,10 +498,10 @@
         ],
         axis=1,
     )
-    found = pick(face_table(faces[...]), hot)
+    found = pick(face_table(faces), hot)
     for d in range(3):
         totals = products(
-            [lambda q: low[:, lanes(q)]], lambda _, q, p: star[q, p, d : d + 1, :], VPAD
+            [lambda q: low[:, lanes(q)]], lambda _, q, p: star[q, p, d : d + 1, :]
         )
         base = REM + OWN + VPAD * d
         for p in range(NQ):
@@ -343,27 +510,35 @@
         totals = products(
             [lambda q: faces[i * FPAD : (i + 1) * FPAD, lanes(q)]],
             lambda _, q, p: flux_self[q, p, i : i + 1, :],
-            FPAD,
         )
         for p in range(NQ):
             stack[REM + FPAD * i : REM + FPAD * (i + 1), lanes(p)] = totals[p]
     for i in range(4):
         totals = products(
-            [lambda q: found[q * FPAD : (q + 1) * FPAD, lanes(i)]],
+            [lambda q: found[place_of(q) : place_of(q) + FPAD, lanes(i)]],
             lambda _, q, p: flux_other[q, p, i : i + 1, :],
-            FPAD,
         )
         for code in range(3):
             mask = jnp.where(orientation[i : i + 1, :] == code, 1.0, 0.0)
             base = FPAD * (3 * i + code)
             for p in range(NQ):
                 stack[base : base + FPAD, lanes(p)] = totals[p] * mask
-    out[...] = state[...] + jnp.dot(
+    total = state + jnp.dot(
         lift[:, 0:DEEP], stack[...], precision=HIGH, preferred_element_type=F32
     )
-
-
-def remote_part(position, near, upper, lower, slot_flux, slot_code, slot_hot, lift, stack):
+    out[...] = total
+    if step + 1 < SUBSTEPS:
+        tall = jnp.concatenate([total[:, lanes(q)] for q in range(NQ)], axis=0)
+        found = pick_across(tall, narrow_hot[...])
+        narrow_out[...] = paired([found[NB * q : NB * (q + 1)] for q in range(NQ)])
+
+
+def by_elements(by_slot, slot_hot):
+    found = pick(by_slot, slot_hot)
+    return jnp.concatenate([found[NB * p : NB * (p + 1)] for p in range(NQ)], axis=1)
+
+
+def remote_part(position, near, upper, lower, slot_flux, slot_code, lift):
     odd = lax.rem(position, 2) == 1
     behind_up = lax.rem(position, 4) < 2
     up, down = upper[...], lower[...]
@@ -383,56 +558,50 @@
     )
     received = jnp.transpose(rows)
     totals = products(
-        [lambda q: received[q * FPAD : (q + 1) * FPAD]],
+        [lambda q: received[place_of(q) : place_of(q) + FPAD]],
         lambda _, q, p: slot_flux[16 * q + p : 16 * q + p + 1, :],
-        FPAD,
-    )
-    codes = [
-        jnp.broadcast_to(slot_code[code : code + 1, :], (SLOT_PAD, LANES)).astype(BF16)
-        for code in range(12)
-    ]
+    )
+    codes = [slot_code[SLOT_PAD * code : SLOT_PAD * (code + 1), :] for code in range(12)]
     gap = jnp.zeros((SLOT_PAD - FPAD, LANES), F32)
+    columns = []
     for p in range(NQ):
-        for half, part in enumerate(halves(jnp.concatenate([totals[p], gap], axis=0))):
-            for code in range(12):
-                start = SLOT_REM * half + SLOT_PAD * code
-                stack[start : start + SLOT_PAD, lanes(p)] = part * codes[code]
-    lifted = jnp.dot(lift[...], stack[...], preferred_element_type=F32)
+        both = halves(jnp.concatenate([totals[p], gap], axis=0))
+        masked = [part * mask for part in both for mask in codes]
+        columns.append(jnp.concatenate(masked, axis=0))
+    masked = jnp.concatenate(columns, axis=1)
+    lifted = jnp.dot(lift[...], masked, preferred_element_type=F32)
     lifted = lifted[0:NB] + lifted[PART : PART + NB]
-    by_slot = jnp.concatenate([lifted[:, lanes(p)] for p in range(NQ)], axis=0)
-    by_element = pick(by_slot, slot_hot[...].astype(BF16))
-    return jnp.concatenate([by_element[p * NB : (p + 1) * NB] for p in range(NQ)], axis=1)
+    return jnp.concatenate([lifted[:, lanes(p)] for p in range(NQ)], axis=0)
 
 
 def next_kernel(
-    place, state, near, upper, lower, slot_flux, slot_code, slot_hot, lift,
-    star, coarse, labels, weights, lists,
-    state_out, low_out, faces_out, pair_out, up_out, down_out, stack, *, step,
+    place, near, upper, lower, slot_flux, slot_code, lift,
+    narrow, slot_narrow, star, weights, tips, send_hot, coarse_sent,
+    by_slot_out, low_out, faces_out, pair_out, up_out, down_out,
 ):
     position = place[0]
-    now = state[...] + remote_part(
-        position, near, upper, lower, slot_flux, slot_code, slot_hot, lift, stack
-    )
-    state_out[...] = now
-    chain = chain_of(now, star, weights)
-    fine = integral_of(chain, taylor_weights(0.0, 1.0 / SUBSTEPS))
-    mask = labels[...] == 1
-    integral = jnp.concatenate(
-        [jnp.where(mask, fine[:, lanes(q)], coarse[step - 1, :, lanes(q)]) for q in range(NQ)],
-        axis=1,
-    )
-    low_out[...] = integral[0:VPAD]
-    project_and_send(
-        integral, weights, lists, position, faces_out, pair_out, up_out, down_out
-    )
+    by_slot = remote_part(position, near, upper, lower, slot_flux, slot_code, lift)
+    by_slot_out[...] = by_slot
+    found = pick(by_slot, slot_narrow[...])
+    now = narrow[...] + paired([found[NB * p : NB * (p + 1)] for p in range(NQ)])
+    chain, end = chain_of(now, star, weights, tips, narrow_sums, narrow_join)
+    first_weights = taylor_weights(0.0, 1.0 / SUBSTEPS)
+    integral = integral_of(chain, first_weights)
+    faces = weigh(weights, BACK, OWN, integral)
+    low, faces = with_end(integral, faces, -first_weights[-1] * end, tips)
+    low_out[...] = low
+    faces_out[...] = faces
+    found = pick_rows(send_hot[...], narrow_table(faces))
+    rows = PEERS * BOTH
+    sent = jnp.concatenate([found[0:rows], found[rows : 2 * rows]], axis=1) + coarse_sent[...]
+    deliver(sent, position, pair_out, up_out, down_out)
 
 
 def last_kernel(
-    place, state, near, upper, lower, slot_flux, slot_code, slot_hot, lift, out, stack
+    place, near, upper, lower, slot_flux, slot_code, lift, state, slot_hot, out
 ):
-    total = state[...] + remote_part(
-        place[0], near, upper, lower, slot_flux, slot_code, slot_hot, lift, stack
-    )
+    by_slot = remote_part(place[0], near, upper, lower, slot_flux, slot_code, lift)
+    total = state[...] + by_elements(by_slot, slot_hot[...])
     for q in range(NQ):
         out[q] = total[:, lanes(q)]
 
@@ -493,7 +662,6 @@
     star = star.transpose(1, 2, 0, 3)
     back = face_back.transpose(1, 0, 2)
     message = floats(BOTH, WIDTH)
-    stack = pltpu.VMEM((2 * SLOT_REM, COLS), BF16)
     sent_shapes = [floats(OWN, COLS), floats(2 * BOTH, WIDTH), message, message]
     like = lambda item: jax.ShapeDtypeStruct(item.shape, item.dtype)
     found = call(
@@ -502,7 +670,8 @@
         + later,
         [floats(NB, COLS), floats(VPAD, COLS), floats(TAIL, COLS)]
         + sent_shapes
-        + [jax.ShapeDtypeStruct((CHAIN_ROWS, 2 * LANES), BF16), like(star), like(labels)]
+        + [jax.ShapeDtypeStruct((CHAIN_ROWS, 2 * LANES), BF16)]
+        + [floats(24 + OWN, LANES), like(star), like(labels)]
         + [jax.ShapeDtypeStruct((PEERS * BOTH, LANES), jnp.int32)]
         + [like(item) for item in later],
         [(CHAIN_ROWS, LANES), (NQ, NB, LANES), stiff_time.shape, back.shape, (16, LANES)]
@@ -511,15 +680,28 @@
         scalars=1,
         inside=True,
     )
-    state, low, tail, faces, pair, up, down, weights, star, labels, lists = found[:11]
-    flux_self, flux_other, source, orientation, front, turn, vol = found[11:]
-    coarse, slot_flux, slot_code, slot_hot, lift, slot_lift = call(
+    state, low, tail, faces, pair, up, down, weights, tips, star, labels, lists = found[:12]
+    flux_self, flux_other, source, orientation, front, turn, vol = found[12:]
+    halved = lambda *shape: jax.ShapeDtypeStruct(shape, BF16)
+    prepared = call(
         prepare_kernel,
-        (state, tail, source, orientation, flux_other, front, turn, vol),
-        [floats(SUBSTEPS - 1, NB, COLS), floats(16 * NQ, LANES), floats(16, LANES), floats(LANES, LANES), floats(NB, DEEP_PAD),
-         jax.ShapeDtypeStruct((2 * PART, 2 * SLOT_REM), BF16)],
-        [(16 * NQ, FACES), (FPAD, FACES), (DEEP_PAD, LANES), (SLOT_REM, LANES)],
-    )
+        (state, tail, source, orientation, flux_other, front, turn, vol, star, labels, lists),
+        [
+            floats(SUBSTEPS - 1, NB, COLS), floats(16 * NQ, LANES), halved(SLOT_REM, LANES),
+            halved(LANES, LANES), floats(NB, DEEP_PAD), halved(2 * PART, 2 * SLOT_REM),
+            halved(LANES, LANES), halved(LANES, LANES), floats(TWOS * STAR_ROWS, LANES),
+            halved(2 * PEERS * BOTH, FACES),
+        ],
+        [
+            (16 * NQ, FACES), (FPAD, FACES), (DEEP_PAD, LANES), (SLOT_REM, LANES),
+            (NQ * STAR_ROWS, LANES),
+        ],
+    )
+    coarse, slot_flux, slot_code, slot_hot, lift, slot_lift = prepared[:6]
+    narrow_hot, slot_narrow, narrow_star, send_hot = prepared[6:]
+    fixed = (star, flux_self, flux_other, source, orientation, lift)
+    fixed += (coarse, weights, lists, narrow_hot, labels)
+    known = (state, low, faces)
     for step in range(SUBSTEPS):
         near = lax.all_gather(pair, "dom", axis_index_groups=pairs, tiled=True)
         relayed = lax.dynamic_slice(near, (partner_relay, 0), (BOTH, WIDTH))
@@ -528,23 +710,28 @@
         upper = jnp.concatenate([up, relayed], axis=0)
         upper = lax.ppermute(upper, "dom", swaps(count, 2))
         lower = lax.ppermute(lower, "dom", swaps(count, 0))
-        (state,) = call(
-            local_kernel,
-            (state, low, faces, star, flux_self, flux_other, source, orientation, lift),
-            [floats(NB, COLS)],
+        ahead = [floats(NB, NARROW), floats(OWN, COLS), floats(PEERS * BOTH, WIDTH)]
+        state, *made = call(
+            functools.partial(local_kernel, step=step),
+            known + fixed,
+            [floats(NB, COLS)] + (ahead if step + 1 < SUBSTEPS else []),
             [(DEEP, COLS)],
         )
-        received = (place, state, near, upper, lower, slot_flux, slot_code, slot_hot, slot_lift)
+        received = (place, near, upper, lower, slot_flux, slot_code, slot_lift)
         if step + 1 < SUBSTEPS:
-            state, low, faces, pair, up, down = call(
-                functools.partial(next_kernel, step=step + 1),
-                received + (star, coarse, labels, weights, lists),
-                [floats(NB, COLS), floats(VPAD, COLS)] + sent_shapes,
-                [stack],
+            narrow, coarse_faces, coarse_sent = made
+            by_slot, low, faces, pair, up, down = call(
+                next_kernel,
+                received
+                + (narrow, slot_narrow, narrow_star, weights, tips, send_hot, coarse_sent),
+                [floats(NQ * NB, LANES), floats(VPAD, NARROW), floats(OWN, NARROW)]
+                + sent_shapes[1:],
+                [],
                 scalars=1,
             )
+            known = (state, by_slot, slot_hot, low, faces, coarse_faces)
     (result,) = call(
-        last_kernel, received, [floats(NQ, NB, LANES)], [stack], scalars=1
+        last_kernel, received + (state, slot_hot), [floats(NQ, NB, LANES)], [], scalars=1
     )
     return result.transpose(1, 0, 2)
 

time: 69.9 us -> 68.8 us (0.984)
  waiting for transfers between devices: 7.09 us -> 4.77 us
  Pallas kernels: 21.4 us -> 22.6 us
    ppermute x4, waiting for transfers between devices: 5.46 us -> 3.91 us  [local(): upper = lax.ppermute(upper, 'dom', swaps(count, 2))]
    pallas_call x10, Pallas kernels: 21.4 us -> 22.6 us  [call(): pl.pallas_call(kernel, in_specs=[smem] * scalars + [given] * (len(args) -...]
    ppermute x4, waiting for transfers between devices: 1.63 us -> 0.86 us  [local(): lower = lax.ppermute(lower, 'dom', swaps(count, 0))]
  transfers between devices with their start and end apart: 8 -> 8, of which waited for: 5 -> 5; matrix products, arithmetic and copies ran while one was open for 0% -> 0% of each run, Pallas kernels for 13% -> 16%
where the time goes in v5:
time: 68.8 us; the launch traced here: 68.5 us
  starting transfers between devices  33.3 us (48%)
  Pallas kernels  22.6 us (33%)
  blocking collectives  7.51 us (11%)
  waiting for transfers between devices  4.77 us (7%)
    ppermute x4, starting transfers between devices, local(): upper = lax.ppermute(upper, 'dom', swaps(count, 2))  25.5 us
    pallas_call x10, Pallas kernels, call(): pl.pallas_call(kernel, in_specs=[smem] * scalars + [given] * (len(args) -...  22.6 us
    ppermute x4, starting transfers between devices, local(): lower = lax.ppermute(lower, 'dom', swaps(count, 0))  7.86 us
    all_gather x4, blocking collectives, local(): near = lax.all_gather(pair, 'dom', axis_index_groups=pairs, tiled=True)  7.51 us
    ppermute x4, waiting for transfers between devices, local(): upper = lax.ppermute(upper, 'dom', swaps(count, 2))  3.91 us
  transfers between devices with their start and end apart: 8, of which 5 were waited for; matrix products, arithmetic and copies ran while one was open for 0% of the time, Pallas kernels for 16%

profile of v5, /device:TPU:384, one launch (start us, length us, event | category | flops | bytes accessed | tf_op | source)
XLA Modules:
  0.0 68.5 jit_solution(7251900279637940962)
XLA Ops:
  0.0 3.2 %shard_map.136 = (f32[56,1152]{1,0:T(8,128)S(1)}, f32[40,1152]{1,0:T(8,128)S(1)}, f32[96,1152]{1,0:T(8,128)S(1)}, f32[96,1152]{1,0:T(8,128)S(1)}, f32[48,256]{1,...) custom-call(s32[1]{0:T(128)} %bitcast.place, ...), custom_call_target="tpu_custom_call" | custom-call | flops 20000000 | bytes 3279612 | tf_op jit(solution)/shard_map/pallas_call | solution.py:622
  3.3 1.9 %all_gather.12.near = f32[96,256]{1,0:T(8,128)S(1)} all-gather(f32[48,256]{1,0:T(8,128)S(1)} %get-tuple-element.76), channel_id=1, replica_groups={{0,1},{2,3},{4,5},{6,7},{8,9},{10,11},{12,13},{14,15},{16,17},{18,19},{..., dimensions={0}, use_global_device_ids=true | all-gather | bytes 147456 | tf_op jit(solution)/shard_map/all_gather | solution.py:706
  5.2 8.8 %collective-permute-start = (f32[48,256]{1,0:T(8,128)S(1)}, f32[48,256]{1,0:T(8,128)S(1)}, u32[]{:S(2)}, u32[]{:S(2)}) collective-permute-start(f32[48,256]{1,0:T(8,128)S(1)} %pad_maximum_fusion.1), channel_id=1, source_target_pairs={{2,4},{4,2},{3,5},{5,3},{6,8},{8,6},{7,9},{9,7},{10,12},{12,10},{1... | collective-permute-start | bytes 147464 | tf_op jit(solution)/shard_map/ppermute | solution.py:711
  13.9 1.9 %collective-permute-start.1 = (f32[48,256]{1,0:T(8,128)S(1)}, f32[48,256]{1,0:T(8,128)S(1)}, u32[]{:S(2)}, u32[]{:S(2)}) collective-permute-start(f32[48,256]{1,0:T(8,128)S(1)} %pad_maximum_fusion), channel_id=1, source_target_pairs={{0,2},{2,0},{1,3},{3,1},{4,6},{6,4},{5,7},{7,5},{8,10},{10,8},{9,1... | collective-permute-start | bytes 147464 | tf_op jit(solution)/shard_map/ppermute | solution.py:712
  15.9 1.1 %shard_map.137 = (f32[3,56,1152]{2,1,0:T(8,128)S(1)}, f32[144,128]{1,0:T(8,128)S(1)}, bf16[384,128]{1,0:T(8,128)(2,1)S(1)}, bf16[128,128]{1,0:T(8,128)(2,1)S(1)}...) custom-call(f32[56,1152]{1,0:T(8,128)S(1)} %get-tuple-element.82.sta, ...), custom_call_target="tpu_custom_call" | custom-call | flops 20000000 | bytes 3336716 | tf_op jit(solution)/shard_map/pallas_call | solution.py:622
  17.0 2.5 %shard_map.138 = (f32[56,1152]{1,0:T(8,128)S(1)}, f32[56,640]{1,0:T(8,128)S(1)}, f32[96,1152]{1,0:T(8,128)S(1)}, f32[96,256]{1,0:T(8,128)S(1)}) custom-call(f32[56,1152]{1,0:T(8,128)S(1)} %get-tuple-element.82.state.refs_0_, f32[40,1152]{1,0:T(8,128)S(1)} %get-tuple-element.96.refs_1_, f32[96,1152]{1,0:T(8,128)S(1)} %get-tuple-element.97.refs_2_, ...), custom_call_target="tpu_custom_call" | custom-call | flops 20000000 | bytes 3717120 | tf_op jit(solution)/shard_map/pallas_call | solution.py:622
  19.5 0.0 collective-permute-done.upper
  19.5 0.4 collective-permute-done.1.lower
  19.9 2.2 %shard_map.139 = (f32[504,128]{1,0:T(8,128)S(1)}, f32[40,640]{1,0:T(8,128)S(1)}, f32[96,640]{1,0:T(8,128)S(1)}, f32[48,256]{1,0:T(8,128)S(1)}, f32[24,256]{1,0:T(8,128)S(1)}, /*index=5*/f32[24,256]{1,0:T(8,128)S(1)}) custom-call(s32[1]{0:T(128)} %bitcast.place, f32[96,256]{1,0:T(8,128)S(1)} %all_gather.12.near, f32[48,256]{1,0:T(8,128)S(1)} %collective-permute-done.upper, ...), custom_call_target="tpu_custom_call" | custom-call | flops 20000000 | bytes 2854916 | tf_op jit(solution)/shard_map/pallas_call | solution.py:622
  22.2 1.9 %all_gather.13.near = f32[96,256]{1,0:T(8,128)S(1)} all-gather(f32[48,256]{1,0:T(8,128)S(1)} %get-tuple-element.109), channel_id=1, replica_groups={{0,1},{2,3},{4,5},{6,7},{8,9},{10,11},{12,13},{14,15},{16,17},{18,19},{..., dimensions={0}, use_global_device_ids=true | all-gather | bytes 147456 | tf_op jit(solution)/shard_map/all_gather | solution.py:706
  24.1 5.4 %collective-permute-start.2 = (f32[48,256]{1,0:T(8,128)S(1)}, f32[48,256]{1,0:T(8,128)S(1)}, u32[]{:S(2)}, u32[]{:S(2)}) collective-permute-start(f32[48,256]{1,0:T(8,128)S(1)} %pad_maximum_fusion.3), channel_id=1, source_target_pairs={{2,4},{4,2},{3,5},{5,3},{6,8},{8,6},{7,9},{9,7},{10,12},{12,10},{1... | collective-permute-start | bytes 147464 | tf_op jit(solution)/shard_map/ppermute | solution.py:711
  29.5 1.9 %collective-permute-start.3 = (f32[48,256]{1,0:T(8,128)S(1)}, f32[48,256]{1,0:T(8,128)S(1)}, u32[]{:S(2)}, u32[]{:S(2)}) collective-permute-start(f32[48,256]{1,0:T(8,128)S(1)} %pad_maximum_fusion.2), channel_id=1, source_target_pairs={{0,2},{2,0},{1,3},{3,1},{4,6},{6,4},{5,7},{7,5},{8,10},{10,8},{9,1... | collective-permute-start | bytes 147464 | tf_op jit(solution)/shard_map/ppermute | solution.py:712
  31.4 2.7 %shard_map.140 = (f32[56,1152]{1,0:T(8,128)S(1)}, f32[56,640]{1,0:T(8,128)S(1)}, f32[96,1152]{1,0:T(8,128)S(1)}, f32[96,256]{1,0:T(8,128)S(1)}) custom-call(f32[56,1152]{1,0:T(8,128)S(1)} %get-tuple-element.115.refs_0_, f32[504,128]{1,0:T(8,128)S(1)} %get-tuple-element.116.refs_1_, bf16[128,128]{1,0:T(8,128)(2,1)S(1)} %get-tuple-element.117.refs_2_.slot_hot, ...), custom_call_target="tpu_custom_call" | custom-call | flops 20000000 | bytes 4204544 | tf_op jit(solution)/shard_map/pallas_call | solution.py:622
  34.1 1.4 %collective-permute-done.2.upper = f32[48,256]{1,0:T(8,128)S(1)} collective-permute-done((f32[48,256]{1,0:T(8,128)S(1)}, f32[48,256]{1,0:T(8,128)S(1)}, u32[]{:S(2)}, u32[]{:S(2)}) %collective-permute-start.2) | collective-permute-done | bytes 49184 | tf_op jit(solution)/shard_map/ppermute | solution.py:711
  35.5 0.0 collective-permute-done.3.lower
  35.5 2.2 %shard_map.141 = (f32[504,128]{1,0:T(8,128)S(1)}, f32[40,640]{1,0:T(8,128)S(1)}, f32[96,640]{1,0:T(8,128)S(1)}, f32[48,256]{1,0:T(8,128)S(1)}, f32[24,256]{1,0:T(8,128)S(1)}, /*index=5*/f32[24,256]{1,0:T(8,128)S(1)}) custom-call(s32[1]{0:T(128)} %bitcast.place, f32[96,256]{1,0:T(8,128)S(1)} %all_gather.13.near, f32[48,256]{1,0:T(8,128)S(1)} %collective-permute-done.2.upper, ...), custom_call_target="tpu_custom_call" | custom-call | flops 20000000 | bytes 2854916 | tf_op jit(solution)/shard_map/pallas_call | solution.py:622
  37.7 1.9 %all_gather.14.near = f32[96,256]{1,0:T(8,128)S(1)} all-gather(f32[48,256]{1,0:T(8,128)S(1)} %get-tuple-element.123), channel_id=1, replica_groups={{0,1},{2,3},{4,5},{6,7},{8,9},{10,11},{12,13},{14,15},{16,17},{18,19},{..., dimensions={0}, use_global_device_ids=true | all-gather | bytes 147456 | tf_op jit(solution)/shard_map/all_gather | solution.py:706
  39.6 5.9 %collective-permute-start.4 = (f32[48,256]{1,0:T(8,128)S(1)}, f32[48,256]{1,0:T(8,128)S(1)}, u32[]{:S(2)}, u32[]{:S(2)}) collective-permute-start(f32[48,256]{1,0:T(8,128)S(1)} %pad_maximum_fusion.5), channel_id=1, source_target_pairs={{2,4},{4,2},{3,5},{5,3},{6,8},{8,6},{7,9},{9,7},{10,12},{12,10},{1... | collective-permute-start | bytes 147464 | tf_op jit(solution)/shard_map/ppermute | solution.py:711
  45.5 2.1 %collective-permute-start.5 = (f32[48,256]{1,0:T(8,128)S(1)}, f32[48,256]{1,0:T(8,128)S(1)}, u32[]{:S(2)}, u32[]{:S(2)}) collective-permute-start(f32[48,256]{1,0:T(8,128)S(1)} %pad_maximum_fusion.4), channel_id=1, source_target_pairs={{0,2},{2,0},{1,3},{3,1},{4,6},{6,4},{5,7},{7,5},{8,10},{10,8},{9,1... | collective-permute-start | bytes 147464 | tf_op jit(solution)/shard_map/ppermute | solution.py:712
  47.6 2.7 %shard_map.142 = (f32[56,1152]{1,0:T(8,128)S(1)}, f32[56,640]{1,0:T(8,128)S(1)}, f32[96,1152]{1,0:T(8,128)S(1)}, f32[96,256]{1,0:T(8,128)S(1)}) custom-call(f32[56,1152]{1,0:T(8,128)S(1)} %get-tuple-element.129.refs_0_, f32[504,128]{1,0:T(8,128)S(1)} %get-tuple-element.130.refs_1_, bf16[128,128]{1,0:T(8,128)(2,1)S(1)} %get-tuple-element.117.refs_2_.slot_hot, ...), custom_call_target="tpu_custom_call" | custom-call | flops 20000000 | bytes 4204544 | tf_op jit(solution)/shard_map/pallas_call | solution.py:622
  50.3 0.8 %collective-permute-done.4.upper = f32[48,256]{1,0:T(8,128)S(1)} collective-permute-done((f32[48,256]{1,0:T(8,128)S(1)}, f32[48,256]{1,0:T(8,128)S(1)}, u32[]{:S(2)}, u32[]{:S(2)}) %collective-permute-start.4) | collective-permute-done | bytes 49184 | tf_op jit(solution)/shard_map/ppermute | solution.py:711
  51.1 0.4 collective-permute-done.5.lower
  51.5 2.2 %shard_map.143 = (f32[504,128]{1,0:T(8,128)S(1)}, f32[40,640]{1,0:T(8,128)S(1)}, f32[96,640]{1,0:T(8,128)S(1)}, f32[48,256]{1,0:T(8,128)S(1)}, f32[24,256]{1,0:T(8,128)S(1)}, /*index=5*/f32[24,256]{1,0:T(8,128)S(1)}) custom-call(s32[1]{0:T(128)} %bitcast.place, f32[96,256]{1,0:T(8,128)S(1)} %all_gather.14.near, f32[48,256]{1,0:T(8,128)S(1)} %collective-permute-done.4.upper, ...), custom_call_target="tpu_custom_call" | custom-call | flops 20000000 | bytes 2854916 | tf_op jit(solution)/shard_map/pallas_call | solution.py:622
  53.7 1.9 %all_gather.15.near = f32[96,256]{1,0:T(8,128)S(1)} all-gather(f32[48,256]{1,0:T(8,128)S(1)} %get-tuple-element.136), channel_id=1, replica_groups={{0,1},{2,3},{4,5},{6,7},{8,9},{10,11},{12,13},{14,15},{16,17},{18,19},{..., dimensions={0}, use_global_device_ids=true | all-gather | bytes 147456 | tf_op jit(solution)/shard_map/all_gather | solution.py:706
  55.6 5.4 %collective-permute-start.6 = (f32[48,256]{1,0:T(8,128)S(1)}, f32[48,256]{1,0:T(8,128)S(1)}, u32[]{:S(2)}, u32[]{:S(2)}) collective-permute-start(f32[48,256]{1,0:T(8,128)S(1)} %pad_maximum_fusion.7), channel_id=1, source_target_pairs={{2,4},{4,2},{3,5},{5,3},{6,8},{8,6},{7,9},{9,7},{10,12},{12,10},{1... | collective-permute-start | bytes 147464 | tf_op jit(solution)/shard_map/ppermute | solution.py:711
  61.1 1.9 %collective-permute-start.7 = (f32[48,256]{1,0:T(8,128)S(1)}, f32[48,256]{1,0:T(8,128)S(1)}, u32[]{:S(2)}, u32[]{:S(2)}) collective-permute-start(f32[48,256]{1,0:T(8,128)S(1)} %pad_maximum_fusion.6), channel_id=1, source_target_pairs={{0,2},{2,0},{1,3},{3,1},{4,6},{6,4},{5,7},{7,5},{8,10},{10,8},{9,1... | collective-permute-start | bytes 147464 | tf_op jit(solution)/shard_map/ppermute | solution.py:712
  63.0 2.3 %shard_map.144.state = f32[56,1152]{1,0:T(8,128)S(1)} custom-call(f32[56,1152]{1,0:T(8,128)S(1)} %get-tuple-element.142.refs_0_, f32[504,128]{1,0:T(8,128)S(1)} %get-tuple-element.143.refs_1_, bf16[128,128]{1,0:T(8,128)(2,1)S(1)} %get-tuple-element.117.refs_2_.slot_hot, f32[40,640]{1,0:T(8,128)S(1)} %get-tuple-element.144.refs_3_, ...), custom_call_target="tpu_custom_call" | custom-call | flops 20000000 | bytes 3520512 | tf_op jit(solution)/shard_map/pallas_call | solution.py:622
  65.3 1.7 %collective-permute-done.6.upper = f32[48,256]{1,0:T(8,128)S(1)} collective-permute-done((f32[48,256]{1,0:T(8,128)S(1)}, f32[48,256]{1,0:T(8,128)S(1)}, u32[]{:S(2)}, u32[]{:S(2)}) %collective-permute-start.6) | collective-permute-done | bytes 49184 | tf_op jit(solution)/shard_map/ppermute | solution.py:711
  67.1 0.0 collective-permute-done.7.lower
  67.1 1.4 %shard_map.145 = f32[9,56,128]{2,1,0:T(8,128)} custom-call(s32[1]{0:T(128)} %bitcast.place, f32[96,256]{1,0:T(8,128)S(1)} %all_gather.15.near, f32[48,256]{1,0:T(8,128)S(1)} %collective-permute-done.6.upper, f32[48,256]{1,0:T(8,128)S(1)} %collective-permute-done.7.lower, f32[144,128]{1,0:T(8,128)S(1)} %get-tuple-element.93.slot_flux, ...), custom_call_target="tpu_custom_call" | custom-call | flops 20000000 | bytes 1441796 | tf_op jit(solution)/shard_map/pallas_call | solution.py:622
  (12 shorter events, 0.1 us)
Async XLA Ops:
  5.2 14.3 %collective-permute-start = (f32[48,256]{1,0:T(8,128)S(1)}, f32[48,256]{1,0:T(8,128)S(1)}, u32[]{:S(2)}, u32[]{:S(2)}) collective-permute-start(f32[48,256]{1,0:T(8,128)S(1)} %pad_maximum_fusion.1), channel_id=1, source_target_pairs={{2,4},{4,2},{3,5},{5,3},{6,8},{8,6},{7,9},{9,7},{10,12},{12,10},{1... | collective-permute-start | bytes 147464 | tf_op jit(solution)/shard_map/ppermute | solution.py:711
  13.9 6.0 %collective-permute-start.1 = (f32[48,256]{1,0:T(8,128)S(1)}, f32[48,256]{1,0:T(8,128)S(1)}, u32[]{:S(2)}, u32[]{:S(2)}) collective-permute-start(f32[48,256]{1,0:T(8,128)S(1)} %pad_maximum_fusion), channel_id=1, source_target_pairs={{0,2},{2,0},{1,3},{3,1},{4,6},{6,4},{5,7},{7,5},{8,10},{10,8},{9,1... | collective-permute-start | bytes 147464 | tf_op jit(solution)/shard_map/ppermute | solution.py:712
  24.1 11.4 %collective-permute-start.2 = (f32[48,256]{1,0:T(8,128)S(1)}, f32[48,256]{1,0:T(8,128)S(1)}, u32[]{:S(2)}, u32[]{:S(2)}) collective-permute-start(f32[48,256]{1,0:T(8,128)S(1)} %pad_maximum_fusion.3), channel_id=1, source_target_pairs={{2,4},{4,2},{3,5},{5,3},{6,8},{8,6},{7,9},{9,7},{10,12},{12,10},{1... | collective-permute-start | bytes 147464 | tf_op jit(solution)/shard_map/ppermute | solution.py:711
  29.5 6.0 %collective-permute-start.3 = (f32[48,256]{1,0:T(8,128)S(1)}, f32[48,256]{1,0:T(8,128)S(1)}, u32[]{:S(2)}, u32[]{:S(2)}) collective-permute-start(f32[48,256]{1,0:T(8,128)S(1)} %pad_maximum_fusion.2), channel_id=1, source_target_pairs={{0,2},{2,0},{1,3},{3,1},{4,6},{6,4},{5,7},{7,5},{8,10},{10,8},{9,1... | collective-permute-start | bytes 147464 | tf_op jit(solution)/shard_map/ppermute | solution.py:712
  39.6 11.4 %collective-permute-start.4 = (f32[48,256]{1,0:T(8,128)S(1)}, f32[48,256]{1,0:T(8,128)S(1)}, u32[]{:S(2)}, u32[]{:S(2)}) collective-permute-start(f32[48,256]{1,0:T(8,128)S(1)} %pad_maximum_fusion.5), channel_id=1, source_target_pairs={{2,4},{4,2},{3,5},{5,3},{6,8},{8,6},{7,9},{9,7},{10,12},{12,10},{1... | collective-permute-start | bytes 147464 | tf_op jit(solution)/shard_map/ppermute | solution.py:711
  45.5 6.0 %collective-permute-start.5 = (f32[48,256]{1,0:T(8,128)S(1)}, f32[48,256]{1,0:T(8,128)S(1)}, u32[]{:S(2)}, u32[]{:S(2)}) collective-permute-start(f32[48,256]{1,0:T(8,128)S(1)} %pad_maximum_fusion.4), channel_id=1, source_target_pairs={{0,2},{2,0},{1,3},{3,1},{4,6},{6,4},{5,7},{7,5},{8,10},{10,8},{9,1... | collective-permute-start | bytes 147464 | tf_op jit(solution)/shard_map/ppermute | solution.py:712
  55.6 11.4 %collective-permute-start.6 = (f32[48,256]{1,0:T(8,128)S(1)}, f32[48,256]{1,0:T(8,128)S(1)}, u32[]{:S(2)}, u32[]{:S(2)}) collective-permute-start(f32[48,256]{1,0:T(8,128)S(1)} %pad_maximum_fusion.7), channel_id=1, source_target_pairs={{2,4},{4,2},{3,5},{5,3},{6,8},{8,6},{7,9},{9,7},{10,12},{12,10},{1... | collective-permute-start | bytes 147464 | tf_op jit(solution)/shard_map/ppermute | solution.py:711
  61.1 6.0 %collective-permute-start.7 = (f32[48,256]{1,0:T(8,128)S(1)}, f32[48,256]{1,0:T(8,128)S(1)}, u32[]{:S(2)}, u32[]{:S(2)}) collective-permute-start(f32[48,256]{1,0:T(8,128)S(1)} %pad_maximum_fusion.6), channel_id=1, source_target_pairs={{0,2},{2,0},{1,3},{3,1},{4,6},{6,4},{5,7},{7,5},{8,10},{10,8},{9,1... | collective-permute-start | bytes 147464 | tf_op jit(solution)/shard_map/ppermute | solution.py:712

commit v6 on v5

--- a/solution.py
+++ b/solution.py
@@ -261,15 +261,12 @@
     return lists[...] == iota((PEERS * BOTH, LANES), 1) + LANES * face
 
 
-def deliver(sent, position, pair_out, up_out, down_out):
+def deliver(sent, position, pair_out, cross_out):
     odd = lax.rem(position, 2) == 1
     first, second = sent[0:BOTH], sent[BOTH : 2 * BOTH]
     pair_out[0:BOTH, :] = jnp.where(odd, second, first)
-    pair_out[BOTH : 2 * BOTH, :] = jnp.where(odd, first, second)
-    behind_up = lax.rem(position, 4) < 2
-    ahead, behind = sent[2 * BOTH : 3 * BOTH], sent[3 * BOTH : 4 * BOTH]
-    up_out[...] = jnp.where(behind_up, behind, ahead)
-    down_out[...] = jnp.where(behind_up, ahead, behind)
+    pair_out[BOTH : 3 * BOTH, :] = sent[2 * BOTH : 4 * BOTH]
+    cross_out[...] = jnp.where(odd, first, second)
 
 
 def list_column(fine, coarse):
@@ -288,11 +285,11 @@
 ):
     later = rest[:7]
     (
-        state_out, low_out, tail_out, faces_out, pair_out, up_out, down_out,
+        state_out, low_out, tail_out, faces_out, pair_out, cross_out,
         weights_out, tips_out, star_out, labels_out, lists_out,
-    ) = rest[7:19]
-    later_out = rest[19:26]
-    raw, dofs_here, time_here, back_here, wide, fine_here, coarse_here, ready = rest[26:]
+    ) = rest[7:18]
+    later_out = rest[18:25]
+    raw, dofs_here, time_here, back_here, wide, fine_here, coarse_here, ready = rest[25:]
     position = place[0]
     moves = [
         (dofs, dofs_here),
@@ -334,7 +331,7 @@
     hot = jnp.concatenate(
         [jnp.where(list_hot(lists_out, j), 1.0, 0.0) for j in range(4)], axis=1
     ).astype(BF16)
-    deliver(pick_rows(hot, face_table(faces)), position, pair_out, up_out, down_out)
+    deliver(pick_rows(hot, face_table(faces)), position, pair_out, cross_out)
     end = jnp.where(iota((8, COLS), 0) == 0, end, 0.0)
     tail_out[...] = jnp.concatenate(chain[1:] + [end], axis=0)
     for copy in copies[first:]:
@@ -544,14 +541,13 @@
     up, down = upper[...], lower[...]
     behind = jnp.where(behind_up, up, down)
     ahead = jnp.where(behind_up, down, up)
-    here = jnp.where(odd, near[0:BOTH, :], near[2 * BOTH : 3 * BOTH, :])
-    relayed = slice(BOTH, 2 * BOTH)
+    here = jnp.where(odd, near[0:BOTH, :], near[3 * BOTH : 4 * BOTH, :])
     rows = jnp.concatenate(
         [
-            jnp.where(odd, here, behind[relayed]),
-            jnp.where(odd, ahead[relayed], here),
-            behind[0:BOTH],
-            ahead[0:BOTH],
+            jnp.where(odd, here, behind[0:BOTH]),
+            jnp.where(odd, ahead[0:BOTH], here),
+            behind[BOTH : 2 * BOTH],
+            ahead[BOTH : 2 * BOTH],
             jnp.zeros((LANES - PEERS * BOTH, WIDTH), F32),
         ],
         axis=0,
@@ -577,7 +573,7 @@
 def next_kernel(
     place, near, upper, lower, slot_flux, slot_code, lift,
     narrow, slot_narrow, star, weights, tips, send_hot, coarse_sent,
-    by_slot_out, low_out, faces_out, pair_out, up_out, down_out,
+    by_slot_out, low_out, faces_out, pair_out, cross_out,
 ):
     position = place[0]
     by_slot = remote_part(position, near, upper, lower, slot_flux, slot_code, lift)
@@ -594,7 +590,7 @@
     found = pick_rows(send_hot[...], narrow_table(faces))
     rows = PEERS * BOTH
     sent = jnp.concatenate([found[0:rows], found[rows : 2 * rows]], axis=1) + coarse_sent[...]
-    deliver(sent, position, pair_out, up_out, down_out)
+    deliver(sent, position, pair_out, cross_out)
 
 
 def last_kernel(
@@ -634,9 +630,9 @@
 
 def swaps(count, first):
     pairs = []
-    for low in range(count - 2):
-        if low % 4 in (first, first + 1):
-            pairs += [(low, low + 2), (low + 2, low)]
+    for low in range(2 * first, count - 2, 4):
+        for one, other in ((low, low + 3), (low + 1, low + 2)):
+            pairs += [(one, other), (other, one)]
     return pairs
 
 
@@ -647,7 +643,9 @@
     count = lax.axis_size("dom")
     pairs = [[low, low + 1] for low in range(0, count, 2)]
     place = lax.axis_index("dom").astype(jnp.int32)
-    partner_relay = jnp.where(place % 2 == 1, BOTH, 3 * BOTH)
+    partner = jnp.where(place % 2 == 1, BOTH, 4 * BOTH)
+    upper_from = partner + jnp.where(place % 4 >= 2, 0, BOTH)
+    lower_from = partner + jnp.where(place % 4 >= 2, BOTH, 0)
     place = place.reshape(1)
     labels = labels.reshape(1, LANES)
     later = (
@@ -662,7 +660,7 @@
     star = star.transpose(1, 2, 0, 3)
     back = face_back.transpose(1, 0, 2)
     message = floats(BOTH, WIDTH)
-    sent_shapes = [floats(OWN, COLS), floats(2 * BOTH, WIDTH), message, message]
+    sent_shapes = [floats(OWN, COLS), floats(3 * BOTH, WIDTH), message]
     like = lambda item: jax.ShapeDtypeStruct(item.shape, item.dtype)
     found = call(
         first_kernel,
@@ -680,8 +678,8 @@
         scalars=1,
         inside=True,
     )
-    state, low, tail, faces, pair, up, down, weights, tips, star, labels, lists = found[:12]
-    flux_self, flux_other, source, orientation, front, turn, vol = found[12:]
+    state, low, tail, faces, pair, cross, weights, tips, star, labels, lists = found[:11]
+    flux_self, flux_other, source, orientation, front, turn, vol = found[11:]
     halved = lambda *shape: jax.ShapeDtypeStruct(shape, BF16)
     prepared = call(
         prepare_kernel,
@@ -704,11 +702,12 @@
     known = (state, low, faces)
     for step in range(SUBSTEPS):
         near = lax.all_gather(pair, "dom", axis_index_groups=pairs, tiled=True)
-        relayed = lax.dynamic_slice(near, (partner_relay, 0), (BOTH, WIDTH))
-        lower = jnp.concatenate([down, relayed], axis=0)
-        lower, up, relayed = lax.optimization_barrier((lower, up, relayed))
-        upper = jnp.concatenate([up, relayed], axis=0)
-        upper = lax.ppermute(upper, "dom", swaps(count, 2))
+        passed = lax.dynamic_slice(near, (lower_from, 0), (BOTH, WIDTH))
+        lower = jnp.concatenate([cross, passed], axis=0)
+        lower, cross, shared = lax.optimization_barrier((lower, cross, near))
+        passed = lax.dynamic_slice(shared, (upper_from, 0), (BOTH, WIDTH))
+        upper = jnp.concatenate([cross, passed], axis=0)
+        upper = lax.ppermute(upper, "dom", swaps(count, 1))
         lower = lax.ppermute(lower, "dom", swaps(count, 0))
         ahead = [floats(NB, NARROW), floats(OWN, COLS), floats(PEERS * BOTH, WIDTH)]
         state, *made = call(
@@ -720,7 +719,7 @@
         received = (place, near, upper, lower, slot_flux, slot_code, slot_lift)
         if step + 1 < SUBSTEPS:
             narrow, coarse_faces, coarse_sent = made
-            by_slot, low, faces, pair, up, down = call(
+            by_slot, low, faces, pair, cross = call(
                 next_kernel,
                 received
                 + (narrow, slot_narrow, narrow_star, weights, tips, send_hot, coarse_sent),

time: 68.8 us -> 67.3 us (0.978)
  waiting for transfers between devices: 4.77 us -> 2.65 us
    ppermute x4, waiting for transfers between devices: 3.91 us -> 2.21 us  [local(): upper = lax.ppermute(upper, 'dom', swaps(count, 1))]
  transfers between devices with their start and end apart: 8 -> 8, of which waited for: 5 -> 5; matrix products, arithmetic and copies ran while one was open for 0% -> 0% of each run, Pallas kernels for 16% -> 17%
where the time goes in v6:
time: 67.3 us; the launch traced here: 66.4 us
  starting transfers between devices  33.2 us (49%)
  Pallas kernels  22.7 us (34%)
  blocking collectives  7.66 us (11%)
  waiting for transfers between devices  2.65 us (4%)
    ppermute x4, starting transfers between devices, local(): upper = lax.ppermute(upper, 'dom', swaps(count, 1))  25.3 us
    pallas_call x10, Pallas kernels, call(): pl.pallas_call(kernel, in_specs=[smem] * scalars + [given] * (len(args) -...  22.7 us
    ppermute x4, starting transfers between devices, local(): lower = lax.ppermute(lower, 'dom', swaps(count, 0))  7.86 us
    all_gather x4, blocking collectives, local(): near = lax.all_gather(pair, 'dom', axis_index_groups=pairs, tiled=True)  7.66 us
    ppermute x4, waiting for transfers between devices, local(): upper = lax.ppermute(upper, 'dom', swaps(count, 1))  2.21 us
  transfers between devices with their start and end apart: 8, of which 5 were waited for; matrix products, arithmetic and copies ran while one was open for 0% of the time, Pallas kernels for 17%

profile of v6, /device:TPU:384, one launch (start us, length us, event | category | flops | bytes accessed | tf_op | source)
XLA Modules:
  0.0 66.4 jit_solution(172148816384165148)
XLA Ops:
  0.0 3.2 %shard_map.136 = (f32[56,1152]{1,0:T(8,128)S(1)}, f32[40,1152]{1,0:T(8,128)S(1)}, f32[96,1152]{1,0:T(8,128)S(1)}, f32[96,1152]{1,0:T(8,128)S(1)}, f32[72,256]{1,...) custom-call(s32[1]{0:T(128)} %bitcast.place, ...), custom_call_target="tpu_custom_call" | custom-call | flops 20000000 | bytes 3279612 | tf_op jit(solution)/shard_map/pallas_call | solution.py:618
  3.3 1.9 %all_gather.12.near = f32[144,256]{1,0:T(8,128)S(1)} all-gather(f32[72,256]{1,0:T(8,128)S(1)} %get-tuple-element.72), channel_id=1, replica_groups={{0,1},{2,3},{4,5},{6,7},{8,9},{10,11},{12,13},{14,15},{16,17},{18,19},{..., dimensions={0}, use_global_device_ids=true | all-gather | bytes 221184 | tf_op jit(solution)/shard_map/all_gather | solution.py:704
  5.2 8.5 %collective-permute-start = (f32[48,256]{1,0:T(8,128)S(1)}, f32[48,256]{1,0:T(8,128)S(1)}, u32[]{:S(2)}, u32[]{:S(2)}) collective-permute-start(f32[48,256]{1,0:T(8,128)S(1)} %pad_maximum_fusion.1), channel_id=1, source_target_pairs={{2,5},{5,2},{3,4},{4,3},{6,9},{9,6},{7,8},{8,7},{10,13},{13,10},{1... | collective-permute-start | bytes 147464 | tf_op jit(solution)/shard_map/ppermute | solution.py:710
  13.7 1.9 %collective-permute-start.1 = (f32[48,256]{1,0:T(8,128)S(1)}, f32[48,256]{1,0:T(8,128)S(1)}, u32[]{:S(2)}, u32[]{:S(2)}) collective-permute-start(f32[48,256]{1,0:T(8,128)S(1)} %pad_maximum_fusion), channel_id=1, source_target_pairs={{0,3},{3,0},{1,2},{2,1},{4,7},{7,4},{5,6},{6,5},{8,11},{11,8},{9,1... | collective-permute-start | bytes 147464 | tf_op jit(solution)/shard_map/ppermute | solution.py:711
  15.7 1.1 %shard_map.137 = (f32[3,56,1152]{2,1,0:T(8,128)S(1)}, f32[144,128]{1,0:T(8,128)S(1)}, bf16[384,128]{1,0:T(8,128)(2,1)S(1)}, bf16[128,128]{1,0:T(8,128)(2,1)S(1)}...) custom-call(f32[56,1152]{1,0:T(8,128)S(1)} %get-tuple-element.77.sta, ...), custom_call_target="tpu_custom_call" | custom-call | flops 20000000 | bytes 3336716 | tf_op jit(solution)/shard_map/pallas_call | solution.py:618
  16.8 2.5 %shard_map.138 = (f32[56,1152]{1,0:T(8,128)S(1)}, f32[56,640]{1,0:T(8,128)S(1)}, f32[96,1152]{1,0:T(8,128)S(1)}, f32[96,256]{1,0:T(8,128)S(1)}) custom-call(f32[56,1152]{1,0:T(8,128)S(1)} %get-tuple-element.77.state.refs_0_, f32[40,1152]{1,0:T(8,128)S(1)} %get-tuple-element.91.refs_1_, f32[96,1152]{1,0:T(8,128)S(1)} %get-tuple-element.92.refs_2_, ...), custom_call_target="tpu_custom_call" | custom-call | flops 20000000 | bytes 3717120 | tf_op jit(solution)/shard_map/pallas_call | solution.py:618
  19.3 0.0 collective-permute-done.upper
  19.3 0.0 collective-permute-done.1.lower
  19.3 2.3 %shard_map.139 = (f32[504,128]{1,0:T(8,128)S(1)}, f32[40,640]{1,0:T(8,128)S(1)}, f32[96,640]{1,0:T(8,128)S(1)}, f32[72,256]{1,0:T(8,128)S(1)}, f32[24,256]{1,0:T(8,128)S(1)}) custom-call(s32[1]{0:T(128)} %bitcast.place, f32[144,256]{1,0:T(8,128)S(1)} %all_gather.12.near, f32[48,256]{1,0:T(8,128)S(1)} %collective-permute-done.upper, ...), custom_call_target="tpu_custom_call" | custom-call | flops 20000000 | bytes 2904068 | tf_op jit(solution)/shard_map/pallas_call | solution.py:618
  21.6 1.9 %all_gather.13.near = f32[144,256]{1,0:T(8,128)S(1)} all-gather(f32[72,256]{1,0:T(8,128)S(1)} %get-tuple-element.104), channel_id=1, replica_groups={{0,1},{2,3},{4,5},{6,7},{8,9},{10,11},{12,13},{14,15},{16,17},{18,19},{..., dimensions={0}, use_global_device_ids=true | all-gather | bytes 221184 | tf_op jit(solution)/shard_map/all_gather | solution.py:704
  23.6 5.4 %collective-permute-start.2 = (f32[48,256]{1,0:T(8,128)S(1)}, f32[48,256]{1,0:T(8,128)S(1)}, u32[]{:S(2)}, u32[]{:S(2)}) collective-permute-start(f32[48,256]{1,0:T(8,128)S(1)} %pad_maximum_fusion.3), channel_id=1, source_target_pairs={{2,5},{5,2},{3,4},{4,3},{6,9},{9,6},{7,8},{8,7},{10,13},{13,10},{1... | collective-permute-start | bytes 147464 | tf_op jit(solution)/shard_map/ppermute | solution.py:710
  29.0 1.9 %collective-permute-start.3 = (f32[48,256]{1,0:T(8,128)S(1)}, f32[48,256]{1,0:T(8,128)S(1)}, u32[]{:S(2)}, u32[]{:S(2)}) collective-permute-start(f32[48,256]{1,0:T(8,128)S(1)} %pad_maximum_fusion.2), channel_id=1, source_target_pairs={{0,3},{3,0},{1,2},{2,1},{4,7},{7,4},{5,6},{6,5},{8,11},{11,8},{9,1... | collective-permute-start | bytes 147464 | tf_op jit(solution)/shard_map/ppermute | solution.py:711
  30.9 2.6 %shard_map.140 = (f32[56,1152]{1,0:T(8,128)S(1)}, f32[56,640]{1,0:T(8,128)S(1)}, f32[96,1152]{1,0:T(8,128)S(1)}, f32[96,256]{1,0:T(8,128)S(1)}) custom-call(f32[56,1152]{1,0:T(8,128)S(1)} %get-tuple-element.109.refs_0_, f32[504,128]{1,0:T(8,128)S(1)} %get-tuple-element.110.refs_1_, bf16[128,128]{1,0:T(8,128)(2,1)S(1)} %get-tuple-element.111.refs_2_.slot_hot, ...), custom_call_target="tpu_custom_call" | custom-call | flops 20000000 | bytes 4204544 | tf_op jit(solution)/shard_map/pallas_call | solution.py:618
  33.6 0.8 %collective-permute-done.2.upper = f32[48,256]{1,0:T(8,128)S(1)} collective-permute-done((f32[48,256]{1,0:T(8,128)S(1)}, f32[48,256]{1,0:T(8,128)S(1)}, u32[]{:S(2)}, u32[]{:S(2)}) %collective-permute-start.2) | collective-permute-done | bytes 49184 | tf_op jit(solution)/shard_map/ppermute | solution.py:710
  34.4 0.0 collective-permute-done.3.lower
  34.4 2.2 %shard_map.141 = (f32[504,128]{1,0:T(8,128)S(1)}, f32[40,640]{1,0:T(8,128)S(1)}, f32[96,640]{1,0:T(8,128)S(1)}, f32[72,256]{1,0:T(8,128)S(1)}, f32[24,256]{1,0:T(8,128)S(1)}) custom-call(s32[1]{0:T(128)} %bitcast.place, f32[144,256]{1,0:T(8,128)S(1)} %all_gather.13.near, f32[48,256]{1,0:T(8,128)S(1)} %collective-permute-done.2.upper, ...), custom_call_target="tpu_custom_call" | custom-call | flops 20000000 | bytes 2904068 | tf_op jit(solution)/shard_map/pallas_call | solution.py:618
  36.7 1.9 %all_gather.14.near = f32[144,256]{1,0:T(8,128)S(1)} all-gather(f32[72,256]{1,0:T(8,128)S(1)} %get-tuple-element.117), channel_id=1, replica_groups={{0,1},{2,3},{4,5},{6,7},{8,9},{10,11},{12,13},{14,15},{16,17},{18,19},{..., dimensions={0}, use_global_device_ids=true | all-gather | bytes 221184 | tf_op jit(solution)/shard_map/all_gather | solution.py:704
  38.6 5.7 %collective-permute-start.4 = (f32[48,256]{1,0:T(8,128)S(1)}, f32[48,256]{1,0:T(8,128)S(1)}, u32[]{:S(2)}, u32[]{:S(2)}) collective-permute-start(f32[48,256]{1,0:T(8,128)S(1)} %pad_maximum_fusion.5), channel_id=1, source_target_pairs={{2,5},{5,2},{3,4},{4,3},{6,9},{9,6},{7,8},{8,7},{10,13},{13,10},{1... | collective-permute-start | bytes 147464 | tf_op jit(solution)/shard_map/ppermute | solution.py:710
  44.4 2.1 %collective-permute-start.5 = (f32[48,256]{1,0:T(8,128)S(1)}, f32[48,256]{1,0:T(8,128)S(1)}, u32[]{:S(2)}, u32[]{:S(2)}) collective-permute-start(f32[48,256]{1,0:T(8,128)S(1)} %pad_maximum_fusion.4), channel_id=1, source_target_pairs={{0,3},{3,0},{1,2},{2,1},{4,7},{7,4},{5,6},{6,5},{8,11},{11,8},{9,1... | collective-permute-start | bytes 147464 | tf_op jit(solution)/shard_map/ppermute | solution.py:711
  46.5 2.6 %shard_map.142 = (f32[56,1152]{1,0:T(8,128)S(1)}, f32[56,640]{1,0:T(8,128)S(1)}, f32[96,1152]{1,0:T(8,128)S(1)}, f32[96,256]{1,0:T(8,128)S(1)}) custom-call(f32[56,1152]{1,0:T(8,128)S(1)} %get-tuple-element.122.refs_0_, f32[504,128]{1,0:T(8,128)S(1)} %get-tuple-element.123.refs_1_, bf16[128,128]{1,0:T(8,128)(2,1)S(1)} %get-tuple-element.111.refs_2_.slot_hot, ...), custom_call_target="tpu_custom_call" | custom-call | flops 20000000 | bytes 4204544 | tf_op jit(solution)/shard_map/pallas_call | solution.py:618
  49.1 0.3 collective-permute-done.4.upper
  49.5 0.3 collective-permute-done.5.lower
  49.8 2.3 %shard_map.143 = (f32[504,128]{1,0:T(8,128)S(1)}, f32[40,640]{1,0:T(8,128)S(1)}, f32[96,640]{1,0:T(8,128)S(1)}, f32[72,256]{1,0:T(8,128)S(1)}, f32[24,256]{1,0:T(8,128)S(1)}) custom-call(s32[1]{0:T(128)} %bitcast.place, f32[144,256]{1,0:T(8,128)S(1)} %all_gather.14.near, f32[48,256]{1,0:T(8,128)S(1)} %collective-permute-done.4.upper, ...), custom_call_target="tpu_custom_call" | custom-call | flops 20000000 | bytes 2904068 | tf_op jit(solution)/shard_map/pallas_call | solution.py:618
  52.0 1.9 %all_gather.15.near = f32[144,256]{1,0:T(8,128)S(1)} all-gather(f32[72,256]{1,0:T(8,128)S(1)} %get-tuple-element.129), channel_id=1, replica_groups={{0,1},{2,3},{4,5},{6,7},{8,9},{10,11},{12,13},{14,15},{16,17},{18,19},{..., dimensions={0}, use_global_device_ids=true | all-gather | bytes 221184 | tf_op jit(solution)/shard_map/all_gather | solution.py:704
  54.0 5.6 %collective-permute-start.6 = (f32[48,256]{1,0:T(8,128)S(1)}, f32[48,256]{1,0:T(8,128)S(1)}, u32[]{:S(2)}, u32[]{:S(2)}) collective-permute-start(f32[48,256]{1,0:T(8,128)S(1)} %pad_maximum_fusion.7), channel_id=1, source_target_pairs={{2,5},{5,2},{3,4},{4,3},{6,9},{9,6},{7,8},{8,7},{10,13},{13,10},{1... | collective-permute-start | bytes 147464 | tf_op jit(solution)/shard_map/ppermute | solution.py:710
  59.6 1.9 %collective-permute-start.7 = (f32[48,256]{1,0:T(8,128)S(1)}, f32[48,256]{1,0:T(8,128)S(1)}, u32[]{:S(2)}, u32[]{:S(2)}) collective-permute-start(f32[48,256]{1,0:T(8,128)S(1)} %pad_maximum_fusion.6), channel_id=1, source_target_pairs={{0,3},{3,0},{1,2},{2,1},{4,7},{7,4},{5,6},{6,5},{8,11},{11,8},{9,1... | collective-permute-start | bytes 147464 | tf_op jit(solution)/shard_map/ppermute | solution.py:711
  61.5 2.3 %shard_map.144.state = f32[56,1152]{1,0:T(8,128)S(1)} custom-call(f32[56,1152]{1,0:T(8,128)S(1)} %get-tuple-element.134.refs_0_, f32[504,128]{1,0:T(8,128)S(1)} %get-tuple-element.135.refs_1_, bf16[128,128]{1,0:T(8,128)(2,1)S(1)} %get-tuple-element.111.refs_2_.slot_hot, f32[40,640]{1,0:T(8,128)S(1)} %get-tuple-element.136.refs_3_, ...), custom_call_target="tpu_custom_call" | custom-call | flops 20000000 | bytes 3520512 | tf_op jit(solution)/shard_map/pallas_call | solution.py:618
  63.9 1.1 %collective-permute-done.6.upper = f32[48,256]{1,0:T(8,128)S(1)} collective-permute-done((f32[48,256]{1,0:T(8,128)S(1)}, f32[48,256]{1,0:T(8,128)S(1)}, u32[]{:S(2)}, u32[]{:S(2)}) %collective-permute-start.6) | collective-permute-done | bytes 49184 | tf_op jit(solution)/shard_map/ppermute | solution.py:710
  64.9 0.1 collective-permute-done.7.lower
  65.0 1.4 %shard_map.145 = f32[9,56,128]{2,1,0:T(8,128)} custom-call(s32[1]{0:T(128)} %bitcast.place, f32[144,256]{1,0:T(8,128)S(1)} %all_gather.15.near, f32[48,256]{1,0:T(8,128)S(1)} %collective-permute-done.6.upper, f32[48,256]{1,0:T(8,128)S(1)} %collective-permute-done.7.lower, f32[144,128]{1,0:T(8,128)S(1)} %get-tuple-element.88.slot_flux, ...), custom_call_target="tpu_custom_call" | custom-call | flops 20000000 | bytes 1490948 | tf_op jit(solution)/shard_map/pallas_call | solution.py:618
  (16 shorter events, 0.1 us)
Async XLA Ops:
  5.2 14.1 %collective-permute-start = (f32[48,256]{1,0:T(8,128)S(1)}, f32[48,256]{1,0:T(8,128)S(1)}, u32[]{:S(2)}, u32[]{:S(2)}) collective-permute-start(f32[48,256]{1,0:T(8,128)S(1)} %pad_maximum_fusion.1), channel_id=1, source_target_pairs={{2,5},{5,2},{3,4},{4,3},{6,9},{9,6},{7,8},{8,7},{10,13},{13,10},{1... | collective-permute-start | bytes 147464 | tf_op jit(solution)/shard_map/ppermute | solution.py:710
  13.7 5.6 %collective-permute-start.1 = (f32[48,256]{1,0:T(8,128)S(1)}, f32[48,256]{1,0:T(8,128)S(1)}, u32[]{:S(2)}, u32[]{:S(2)}) collective-permute-start(f32[48,256]{1,0:T(8,128)S(1)} %pad_maximum_fusion), channel_id=1, source_target_pairs={{0,3},{3,0},{1,2},{2,1},{4,7},{7,4},{5,6},{6,5},{8,11},{11,8},{9,1... | collective-permute-start | bytes 147464 | tf_op jit(solution)/shard_map/ppermute | solution.py:711
  23.6 10.9 %collective-permute-start.2 = (f32[48,256]{1,0:T(8,128)S(1)}, f32[48,256]{1,0:T(8,128)S(1)}, u32[]{:S(2)}, u32[]{:S(2)}) collective-permute-start(f32[48,256]{1,0:T(8,128)S(1)} %pad_maximum_fusion.3), channel_id=1, source_target_pairs={{2,5},{5,2},{3,4},{4,3},{6,9},{9,6},{7,8},{8,7},{10,13},{13,10},{1... | collective-permute-start | bytes 147464 | tf_op jit(solution)/shard_map/ppermute | solution.py:710
  29.0 5.4 %collective-permute-start.3 = (f32[48,256]{1,0:T(8,128)S(1)}, f32[48,256]{1,0:T(8,128)S(1)}, u32[]{:S(2)}, u32[]{:S(2)}) collective-permute-start(f32[48,256]{1,0:T(8,128)S(1)} %pad_maximum_fusion.2), channel_id=1, source_target_pairs={{0,3},{3,0},{1,2},{2,1},{4,7},{7,4},{5,6},{6,5},{8,11},{11,8},{9,1... | collective-permute-start | bytes 147464 | tf_op jit(solution)/shard_map/ppermute | solution.py:711
  38.6 10.8 %collective-permute-start.4 = (f32[48,256]{1,0:T(8,128)S(1)}, f32[48,256]{1,0:T(8,128)S(1)}, u32[]{:S(2)}, u32[]{:S(2)}) collective-permute-start(f32[48,256]{1,0:T(8,128)S(1)} %pad_maximum_fusion.5), channel_id=1, source_target_pairs={{2,5},{5,2},{3,4},{4,3},{6,9},{9,6},{7,8},{8,7},{10,13},{13,10},{1... | collective-permute-start | bytes 147464 | tf_op jit(solution)/shard_map/ppermute | solution.py:710
  44.4 5.4 %collective-permute-start.5 = (f32[48,256]{1,0:T(8,128)S(1)}, f32[48,256]{1,0:T(8,128)S(1)}, u32[]{:S(2)}, u32[]{:S(2)}) collective-permute-start(f32[48,256]{1,0:T(8,128)S(1)} %pad_maximum_fusion.4), channel_id=1, source_target_pairs={{0,3},{3,0},{1,2},{2,1},{4,7},{7,4},{5,6},{6,5},{8,11},{11,8},{9,1... | collective-permute-start | bytes 147464 | tf_op jit(solution)/shard_map/ppermute | solution.py:711
  54.0 10.9 %collective-permute-start.6 = (f32[48,256]{1,0:T(8,128)S(1)}, f32[48,256]{1,0:T(8,128)S(1)}, u32[]{:S(2)}, u32[]{:S(2)}) collective-permute-start(f32[48,256]{1,0:T(8,128)S(1)} %pad_maximum_fusion.7), channel_id=1, source_target_pairs={{2,5},{5,2},{3,4},{4,3},{6,9},{9,6},{7,8},{8,7},{10,13},{13,10},{1... | collective-permute-start | bytes 147464 | tf_op jit(solution)/shard_map/ppermute | solution.py:710
  59.6 5.4 %collective-permute-start.7 = (f32[48,256]{1,0:T(8,128)S(1)}, f32[48,256]{1,0:T(8,128)S(1)}, u32[]{:S(2)}, u32[]{:S(2)}) collective-permute-start(f32[48,256]{1,0:T(8,128)S(1)} %pad_maximum_fusion.6), channel_id=1, source_target_pairs={{0,3},{3,0},{1,2},{2,1},{4,7},{7,4},{5,6},{6,5},{8,11},{11,8},{9,1... | collective-permute-start | bytes 147464 | tf_op jit(solution)/shard_map/ppermute | solution.py:711

commit v7 on v6

--- a/solution.py
+++ b/solution.py
@@ -189,11 +189,13 @@
     return jnp.concatenate(totals, axis=1)
 
 
-def chain_of(first, star, weights, tips, sums, join):
+def chain_of(first, star, weights, tips, sums, join, arrived=None):
     now = first
     chain = [first]
     for start, _, padded, rows in LEVELS[:-1]:
         found = weigh(weights, start, rows, now)
+        if arrived is not None and len(chain) == 1:
+            arrived()
         now = join(
             sums(lambda d, c: found[d * padded : (d + 1) * padded, lanes(c)], star)
         )
@@ -306,7 +308,7 @@
         pltpu.make_async_copy(source, target, ready.at[number])
         for number, (source, target) in enumerate(moves)
     ]
-    for copy in copies:
+    for copy in (copies[1], copies[2], copies[0], *copies[3:]):
         copy.start()
     for copy in copies[1:3]:
         copy.wait()
@@ -314,8 +316,9 @@
     copies[0].wait()
     state = jnp.concatenate([dofs_here[q] for q in range(NQ)], axis=1)
     state_out[...] = state
-    copies[3].wait()
-    chain, end = chain_of(state, star_out, weights_out, tips_out, wide_sums, wide_join)
+    chain, end = chain_of(
+        state, star_out, weights_out, tips_out, wide_sums, wide_join, copies[3].wait
+    )
     first_weights = taylor_weights(0.0, 1.0 / SUBSTEPS)
     integral = integral_of(chain, first_weights)
     for copy in copies[4:first]:
@@ -339,9 +342,9 @@
 
 
 def prepare_kernel(
-    state, tail, source, orientation, flux_other, face_front, face_turn, stiff_vol,
+    source, orientation, flux_other, face_front, face_turn, stiff_vol,
     star, labels, lists,
-    coarse_out, slot_flux_out, slot_code_out, slot_hot_out, lift_out, slot_lift_out,
+    slot_flux_out, slot_code_out, slot_hot_out, lift_out, slot_lift_out,
     narrow_hot_out, slot_narrow_out, star_out, send_out,
     table, fronts, tall, slot_tall, flat,
 ):
@@ -372,15 +375,6 @@
         found = lax.dot_general(chosen, narrow_hot, across, preferred_element_type=F32)
         send_out[0 : PEERS * BOTH, lanes(j)] = jnp.where(half, found, 0.0).astype(BF16)
         send_out[PEERS * BOTH :, lanes(j)] = jnp.where(half, 0.0, found).astype(BF16)
-    chain = [state[...]]
-    start = 0
-    for _, _, padded, _ in LEVELS:
-        chain.append(tail[start : start + padded, :])
-        start += padded
-    for step in range(1, SUBSTEPS):
-        coarse_out[step - 1] = integral_of(
-            chain, taylor_weights(step / SUBSTEPS, (step + 1) / SUBSTEPS)
-        )
     row = iota((LANES, LANES), 0)
     peer = (row >= BOTH).astype(jnp.int32) + (row >= 2 * BOTH).astype(jnp.int32)
     peer = peer + (row >= 3 * BOTH).astype(jnp.int32)
@@ -449,9 +443,9 @@
         state, low, faces, *rest = refs
         state, low, faces = state[...], low[...], faces[...]
     else:
-        state, by_slot, slot_hot, low, faces, coarse_faces, *rest = refs
+        state, by_slot, slot_hot, low, faces, coarse_low, coarse_faces, *rest = refs
     star, flux_self, flux_other, source, orientation, lift, *rest = rest
-    coarse, weights, lists, narrow_hot, labels, *rest = rest
+    begin, tail, weights, lists, narrow_hot, labels, *rest = rest
     out, *rest = rest
     if step > 0:
         state = state[...] + by_elements(by_slot[...], slot_hot[...])
@@ -473,11 +467,20 @@
         wide = jnp.concatenate(wide, axis=1)[:, 0:COLS]
         fine = labels[...] == 1
         fine = jnp.concatenate([fine] * NQ, axis=1)
-        low = jnp.where(fine, wide[0:VPAD], coarse[step - 1, 0:VPAD, :])
+        low = jnp.where(fine, wide[0:VPAD], coarse_low[...])
         faces = jnp.where(fine, wide[VPAD:both], coarse_faces[...])
     if step + 1 < SUBSTEPS:
-        narrow_out, next_faces_out, next_sent_out, stack = rest
-        next_faces = weigh(weights, BACK, OWN, coarse[step])
+        narrow_out, next_low_out, next_faces_out, next_sent_out, stack = rest
+        chain = [begin[...]]
+        start = 0
+        for _, _, padded, _ in LEVELS:
+            chain.append(tail[start : start + padded, :])
+            start += padded
+        coarse = integral_of(
+            chain, taylor_weights((step + 1) / SUBSTEPS, (step + 2) / SUBSTEPS)
+        )
+        next_low_out[...] = coarse[0:VPAD]
+        next_faces = weigh(weights, BACK, OWN, coarse)
         next_faces_out[...] = next_faces
         _, inner = list_rows()
         hot = jnp.concatenate(
@@ -683,9 +686,9 @@
     halved = lambda *shape: jax.ShapeDtypeStruct(shape, BF16)
     prepared = call(
         prepare_kernel,
-        (state, tail, source, orientation, flux_other, front, turn, vol, star, labels, lists),
+        (source, orientation, flux_other, front, turn, vol, star, labels, lists),
         [
-            floats(SUBSTEPS - 1, NB, COLS), floats(16 * NQ, LANES), halved(SLOT_REM, LANES),
+            floats(16 * NQ, LANES), halved(SLOT_REM, LANES),
             halved(LANES, LANES), floats(NB, DEEP_PAD), halved(2 * PART, 2 * SLOT_REM),
             halved(LANES, LANES), halved(LANES, LANES), floats(TWOS * STAR_ROWS, LANES),
             halved(2 * PEERS * BOTH, FACES),
@@ -695,10 +698,10 @@
             (NQ * STAR_ROWS, LANES),
         ],
     )
-    coarse, slot_flux, slot_code, slot_hot, lift, slot_lift = prepared[:6]
-    narrow_hot, slot_narrow, narrow_star, send_hot = prepared[6:]
+    slot_flux, slot_code, slot_hot, lift, slot_lift = prepared[:5]
+    narrow_hot, slot_narrow, narrow_star, send_hot = prepared[5:]
     fixed = (star, flux_self, flux_other, source, orientation, lift)
-    fixed += (coarse, weights, lists, narrow_hot, labels)
+    fixed += (state, tail, weights, lists, narrow_hot, labels)
     known = (state, low, faces)
     for step in range(SUBSTEPS):
         near = lax.all_gather(pair, "dom", axis_index_groups=pairs, tiled=True)
@@ -709,7 +712,8 @@
         upper = jnp.concatenate([cross, passed], axis=0)
         upper = lax.ppermute(upper, "dom", swaps(count, 1))
         lower = lax.ppermute(lower, "dom", swaps(count, 0))
-        ahead = [floats(NB, NARROW), floats(OWN, COLS), floats(PEERS * BOTH, WIDTH)]
+        ahead = [floats(NB, NARROW), floats(VPAD, COLS), floats(OWN, COLS)]
+        ahead += [floats(PEERS * BOTH, WIDTH)]
         state, *made = call(
             functools.partial(local_kernel, step=step),
             known + fixed,
@@ -718,7 +722,7 @@
         )
         received = (place, near, upper, lower, slot_flux, slot_code, slot_lift)
         if step + 1 < SUBSTEPS:
-            narrow, coarse_faces, coarse_sent = made
+            narrow, coarse_low, coarse_faces, coarse_sent = made
             by_slot, low, faces, pair, cross = call(
                 next_kernel,
                 received
@@ -728,7 +732,7 @@
                 [],
                 scalars=1,
             )
-            known = (state, by_slot, slot_hot, low, faces, coarse_faces)
+            known = (state, by_slot, slot_hot, low, faces, coarse_low, coarse_faces)
     (result,) = call(
         last_kernel, received + (state, slot_hot), [floats(NQ, NB, LANES)], [], scalars=1
     )

time: 67.3 us -> 67.2 us (level)
  transfers between devices with their start and end apart: 8 -> 8, of which waited for: 5 -> 6; matrix products, arithmetic and copies ran while one was open for 0% -> 0% of each run, Pallas kernels for 17% -> 17%
where the time goes in v7:
time: 67.2 us; the launch traced here: 66.3 us
  starting transfers between devices  33.2 us (49%)
  Pallas kernels  22.5 us (33%)
  blocking collectives  7.67 us (11%)
  waiting for transfers between devices  2.61 us (4%)
    ppermute x4, starting transfers between devices, local(): upper = lax.ppermute(upper, 'dom', swaps(count, 1))  25.3 us
    pallas_call x10, Pallas kernels, call(): pl.pallas_call(kernel, in_specs=[smem] * scalars + [given] * (len(args) -...  22.5 us
    ppermute x4, starting transfers between devices, local(): lower = lax.ppermute(lower, 'dom', swaps(count, 0))  7.86 us
    all_gather x4, blocking collectives, local(): near = lax.all_gather(pair, 'dom', axis_index_groups=pairs, tiled=True)  7.67 us
    ppermute x4, waiting for transfers between devices, local(): upper = lax.ppermute(upper, 'dom', swaps(count, 1))  2.14 us
  transfers between devices with their start and end apart: 8, of which 6 were waited for; matrix products, arithmetic and copies ran while one was open for 0% of the time, Pallas kernels for 17%

profile of v7, /device:TPU:384, one launch (start us, length us, event | category | flops | bytes accessed | tf_op | source)
XLA Modules:
  0.0 66.3 jit_solution(10150706577497580874)
XLA Ops:
  0.0 3.2 %shard_map.136 = (f32[56,1152]{1,0:T(8,128)S(1)}, f32[40,1152]{1,0:T(8,128)S(1)}, f32[96,1152]{1,0:T(8,128)S(1)}, f32[96,1152]{1,0:T(8,128)S(1)}, f32[72,256]{1,...) custom-call(s32[1]{0:T(128)} %bitcast.place, ...), custom_call_target="tpu_custom_call" | custom-call | flops 20000000 | bytes 3279612 | tf_op jit(solution)/shard_map/pallas_call | solution.py:621
  3.2 1.9 %all_gather.12.near = f32[144,256]{1,0:T(8,128)S(1)} all-gather(f32[72,256]{1,0:T(8,128)S(1)} %get-tuple-element.74), channel_id=1, replica_groups={{0,1},{2,3},{4,5},{6,7},{8,9},{10,11},{12,13},{14,15},{16,17},{18,19},{..., dimensions={0}, use_global_device_ids=true | all-gather | bytes 221184 | tf_op jit(solution)/shard_map/all_gather | solution.py:707
  5.1 8.5 %collective-permute-start = (f32[48,256]{1,0:T(8,128)S(1)}, f32[48,256]{1,0:T(8,128)S(1)}, u32[]{:S(2)}, u32[]{:S(2)}) collective-permute-start(f32[48,256]{1,0:T(8,128)S(1)} %pad_maximum_fusion.1), channel_id=1, source_target_pairs={{2,5},{5,2},{3,4},{4,3},{6,9},{9,6},{7,8},{8,7},{10,13},{13,10},{1... | collective-permute-start | bytes 147464 | tf_op jit(solution)/shard_map/ppermute | solution.py:713
  13.7 1.9 %collective-permute-start.1 = (f32[48,256]{1,0:T(8,128)S(1)}, f32[48,256]{1,0:T(8,128)S(1)}, u32[]{:S(2)}, u32[]{:S(2)}) collective-permute-start(f32[48,256]{1,0:T(8,128)S(1)} %pad_maximum_fusion), channel_id=1, source_target_pairs={{0,3},{3,0},{1,2},{2,1},{4,7},{7,4},{5,6},{6,5},{8,11},{11,8},{9,1... | collective-permute-start | bytes 147464 | tf_op jit(solution)/shard_map/ppermute | solution.py:714
  15.6 1.0 %shard_map.137 = (f32[144,128]{1,0:T(8,128)S(1)}, bf16[384,128]{1,0:T(8,128)(2,1)S(1)}, bf16[128,128]{1,0:T(8,128)(2,1)S(1)}, f32[56,512]{1,0:T(8,128)S(1)}, bf1...) custom-call(s32[4,128]{1,0:T(4,128)S(1)} %get-tuple-element.79.sourc, ...), custom_call_target="tpu_custom_call" | custom-call | flops 20000000 | bytes 1862156 | tf_op jit(solution)/shard_map/pallas_call | solution.py:621
  16.6 2.5 %shard_map.138 = (f32[56,1152]{1,0:T(8,128)S(1)}, f32[56,640]{1,0:T(8,128)S(1)}, f32[40,1152]{1,0:T(8,128)S(1)}, f32[96,1152]{1,0:T(8,128)S(1)}, f32[96,256]{1,0:T(8,128)S(1)}) custom-call(f32[56,1152]{1,0:T(8,128)S(1)} %get-tuple-element.91.refs_0_.refs_9_.refs_13_, f32[40,1152]{1,0:T(8,128)S(1)} %get-tuple-element.92.refs_1_, ...), custom_call_target="tpu_custom_call" | custom-call | flops 20000000 | bytes 3827712 | tf_op jit(solution)/shard_map/pallas_call | solution.py:621
  19.1 0.0 collective-permute-done.upper
  19.1 0.0 collective-permute-done.1.lower
  19.1 2.3 %shard_map.139 = (f32[504,128]{1,0:T(8,128)S(1)}, f32[40,640]{1,0:T(8,128)S(1)}, f32[96,640]{1,0:T(8,128)S(1)}, f32[72,256]{1,0:T(8,128)S(1)}, f32[24,256]{1,0:T(8,128)S(1)}) custom-call(s32[1]{0:T(128)} %bitcast.place, f32[144,256]{1,0:T(8,128)S(1)} %all_gather.12.near, f32[48,256]{1,0:T(8,128)S(1)} %collective-permute-done.upper, ...), custom_call_target="tpu_custom_call" | custom-call | flops 20000000 | bytes 2904068 | tf_op jit(solution)/shard_map/pallas_call | solution.py:621
  21.4 1.9 %all_gather.13.near = f32[144,256]{1,0:T(8,128)S(1)} all-gather(f32[72,256]{1,0:T(8,128)S(1)} %get-tuple-element.105), channel_id=1, replica_groups={{0,1},{2,3},{4,5},{6,7},{8,9},{10,11},{12,13},{14,15},{16,17},{18,19},{..., dimensions={0}, use_global_device_ids=true | all-gather | bytes 221184 | tf_op jit(solution)/shard_map/all_gather | solution.py:707
  23.4 5.6 %collective-permute-start.2 = (f32[48,256]{1,0:T(8,128)S(1)}, f32[48,256]{1,0:T(8,128)S(1)}, u32[]{:S(2)}, u32[]{:S(2)}) collective-permute-start(f32[48,256]{1,0:T(8,128)S(1)} %pad_maximum_fusion.3), channel_id=1, source_target_pairs={{2,5},{5,2},{3,4},{4,3},{6,9},{9,6},{7,8},{8,7},{10,13},{13,10},{1... | collective-permute-start | bytes 147464 | tf_op jit(solution)/shard_map/ppermute | solution.py:713
  28.9 1.9 %collective-permute-start.3 = (f32[48,256]{1,0:T(8,128)S(1)}, f32[48,256]{1,0:T(8,128)S(1)}, u32[]{:S(2)}, u32[]{:S(2)}) collective-permute-start(f32[48,256]{1,0:T(8,128)S(1)} %pad_maximum_fusion.2), channel_id=1, source_target_pairs={{0,3},{3,0},{1,2},{2,1},{4,7},{7,4},{5,6},{6,5},{8,11},{11,8},{9,1... | collective-permute-start | bytes 147464 | tf_op jit(solution)/shard_map/ppermute | solution.py:714
  30.9 2.7 %shard_map.140 = (f32[56,1152]{1,0:T(8,128)S(1)}, f32[56,640]{1,0:T(8,128)S(1)}, f32[40,1152]{1,0:T(8,128)S(1)}, f32[96,1152]{1,0:T(8,128)S(1)}, f32[96,256]{1,0:T(8,128)S(1)}) custom-call(f32[56,1152]{1,0:T(8,128)S(1)} %get-tuple-element.110.refs_0_, f32[504,128]{1,0:T(8,128)S(1)} %get-tuple-element.111.refs_1_, ...), custom_call_target="tpu_custom_call" | custom-call | flops 20000000 | bytes 4499456 | tf_op jit(solution)/shard_map/pallas_call | solution.py:621
  33.5 0.7 %collective-permute-done.2.upper = f32[48,256]{1,0:T(8,128)S(1)} collective-permute-done((f32[48,256]{1,0:T(8,128)S(1)}, f32[48,256]{1,0:T(8,128)S(1)}, u32[]{:S(2)}, u32[]{:S(2)}) %collective-permute-start.2) | collective-permute-done | bytes 49184 | tf_op jit(solution)/shard_map/ppermute | solution.py:713
  34.2 0.1 collective-permute-done.3.lower
  34.4 2.3 %shard_map.141 = (f32[504,128]{1,0:T(8,128)S(1)}, f32[40,640]{1,0:T(8,128)S(1)}, f32[96,640]{1,0:T(8,128)S(1)}, f32[72,256]{1,0:T(8,128)S(1)}, f32[24,256]{1,0:T(8,128)S(1)}) custom-call(s32[1]{0:T(128)} %bitcast.place, f32[144,256]{1,0:T(8,128)S(1)} %all_gather.13.near, f32[48,256]{1,0:T(8,128)S(1)} %collective-permute-done.2.upper, ...), custom_call_target="tpu_custom_call" | custom-call | flops 20000000 | bytes 2904068 | tf_op jit(solution)/shard_map/pallas_call | solution.py:621
  36.6 1.9 %all_gather.14.near = f32[144,256]{1,0:T(8,128)S(1)} all-gather(f32[72,256]{1,0:T(8,128)S(1)} %get-tuple-element.119), channel_id=1, replica_groups={{0,1},{2,3},{4,5},{6,7},{8,9},{10,11},{12,13},{14,15},{16,17},{18,19},{..., dimensions={0}, use_global_device_ids=true | all-gather | bytes 221184 | tf_op jit(solution)/shard_map/all_gather | solution.py:707
  38.6 5.6 %collective-permute-start.4 = (f32[48,256]{1,0:T(8,128)S(1)}, f32[48,256]{1,0:T(8,128)S(1)}, u32[]{:S(2)}, u32[]{:S(2)}) collective-permute-start(f32[48,256]{1,0:T(8,128)S(1)} %pad_maximum_fusion.5), channel_id=1, source_target_pairs={{2,5},{5,2},{3,4},{4,3},{6,9},{9,6},{7,8},{8,7},{10,13},{13,10},{1... | collective-permute-start | bytes 147464 | tf_op jit(solution)/shard_map/ppermute | solution.py:713
  44.2 2.1 %collective-permute-start.5 = (f32[48,256]{1,0:T(8,128)S(1)}, f32[48,256]{1,0:T(8,128)S(1)}, u32[]{:S(2)}, u32[]{:S(2)}) collective-permute-start(f32[48,256]{1,0:T(8,128)S(1)} %pad_maximum_fusion.4), channel_id=1, source_target_pairs={{0,3},{3,0},{1,2},{2,1},{4,7},{7,4},{5,6},{6,5},{8,11},{11,8},{9,1... | collective-permute-start | bytes 147464 | tf_op jit(solution)/shard_map/ppermute | solution.py:714
  46.3 2.7 %shard_map.142 = (f32[56,1152]{1,0:T(8,128)S(1)}, f32[56,640]{1,0:T(8,128)S(1)}, f32[40,1152]{1,0:T(8,128)S(1)}, f32[96,1152]{1,0:T(8,128)S(1)}, f32[96,256]{1,0:T(8,128)S(1)}) custom-call(f32[56,1152]{1,0:T(8,128)S(1)} %get-tuple-element.124.refs_0_, f32[504,128]{1,0:T(8,128)S(1)} %get-tuple-element.125.refs_1_, ...), custom_call_target="tpu_custom_call" | custom-call | flops 20000000 | bytes 4499456 | tf_op jit(solution)/shard_map/pallas_call | solution.py:621
  49.0 0.5 collective-permute-done.4.upper
  49.5 0.1 collective-permute-done.5.lower
  49.6 2.2 %shard_map.143 = (f32[504,128]{1,0:T(8,128)S(1)}, f32[40,640]{1,0:T(8,128)S(1)}, f32[96,640]{1,0:T(8,128)S(1)}, f32[72,256]{1,0:T(8,128)S(1)}, f32[24,256]{1,0:T(8,128)S(1)}) custom-call(s32[1]{0:T(128)} %bitcast.place, f32[144,256]{1,0:T(8,128)S(1)} %all_gather.14.near, f32[48,256]{1,0:T(8,128)S(1)} %collective-permute-done.4.upper, ...), custom_call_target="tpu_custom_call" | custom-call | flops 20000000 | bytes 2904068 | tf_op jit(solution)/shard_map/pallas_call | solution.py:621
  51.9 1.9 %all_gather.15.near = f32[144,256]{1,0:T(8,128)S(1)} all-gather(f32[72,256]{1,0:T(8,128)S(1)} %get-tuple-element.132), channel_id=1, replica_groups={{0,1},{2,3},{4,5},{6,7},{8,9},{10,11},{12,13},{14,15},{16,17},{18,19},{..., dimensions={0}, use_global_device_ids=true | all-gather | bytes 221184 | tf_op jit(solution)/shard_map/all_gather | solution.py:707
  53.8 5.6 %collective-permute-start.6 = (f32[48,256]{1,0:T(8,128)S(1)}, f32[48,256]{1,0:T(8,128)S(1)}, u32[]{:S(2)}, u32[]{:S(2)}) collective-permute-start(f32[48,256]{1,0:T(8,128)S(1)} %pad_maximum_fusion.7), channel_id=1, source_target_pairs={{2,5},{5,2},{3,4},{4,3},{6,9},{9,6},{7,8},{8,7},{10,13},{13,10},{1... | collective-permute-start | bytes 147464 | tf_op jit(solution)/shard_map/ppermute | solution.py:713
  59.4 1.9 %collective-permute-start.7 = (f32[48,256]{1,0:T(8,128)S(1)}, f32[48,256]{1,0:T(8,128)S(1)}, u32[]{:S(2)}, u32[]{:S(2)}) collective-permute-start(f32[48,256]{1,0:T(8,128)S(1)} %pad_maximum_fusion.6), channel_id=1, source_target_pairs={{0,3},{3,0},{1,2},{2,1},{4,7},{7,4},{5,6},{6,5},{8,11},{11,8},{9,1... | collective-permute-start | bytes 147464 | tf_op jit(solution)/shard_map/ppermute | solution.py:714
  61.4 2.3 %shard_map.144.state = f32[56,1152]{1,0:T(8,128)S(1)} custom-call(f32[56,1152]{1,0:T(8,128)S(1)} %get-tuple-element.137.refs_0_, f32[504,128]{1,0:T(8,128)S(1)} %get-tuple-element.138.refs_1_, bf16[128,128]{1,0:T(8,128)(2,1)S(1)} %get-tuple-element.112.refs_2_.slot_hot, f32[40,640]{1,0:T(8,128)S(1)} %get-tuple-element.139.refs_3_, ...), custom_call_target="tpu_custom_call" | custom-call | flops 20000000 | bytes 3631104 | tf_op jit(solution)/shard_map/pallas_call | solution.py:621
  63.7 1.0 %collective-permute-done.6.upper = f32[48,256]{1,0:T(8,128)S(1)} collective-permute-done((f32[48,256]{1,0:T(8,128)S(1)}, f32[48,256]{1,0:T(8,128)S(1)}, u32[]{:S(2)}, u32[]{:S(2)}) %collective-permute-start.6) | collective-permute-done | bytes 49184 | tf_op jit(solution)/shard_map/ppermute | solution.py:713
  64.7 0.2 collective-permute-done.7.lower
  64.9 1.4 %shard_map.145 = f32[9,56,128]{2,1,0:T(8,128)} custom-call(s32[1]{0:T(128)} %bitcast.place, f32[144,256]{1,0:T(8,128)S(1)} %all_gather.15.near, f32[48,256]{1,0:T(8,128)S(1)} %collective-permute-done.6.upper, f32[48,256]{1,0:T(8,128)S(1)} %collective-permute-done.7.lower, f32[144,128]{1,0:T(8,128)S(1)} %get-tuple-element.88.slot_flux, ...), custom_call_target="tpu_custom_call" | custom-call | flops 20000000 | bytes 1490948 | tf_op jit(solution)/shard_map/pallas_call | solution.py:621
  (16 shorter events, 0.1 us)
Async XLA Ops:
  5.1 14.0 %collective-permute-start = (f32[48,256]{1,0:T(8,128)S(1)}, f32[48,256]{1,0:T(8,128)S(1)}, u32[]{:S(2)}, u32[]{:S(2)}) collective-permute-start(f32[48,256]{1,0:T(8,128)S(1)} %pad_maximum_fusion.1), channel_id=1, source_target_pairs={{2,5},{5,2},{3,4},{4,3},{6,9},{9,6},{7,8},{8,7},{10,13},{13,10},{1... | collective-permute-start | bytes 147464 | tf_op jit(solution)/shard_map/ppermute | solution.py:713
  13.7 5.5 %collective-permute-start.1 = (f32[48,256]{1,0:T(8,128)S(1)}, f32[48,256]{1,0:T(8,128)S(1)}, u32[]{:S(2)}, u32[]{:S(2)}) collective-permute-start(f32[48,256]{1,0:T(8,128)S(1)} %pad_maximum_fusion), channel_id=1, source_target_pairs={{0,3},{3,0},{1,2},{2,1},{4,7},{7,4},{5,6},{6,5},{8,11},{11,8},{9,1... | collective-permute-start | bytes 147464 | tf_op jit(solution)/shard_map/ppermute | solution.py:714
  23.4 10.9 %collective-permute-start.2 = (f32[48,256]{1,0:T(8,128)S(1)}, f32[48,256]{1,0:T(8,128)S(1)}, u32[]{:S(2)}, u32[]{:S(2)}) collective-permute-start(f32[48,256]{1,0:T(8,128)S(1)} %pad_maximum_fusion.3), channel_id=1, source_target_pairs={{2,5},{5,2},{3,4},{4,3},{6,9},{9,6},{7,8},{8,7},{10,13},{13,10},{1... | collective-permute-start | bytes 147464 | tf_op jit(solution)/shard_map/ppermute | solution.py:713
  28.9 5.4 %collective-permute-start.3 = (f32[48,256]{1,0:T(8,128)S(1)}, f32[48,256]{1,0:T(8,128)S(1)}, u32[]{:S(2)}, u32[]{:S(2)}) collective-permute-start(f32[48,256]{1,0:T(8,128)S(1)} %pad_maximum_fusion.2), channel_id=1, source_target_pairs={{0,3},{3,0},{1,2},{2,1},{4,7},{7,4},{5,6},{6,5},{8,11},{11,8},{9,1... | collective-permute-start | bytes 147464 | tf_op jit(solution)/shard_map/ppermute | solution.py:714
  38.6 10.9 %collective-permute-start.4 = (f32[48,256]{1,0:T(8,128)S(1)}, f32[48,256]{1,0:T(8,128)S(1)}, u32[]{:S(2)}, u32[]{:S(2)}) collective-permute-start(f32[48,256]{1,0:T(8,128)S(1)} %pad_maximum_fusion.5), channel_id=1, source_target_pairs={{2,5},{5,2},{3,4},{4,3},{6,9},{9,6},{7,8},{8,7},{10,13},{13,10},{1... | collective-permute-start | bytes 147464 | tf_op jit(solution)/shard_map/ppermute | solution.py:713
  44.2 5.4 %collective-permute-start.5 = (f32[48,256]{1,0:T(8,128)S(1)}, f32[48,256]{1,0:T(8,128)S(1)}, u32[]{:S(2)}, u32[]{:S(2)}) collective-permute-start(f32[48,256]{1,0:T(8,128)S(1)} %pad_maximum_fusion.4), channel_id=1, source_target_pairs={{0,3},{3,0},{1,2},{2,1},{4,7},{7,4},{5,6},{6,5},{8,11},{11,8},{9,1... | collective-permute-start | bytes 147464 | tf_op jit(solution)/shard_map/ppermute | solution.py:714
  53.8 10.8 %collective-permute-start.6 = (f32[48,256]{1,0:T(8,128)S(1)}, f32[48,256]{1,0:T(8,128)S(1)}, u32[]{:S(2)}, u32[]{:S(2)}) collective-permute-start(f32[48,256]{1,0:T(8,128)S(1)} %pad_maximum_fusion.7), channel_id=1, source_target_pairs={{2,5},{5,2},{3,4},{4,3},{6,9},{9,6},{7,8},{8,7},{10,13},{13,10},{1... | collective-permute-start | bytes 147464 | tf_op jit(solution)/shard_map/ppermute | solution.py:713
  59.4 5.4 %collective-permute-start.7 = (f32[48,256]{1,0:T(8,128)S(1)}, f32[48,256]{1,0:T(8,128)S(1)}, u32[]{:S(2)}, u32[]{:S(2)}) collective-permute-start(f32[48,256]{1,0:T(8,128)S(1)} %pad_maximum_fusion.6), channel_id=1, source_target_pairs={{0,3},{3,0},{1,2},{2,1},{4,7},{7,4},{5,6},{6,5},{8,11},{11,8},{9,1... | collective-permute-start | bytes 147464 | tf_op jit(solution)/shard_map/ppermute | solution.py:714

commit v8 on v6

--- a/solution.py
+++ b/solution.py
@@ -32,6 +32,8 @@
 LEVELS = [(0, 35, 40, 128), (128, 20, 24, 80), (208, 10, 16, 48), (256, 4, 8, 32), (288, 1, 8, 32)]
 BACK = 320
 CHAIN_ROWS = BACK + OWN
+DEPTH_3 = 10
+TIP_ROWS = 24 + OWN
 TAIL = 96
 PART = 64
 TWOS = 5
@@ -153,6 +155,10 @@
         column = turned[0:8, 8 * d : 8 * d + 1]
         tips[8 * d : 8 * d + 8, :] = jnp.broadcast_to(column, (8, LANES))
     tips[24 : 24 + OWN, :] = jnp.broadcast_to(once[BACK : BACK + OWN, 0:1], (OWN, LANES))
+    start = LEVELS[3][0]
+    for b in range(DEPTH_3):
+        column = jnp.broadcast_to(once[start : start + 24, b : b + 1], (24, LANES))
+        tips[TIP_ROWS + 24 * b : TIP_ROWS + 24 * (b + 1), :] = column
 
 
 def weigh(weights, start, rows, value):
@@ -189,11 +195,26 @@
     return jnp.concatenate(totals, axis=1)
 
 
+def by_rows(value, tips):
+    columns = []
+    for c in range(value.shape[1] // LANES):
+        total = None
+        for b in range(DEPTH_3):
+            column = tips[TIP_ROWS + 24 * b : TIP_ROWS + 24 * (b + 1), :]
+            term = column * value[b : b + 1, lanes(c)]
+            total = term if total is None else total + term
+        columns.append(total)
+    return jnp.concatenate(columns, axis=1)
+
+
 def chain_of(first, star, weights, tips, sums, join):
     now = first
     chain = [first]
-    for start, _, padded, rows in LEVELS[:-1]:
-        found = weigh(weights, start, rows, now)
+    for level, (start, _, padded, rows) in enumerate(LEVELS[:-1]):
+        if level == 3 and sums is narrow_sums:
+            found = by_rows(now, tips)
+        else:
+            found = weigh(weights, start, rows, now)
         now = join(
             sums(lambda d, c: found[d * padded : (d + 1) * padded, lanes(c)], star)
         )
@@ -669,7 +690,7 @@
         [floats(NB, COLS), floats(VPAD, COLS), floats(TAIL, COLS)]
         + sent_shapes
         + [jax.ShapeDtypeStruct((CHAIN_ROWS, 2 * LANES), BF16)]
-        + [floats(24 + OWN, LANES), like(star), like(labels)]
+        + [floats(TIP_ROWS + 24 * DEPTH_3, LANES), like(star), like(labels)]
         + [jax.ShapeDtypeStruct((PEERS * BOTH, LANES), jnp.int32)]
         + [like(item) for item in later],
         [(CHAIN_ROWS, LANES), (NQ, NB, LANES), stiff_time.shape, back.shape, (16, LANES)]

time: 67.3 us -> 67 us (level)
  no operation moved by 1% of the time
where the time goes in v8:
time: 67 us; the launch traced here: 66.1 us
  starting transfers between devices  33.2 us (50%)
  Pallas kernels  22.3 us (33%)
  blocking collectives  7.68 us (11%)
  waiting for transfers between devices  2.68 us (4%)
    ppermute x4, starting transfers between devices, local(): upper = lax.ppermute(upper, 'dom', swaps(count, 1))  25.3 us
    pallas_call x10, Pallas kernels, call(): pl.pallas_call(kernel, in_specs=[smem] * scalars + [given] * (len(args) -...  22.3 us
    ppermute x4, starting transfers between devices, local(): lower = lax.ppermute(lower, 'dom', swaps(count, 0))  7.86 us
    all_gather x4, blocking collectives, local(): near = lax.all_gather(pair, 'dom', axis_index_groups=pairs, tiled=True)  7.68 us
    ppermute x4, waiting for transfers between devices, local(): upper = lax.ppermute(upper, 'dom', swaps(count, 1))  2.16 us
  transfers between devices with their start and end apart: 8, of which 5 were waited for; matrix products, arithmetic and copies ran while one was open for 0% of the time, Pallas kernels for 17%

profile of v8, /device:TPU:384, one launch (start us, length us, event | category | flops | bytes accessed | tf_op | source)
XLA Modules:
  0.0 66.1 jit_solution(15436548706008286002)
XLA Ops:
  0.0 3.3 %shard_map.136 = (f32[56,1152]{1,0:T(8,128)S(1)}, f32[40,1152]{1,0:T(8,128)S(1)}, f32[96,1152]{1,0:T(8,128)S(1)}, f32[96,1152]{1,0:T(8,128)S(1)}, f32[72,256]{1,...) custom-call(s32[1]{0:T(128)} %bitcast.place, ...), custom_call_target="tpu_custom_call" | custom-call | flops 20000000 | bytes 3402492 | tf_op jit(solution)/shard_map/pallas_call | solution.py:639
  3.3 1.9 %all_gather.12.near = f32[144,256]{1,0:T(8,128)S(1)} all-gather(f32[72,256]{1,0:T(8,128)S(1)} %get-tuple-element.72), channel_id=1, replica_groups={{0,1},{2,3},{4,5},{6,7},{8,9},{10,11},{12,13},{14,15},{16,17},{18,19},{..., dimensions={0}, use_global_device_ids=true | all-gather | bytes 221184 | tf_op jit(solution)/shard_map/all_gather | solution.py:725
  5.2 8.5 %collective-permute-start = (f32[48,256]{1,0:T(8,128)S(1)}, f32[48,256]{1,0:T(8,128)S(1)}, u32[]{:S(2)}, u32[]{:S(2)}) collective-permute-start(f32[48,256]{1,0:T(8,128)S(1)} %pad_maximum_fusion.1), channel_id=1, source_target_pairs={{2,5},{5,2},{3,4},{4,3},{6,9},{9,6},{7,8},{8,7},{10,13},{13,10},{1... | collective-permute-start | bytes 147464 | tf_op jit(solution)/shard_map/ppermute | solution.py:731
  13.7 1.9 %collective-permute-start.1 = (f32[48,256]{1,0:T(8,128)S(1)}, f32[48,256]{1,0:T(8,128)S(1)}, u32[]{:S(2)}, u32[]{:S(2)}) collective-permute-start(f32[48,256]{1,0:T(8,128)S(1)} %pad_maximum_fusion), channel_id=1, source_target_pairs={{0,3},{3,0},{1,2},{2,1},{4,7},{7,4},{5,6},{6,5},{8,11},{11,8},{9,1... | collective-permute-start | bytes 147464 | tf_op jit(solution)/shard_map/ppermute | solution.py:732
  15.7 1.1 %shard_map.137 = (f32[3,56,1152]{2,1,0:T(8,128)S(1)}, f32[144,128]{1,0:T(8,128)S(1)}, bf16[384,128]{1,0:T(8,128)(2,1)S(1)}, bf16[128,128]{1,0:T(8,128)(2,1)S(1)}...) custom-call(f32[56,1152]{1,0:T(8,128)S(1)} %get-tuple-element.77.sta, ...), custom_call_target="tpu_custom_call" | custom-call | flops 20000000 | bytes 3336716 | tf_op jit(solution)/shard_map/pallas_call | solution.py:639
  16.8 2.5 %shard_map.138 = (f32[56,1152]{1,0:T(8,128)S(1)}, f32[56,640]{1,0:T(8,128)S(1)}, f32[96,1152]{1,0:T(8,128)S(1)}, f32[96,256]{1,0:T(8,128)S(1)}) custom-call(f32[56,1152]{1,0:T(8,128)S(1)} %get-tuple-element.77.state.refs_0_, f32[40,1152]{1,0:T(8,128)S(1)} %get-tuple-element.91.refs_1_, f32[96,1152]{1,0:T(8,128)S(1)} %get-tuple-element.92.refs_2_, ...), custom_call_target="tpu_custom_call" | custom-call | flops 20000000 | bytes 3717120 | tf_op jit(solution)/shard_map/pallas_call | solution.py:639
  19.3 0.0 collective-permute-done.upper
  19.3 0.0 collective-permute-done.1.lower
  19.3 2.1 %shard_map.139 = (f32[504,128]{1,0:T(8,128)S(1)}, f32[40,640]{1,0:T(8,128)S(1)}, f32[96,640]{1,0:T(8,128)S(1)}, f32[72,256]{1,0:T(8,128)S(1)}, f32[24,256]{1,0:T(8,128)S(1)}) custom-call(s32[1]{0:T(128)} %bitcast.place, f32[144,256]{1,0:T(8,128)S(1)} %all_gather.12.near, f32[48,256]{1,0:T(8,128)S(1)} %collective-permute-done.upper, ...), custom_call_target="tpu_custom_call" | custom-call | flops 20000000 | bytes 3026948 | tf_op jit(solution)/shard_map/pallas_call | solution.py:639
  21.5 1.9 %all_gather.13.near = f32[144,256]{1,0:T(8,128)S(1)} all-gather(f32[72,256]{1,0:T(8,128)S(1)} %get-tuple-element.104), channel_id=1, replica_groups={{0,1},{2,3},{4,5},{6,7},{8,9},{10,11},{12,13},{14,15},{16,17},{18,19},{..., dimensions={0}, use_global_device_ids=true | all-gather | bytes 221184 | tf_op jit(solution)/shard_map/all_gather | solution.py:725
  23.5 5.4 %collective-permute-start.2 = (f32[48,256]{1,0:T(8,128)S(1)}, f32[48,256]{1,0:T(8,128)S(1)}, u32[]{:S(2)}, u32[]{:S(2)}) collective-permute-start(f32[48,256]{1,0:T(8,128)S(1)} %pad_maximum_fusion.3), channel_id=1, source_target_pairs={{2,5},{5,2},{3,4},{4,3},{6,9},{9,6},{7,8},{8,7},{10,13},{13,10},{1... | collective-permute-start | bytes 147464 | tf_op jit(solution)/shard_map/ppermute | solution.py:731
  28.9 1.9 %collective-permute-start.3 = (f32[48,256]{1,0:T(8,128)S(1)}, f32[48,256]{1,0:T(8,128)S(1)}, u32[]{:S(2)}, u32[]{:S(2)}) collective-permute-start(f32[48,256]{1,0:T(8,128)S(1)} %pad_maximum_fusion.2), channel_id=1, source_target_pairs={{0,3},{3,0},{1,2},{2,1},{4,7},{7,4},{5,6},{6,5},{8,11},{11,8},{9,1... | collective-permute-start | bytes 147464 | tf_op jit(solution)/shard_map/ppermute | solution.py:732
  30.8 2.6 %shard_map.140 = (f32[56,1152]{1,0:T(8,128)S(1)}, f32[56,640]{1,0:T(8,128)S(1)}, f32[96,1152]{1,0:T(8,128)S(1)}, f32[96,256]{1,0:T(8,128)S(1)}) custom-call(f32[56,1152]{1,0:T(8,128)S(1)} %get-tuple-element.109.refs_0_, f32[504,128]{1,0:T(8,128)S(1)} %get-tuple-element.110.refs_1_, bf16[128,128]{1,0:T(8,128)(2,1)S(1)} %get-tuple-element.111.refs_2_.slot_hot, ...), custom_call_target="tpu_custom_call" | custom-call | flops 20000000 | bytes 4204544 | tf_op jit(solution)/shard_map/pallas_call | solution.py:639
  33.4 0.9 %collective-permute-done.2.upper = f32[48,256]{1,0:T(8,128)S(1)} collective-permute-done((f32[48,256]{1,0:T(8,128)S(1)}, f32[48,256]{1,0:T(8,128)S(1)}, u32[]{:S(2)}, u32[]{:S(2)}) %collective-permute-start.2) | collective-permute-done | bytes 49184 | tf_op jit(solution)/shard_map/ppermute | solution.py:731
  34.3 0.0 collective-permute-done.3.lower
  34.3 2.1 %shard_map.141 = (f32[504,128]{1,0:T(8,128)S(1)}, f32[40,640]{1,0:T(8,128)S(1)}, f32[96,640]{1,0:T(8,128)S(1)}, f32[72,256]{1,0:T(8,128)S(1)}, f32[24,256]{1,0:T(8,128)S(1)}) custom-call(s32[1]{0:T(128)} %bitcast.place, f32[144,256]{1,0:T(8,128)S(1)} %all_gather.13.near, f32[48,256]{1,0:T(8,128)S(1)} %collective-permute-done.2.upper, ...), custom_call_target="tpu_custom_call" | custom-call | flops 20000000 | bytes 3026948 | tf_op jit(solution)/shard_map/pallas_call | solution.py:639
  36.4 1.9 %all_gather.14.near = f32[144,256]{1,0:T(8,128)S(1)} all-gather(f32[72,256]{1,0:T(8,128)S(1)} %get-tuple-element.117), channel_id=1, replica_groups={{0,1},{2,3},{4,5},{6,7},{8,9},{10,11},{12,13},{14,15},{16,17},{18,19},{..., dimensions={0}, use_global_device_ids=true | all-gather | bytes 221184 | tf_op jit(solution)/shard_map/all_gather | solution.py:725
  38.4 5.8 %collective-permute-start.4 = (f32[48,256]{1,0:T(8,128)S(1)}, f32[48,256]{1,0:T(8,128)S(1)}, u32[]{:S(2)}, u32[]{:S(2)}) collective-permute-start(f32[48,256]{1,0:T(8,128)S(1)} %pad_maximum_fusion.5), channel_id=1, source_target_pairs={{2,5},{5,2},{3,4},{4,3},{6,9},{9,6},{7,8},{8,7},{10,13},{13,10},{1... | collective-permute-start | bytes 147464 | tf_op jit(solution)/shard_map/ppermute | solution.py:731
  44.2 2.1 %collective-permute-start.5 = (f32[48,256]{1,0:T(8,128)S(1)}, f32[48,256]{1,0:T(8,128)S(1)}, u32[]{:S(2)}, u32[]{:S(2)}) collective-permute-start(f32[48,256]{1,0:T(8,128)S(1)} %pad_maximum_fusion.4), channel_id=1, source_target_pairs={{0,3},{3,0},{1,2},{2,1},{4,7},{7,4},{5,6},{6,5},{8,11},{11,8},{9,1... | collective-permute-start | bytes 147464 | tf_op jit(solution)/shard_map/ppermute | solution.py:732
  46.3 2.6 %shard_map.142 = (f32[56,1152]{1,0:T(8,128)S(1)}, f32[56,640]{1,0:T(8,128)S(1)}, f32[96,1152]{1,0:T(8,128)S(1)}, f32[96,256]{1,0:T(8,128)S(1)}) custom-call(f32[56,1152]{1,0:T(8,128)S(1)} %get-tuple-element.122.refs_0_, f32[504,128]{1,0:T(8,128)S(1)} %get-tuple-element.123.refs_1_, bf16[128,128]{1,0:T(8,128)(2,1)S(1)} %get-tuple-element.111.refs_2_.slot_hot, ...), custom_call_target="tpu_custom_call" | custom-call | flops 20000000 | bytes 4204544 | tf_op jit(solution)/shard_map/pallas_call | solution.py:639
  48.9 0.3 collective-permute-done.4.upper
  49.2 0.3 collective-permute-done.5.lower
  49.6 2.1 %shard_map.143 = (f32[504,128]{1,0:T(8,128)S(1)}, f32[40,640]{1,0:T(8,128)S(1)}, f32[96,640]{1,0:T(8,128)S(1)}, f32[72,256]{1,0:T(8,128)S(1)}, f32[24,256]{1,0:T(8,128)S(1)}) custom-call(s32[1]{0:T(128)} %bitcast.place, f32[144,256]{1,0:T(8,128)S(1)} %all_gather.14.near, f32[48,256]{1,0:T(8,128)S(1)} %collective-permute-done.4.upper, ...), custom_call_target="tpu_custom_call" | custom-call | flops 20000000 | bytes 3026948 | tf_op jit(solution)/shard_map/pallas_call | solution.py:639
  51.7 1.9 %all_gather.15.near = f32[144,256]{1,0:T(8,128)S(1)} all-gather(f32[72,256]{1,0:T(8,128)S(1)} %get-tuple-element.129), channel_id=1, replica_groups={{0,1},{2,3},{4,5},{6,7},{8,9},{10,11},{12,13},{14,15},{16,17},{18,19},{..., dimensions={0}, use_global_device_ids=true | all-gather | bytes 221184 | tf_op jit(solution)/shard_map/all_gather | solution.py:725
  53.6 5.6 %collective-permute-start.6 = (f32[48,256]{1,0:T(8,128)S(1)}, f32[48,256]{1,0:T(8,128)S(1)}, u32[]{:S(2)}, u32[]{:S(2)}) collective-permute-start(f32[48,256]{1,0:T(8,128)S(1)} %pad_maximum_fusion.7), channel_id=1, source_target_pairs={{2,5},{5,2},{3,4},{4,3},{6,9},{9,6},{7,8},{8,7},{10,13},{13,10},{1... | collective-permute-start | bytes 147464 | tf_op jit(solution)/shard_map/ppermute | solution.py:731
  59.3 1.9 %collective-permute-start.7 = (f32[48,256]{1,0:T(8,128)S(1)}, f32[48,256]{1,0:T(8,128)S(1)}, u32[]{:S(2)}, u32[]{:S(2)}) collective-permute-start(f32[48,256]{1,0:T(8,128)S(1)} %pad_maximum_fusion.6), channel_id=1, source_target_pairs={{0,3},{3,0},{1,2},{2,1},{4,7},{7,4},{5,6},{6,5},{8,11},{11,8},{9,1... | collective-permute-start | bytes 147464 | tf_op jit(solution)/shard_map/ppermute | solution.py:732
  61.2 2.3 %shard_map.144.state = f32[56,1152]{1,0:T(8,128)S(1)} custom-call(f32[56,1152]{1,0:T(8,128)S(1)} %get-tuple-element.134.refs_0_, f32[504,128]{1,0:T(8,128)S(1)} %get-tuple-element.135.refs_1_, bf16[128,128]{1,0:T(8,128)(2,1)S(1)} %get-tuple-element.111.refs_2_.slot_hot, f32[40,640]{1,0:T(8,128)S(1)} %get-tuple-element.136.refs_3_, ...), custom_call_target="tpu_custom_call" | custom-call | flops 20000000 | bytes 3520512 | tf_op jit(solution)/shard_map/pallas_call | solution.py:639
  63.5 1.0 %collective-permute-done.6.upper = f32[48,256]{1,0:T(8,128)S(1)} collective-permute-done((f32[48,256]{1,0:T(8,128)S(1)}, f32[48,256]{1,0:T(8,128)S(1)}, u32[]{:S(2)}, u32[]{:S(2)}) %collective-permute-start.6) | collective-permute-done | bytes 49184 | tf_op jit(solution)/shard_map/ppermute | solution.py:731
  64.5 0.2 collective-permute-done.7.lower
  64.7 1.4 %shard_map.145 = f32[9,56,128]{2,1,0:T(8,128)} custom-call(s32[1]{0:T(128)} %bitcast.place, f32[144,256]{1,0:T(8,128)S(1)} %all_gather.15.near, f32[48,256]{1,0:T(8,128)S(1)} %collective-permute-done.6.upper, f32[48,256]{1,0:T(8,128)S(1)} %collective-permute-done.7.lower, f32[144,128]{1,0:T(8,128)S(1)} %get-tuple-element.88.slot_flux, ...), custom_call_target="tpu_custom_call" | custom-call | flops 20000000 | bytes 1490948 | tf_op jit(solution)/shard_map/pallas_call | solution.py:639
  (16 shorter events, 0.1 us)
Async XLA Ops:
  5.2 14.1 %collective-permute-start = (f32[48,256]{1,0:T(8,128)S(1)}, f32[48,256]{1,0:T(8,128)S(1)}, u32[]{:S(2)}, u32[]{:S(2)}) collective-permute-start(f32[48,256]{1,0:T(8,128)S(1)} %pad_maximum_fusion.1), channel_id=1, source_target_pairs={{2,5},{5,2},{3,4},{4,3},{6,9},{9,6},{7,8},{8,7},{10,13},{13,10},{1... | collective-permute-start | bytes 147464 | tf_op jit(solution)/shard_map/ppermute | solution.py:731
  13.7 5.6 %collective-permute-start.1 = (f32[48,256]{1,0:T(8,128)S(1)}, f32[48,256]{1,0:T(8,128)S(1)}, u32[]{:S(2)}, u32[]{:S(2)}) collective-permute-start(f32[48,256]{1,0:T(8,128)S(1)} %pad_maximum_fusion), channel_id=1, source_target_pairs={{0,3},{3,0},{1,2},{2,1},{4,7},{7,4},{5,6},{6,5},{8,11},{11,8},{9,1... | collective-permute-start | bytes 147464 | tf_op jit(solution)/shard_map/ppermute | solution.py:732
  23.5 10.9 %collective-permute-start.2 = (f32[48,256]{1,0:T(8,128)S(1)}, f32[48,256]{1,0:T(8,128)S(1)}, u32[]{:S(2)}, u32[]{:S(2)}) collective-permute-start(f32[48,256]{1,0:T(8,128)S(1)} %pad_maximum_fusion.3), channel_id=1, source_target_pairs={{2,5},{5,2},{3,4},{4,3},{6,9},{9,6},{7,8},{8,7},{10,13},{13,10},{1... | collective-permute-start | bytes 147464 | tf_op jit(solution)/shard_map/ppermute | solution.py:731
  28.9 5.4 %collective-permute-start.3 = (f32[48,256]{1,0:T(8,128)S(1)}, f32[48,256]{1,0:T(8,128)S(1)}, u32[]{:S(2)}, u32[]{:S(2)}) collective-permute-start(f32[48,256]{1,0:T(8,128)S(1)} %pad_maximum_fusion.2), channel_id=1, source_target_pairs={{0,3},{3,0},{1,2},{2,1},{4,7},{7,4},{5,6},{6,5},{8,11},{11,8},{9,1... | collective-permute-start | bytes 147464 | tf_op jit(solution)/shard_map/ppermute | solution.py:732
  38.4 10.9 %collective-permute-start.4 = (f32[48,256]{1,0:T(8,128)S(1)}, f32[48,256]{1,0:T(8,128)S(1)}, u32[]{:S(2)}, u32[]{:S(2)}) collective-permute-start(f32[48,256]{1,0:T(8,128)S(1)} %pad_maximum_fusion.5), channel_id=1, source_target_pairs={{2,5},{5,2},{3,4},{4,3},{6,9},{9,6},{7,8},{8,7},{10,13},{13,10},{1... | collective-permute-start | bytes 147464 | tf_op jit(solution)/shard_map/ppermute | solution.py:731
  44.2 5.4 %collective-permute-start.5 = (f32[48,256]{1,0:T(8,128)S(1)}, f32[48,256]{1,0:T(8,128)S(1)}, u32[]{:S(2)}, u32[]{:S(2)}) collective-permute-start(f32[48,256]{1,0:T(8,128)S(1)} %pad_maximum_fusion.4), channel_id=1, source_target_pairs={{0,3},{3,0},{1,2},{2,1},{4,7},{7,4},{5,6},{6,5},{8,11},{11,8},{9,1... | collective-permute-start | bytes 147464 | tf_op jit(solution)/shard_map/ppermute | solution.py:732
  53.6 10.8 %collective-permute-start.6 = (f32[48,256]{1,0:T(8,128)S(1)}, f32[48,256]{1,0:T(8,128)S(1)}, u32[]{:S(2)}, u32[]{:S(2)}) collective-permute-start(f32[48,256]{1,0:T(8,128)S(1)} %pad_maximum_fusion.7), channel_id=1, source_target_pairs={{2,5},{5,2},{3,4},{4,3},{6,9},{9,6},{7,8},{8,7},{10,13},{13,10},{1... | collective-permute-start | bytes 147464 | tf_op jit(solution)/shard_map/ppermute | solution.py:731
  59.3 5.4 %collective-permute-start.7 = (f32[48,256]{1,0:T(8,128)S(1)}, f32[48,256]{1,0:T(8,128)S(1)}, u32[]{:S(2)}, u32[]{:S(2)}) collective-permute-start(f32[48,256]{1,0:T(8,128)S(1)} %pad_maximum_fusion.6), channel_id=1, source_target_pairs={{0,3},{3,0},{1,2},{2,1},{4,7},{7,4},{5,6},{6,5},{8,11},{11,8},{9,1... | collective-permute-start | bytes 147464 | tf_op jit(solution)/shard_map/ppermute | solution.py:732

commit v9 on v8

--- a/solution.py
+++ b/solution.py
@@ -211,7 +211,7 @@
     now = first
     chain = [first]
     for level, (start, _, padded, rows) in enumerate(LEVELS[:-1]):
-        if level == 3 and sums is narrow_sums:
+        if level == 3:
             found = by_rows(now, tips)
         else:
             found = weigh(weights, start, rows, now)

time: 67 us -> 66.9 us (level)
  no operation moved by 1% of the time
where the time goes in v9:
time: 66.9 us; the launch traced here: 66.1 us
  starting transfers between devices  33.2 us (50%)
  Pallas kernels  22.2 us (33%)
  blocking collectives  7.68 us (11%)
  waiting for transfers between devices  2.68 us (4%)
    ppermute x4, starting transfers between devices, local(): upper = lax.ppermute(upper, 'dom', swaps(count, 1))  25.3 us
    pallas_call x10, Pallas kernels, call(): pl.pallas_call(kernel, in_specs=[smem] * scalars + [given] * (len(args) -...  22.2 us
    ppermute x4, starting transfers between devices, local(): lower = lax.ppermute(lower, 'dom', swaps(count, 0))  7.86 us
    all_gather x4, blocking collectives, local(): near = lax.all_gather(pair, 'dom', axis_index_groups=pairs, tiled=True)  7.68 us
    ppermute x4, waiting for transfers between devices, local(): upper = lax.ppermute(upper, 'dom', swaps(count, 1))  2.16 us
  transfers between devices with their start and end apart: 8, of which 5 were waited for; matrix products, arithmetic and copies ran while one was open for 0% of the time, Pallas kernels for 17%

profile of v9, /device:TPU:384, one launch (start us, length us, event | category | flops | bytes accessed | tf_op | source)
XLA Modules:
  0.0 66.1 jit_solution(2377160632972924435)
XLA Ops:
  0.0 3.2 %shard_map.136 = (f32[56,1152]{1,0:T(8,128)S(1)}, f32[40,1152]{1,0:T(8,128)S(1)}, f32[96,1152]{1,0:T(8,128)S(1)}, f32[96,1152]{1,0:T(8,128)S(1)}, f32[72,256]{1,...) custom-call(s32[1]{0:T(128)} %bitcast.place, ...), custom_call_target="tpu_custom_call" | custom-call | flops 20000000 | bytes 3402492 | tf_op jit(solution)/shard_map/pallas_call | solution.py:639
  3.2 1.9 %all_gather.12.near = f32[144,256]{1,0:T(8,128)S(1)} all-gather(f32[72,256]{1,0:T(8,128)S(1)} %get-tuple-element.72), channel_id=1, replica_groups={{0,1},{2,3},{4,5},{6,7},{8,9},{10,11},{12,13},{14,15},{16,17},{18,19},{..., dimensions={0}, use_global_device_ids=true | all-gather | bytes 221184 | tf_op jit(solution)/shard_map/all_gather | solution.py:725
  5.2 8.5 %collective-permute-start = (f32[48,256]{1,0:T(8,128)S(1)}, f32[48,256]{1,0:T(8,128)S(1)}, u32[]{:S(2)}, u32[]{:S(2)}) collective-permute-start(f32[48,256]{1,0:T(8,128)S(1)} %pad_maximum_fusion.1), channel_id=1, source_target_pairs={{2,5},{5,2},{3,4},{4,3},{6,9},{9,6},{7,8},{8,7},{10,13},{13,10},{1... | collective-permute-start | bytes 147464 | tf_op jit(solution)/shard_map/ppermute | solution.py:731
  13.7 1.9 %collective-permute-start.1 = (f32[48,256]{1,0:T(8,128)S(1)}, f32[48,256]{1,0:T(8,128)S(1)}, u32[]{:S(2)}, u32[]{:S(2)}) collective-permute-start(f32[48,256]{1,0:T(8,128)S(1)} %pad_maximum_fusion), channel_id=1, source_target_pairs={{0,3},{3,0},{1,2},{2,1},{4,7},{7,4},{5,6},{6,5},{8,11},{11,8},{9,1... | collective-permute-start | bytes 147464 | tf_op jit(solution)/shard_map/ppermute | solution.py:732
  15.6 1.1 %shard_map.137 = (f32[3,56,1152]{2,1,0:T(8,128)S(1)}, f32[144,128]{1,0:T(8,128)S(1)}, bf16[384,128]{1,0:T(8,128)(2,1)S(1)}, bf16[128,128]{1,0:T(8,128)(2,1)S(1)}...) custom-call(f32[56,1152]{1,0:T(8,128)S(1)} %get-tuple-element.77.sta, ...), custom_call_target="tpu_custom_call" | custom-call | flops 20000000 | bytes 3336716 | tf_op jit(solution)/shard_map/pallas_call | solution.py:639
  16.8 2.5 %shard_map.138 = (f32[56,1152]{1,0:T(8,128)S(1)}, f32[56,640]{1,0:T(8,128)S(1)}, f32[96,1152]{1,0:T(8,128)S(1)}, f32[96,256]{1,0:T(8,128)S(1)}) custom-call(f32[56,1152]{1,0:T(8,128)S(1)} %get-tuple-element.77.state.refs_0_, f32[40,1152]{1,0:T(8,128)S(1)} %get-tuple-element.91.refs_1_, f32[96,1152]{1,0:T(8,128)S(1)} %get-tuple-element.92.refs_2_, ...), custom_call_target="tpu_custom_call" | custom-call | flops 20000000 | bytes 3717120 | tf_op jit(solution)/shard_map/pallas_call | solution.py:639
  19.3 0.0 collective-permute-done.upper
  19.3 0.0 collective-permute-done.1.lower
  19.3 2.1 %shard_map.139 = (f32[504,128]{1,0:T(8,128)S(1)}, f32[40,640]{1,0:T(8,128)S(1)}, f32[96,640]{1,0:T(8,128)S(1)}, f32[72,256]{1,0:T(8,128)S(1)}, f32[24,256]{1,0:T(8,128)S(1)}) custom-call(s32[1]{0:T(128)} %bitcast.place, f32[144,256]{1,0:T(8,128)S(1)} %all_gather.12.near, f32[48,256]{1,0:T(8,128)S(1)} %collective-permute-done.upper, ...), custom_call_target="tpu_custom_call" | custom-call | flops 20000000 | bytes 3026948 | tf_op jit(solution)/shard_map/pallas_call | solution.py:639
  21.5 1.9 %all_gather.13.near = f32[144,256]{1,0:T(8,128)S(1)} all-gather(f32[72,256]{1,0:T(8,128)S(1)} %get-tuple-element.104), channel_id=1, replica_groups={{0,1},{2,3},{4,5},{6,7},{8,9},{10,11},{12,13},{14,15},{16,17},{18,19},{..., dimensions={0}, use_global_device_ids=true | all-gather | bytes 221184 | tf_op jit(solution)/shard_map/all_gather | solution.py:725
  23.4 5.4 %collective-permute-start.2 = (f32[48,256]{1,0:T(8,128)S(1)}, f32[48,256]{1,0:T(8,128)S(1)}, u32[]{:S(2)}, u32[]{:S(2)}) collective-permute-start(f32[48,256]{1,0:T(8,128)S(1)} %pad_maximum_fusion.3), channel_id=1, source_target_pairs={{2,5},{5,2},{3,4},{4,3},{6,9},{9,6},{7,8},{8,7},{10,13},{13,10},{1... | collective-permute-start | bytes 147464 | tf_op jit(solution)/shard_map/ppermute | solution.py:731
  28.8 1.9 %collective-permute-start.3 = (f32[48,256]{1,0:T(8,128)S(1)}, f32[48,256]{1,0:T(8,128)S(1)}, u32[]{:S(2)}, u32[]{:S(2)}) collective-permute-start(f32[48,256]{1,0:T(8,128)S(1)} %pad_maximum_fusion.2), channel_id=1, source_target_pairs={{0,3},{3,0},{1,2},{2,1},{4,7},{7,4},{5,6},{6,5},{8,11},{11,8},{9,1... | collective-permute-start | bytes 147464 | tf_op jit(solution)/shard_map/ppermute | solution.py:732
  30.8 2.6 %shard_map.140 = (f32[56,1152]{1,0:T(8,128)S(1)}, f32[56,640]{1,0:T(8,128)S(1)}, f32[96,1152]{1,0:T(8,128)S(1)}, f32[96,256]{1,0:T(8,128)S(1)}) custom-call(f32[56,1152]{1,0:T(8,128)S(1)} %get-tuple-element.109.refs_0_, f32[504,128]{1,0:T(8,128)S(1)} %get-tuple-element.110.refs_1_, bf16[128,128]{1,0:T(8,128)(2,1)S(1)} %get-tuple-element.111.refs_2_.slot_hot, ...), custom_call_target="tpu_custom_call" | custom-call | flops 20000000 | bytes 4204544 | tf_op jit(solution)/shard_map/pallas_call | solution.py:639
  33.4 0.9 %collective-permute-done.2.upper = f32[48,256]{1,0:T(8,128)S(1)} collective-permute-done((f32[48,256]{1,0:T(8,128)S(1)}, f32[48,256]{1,0:T(8,128)S(1)}, u32[]{:S(2)}, u32[]{:S(2)}) %collective-permute-start.2) | collective-permute-done | bytes 49184 | tf_op jit(solution)/shard_map/ppermute | solution.py:731
  34.3 0.0 collective-permute-done.3.lower
  34.3 2.1 %shard_map.141 = (f32[504,128]{1,0:T(8,128)S(1)}, f32[40,640]{1,0:T(8,128)S(1)}, f32[96,640]{1,0:T(8,128)S(1)}, f32[72,256]{1,0:T(8,128)S(1)}, f32[24,256]{1,0:T(8,128)S(1)}) custom-call(s32[1]{0:T(128)} %bitcast.place, f32[144,256]{1,0:T(8,128)S(1)} %all_gather.13.near, f32[48,256]{1,0:T(8,128)S(1)} %collective-permute-done.2.upper, ...), custom_call_target="tpu_custom_call" | custom-call | flops 20000000 | bytes 3026948 | tf_op jit(solution)/shard_map/pallas_call | solution.py:639
  36.4 1.9 %all_gather.14.near = f32[144,256]{1,0:T(8,128)S(1)} all-gather(f32[72,256]{1,0:T(8,128)S(1)} %get-tuple-element.117), channel_id=1, replica_groups={{0,1},{2,3},{4,5},{6,7},{8,9},{10,11},{12,13},{14,15},{16,17},{18,19},{..., dimensions={0}, use_global_device_ids=true | all-gather | bytes 221184 | tf_op jit(solution)/shard_map/all_gather | solution.py:725
  38.4 5.8 %collective-permute-start.4 = (f32[48,256]{1,0:T(8,128)S(1)}, f32[48,256]{1,0:T(8,128)S(1)}, u32[]{:S(2)}, u32[]{:S(2)}) collective-permute-start(f32[48,256]{1,0:T(8,128)S(1)} %pad_maximum_fusion.5), channel_id=1, source_target_pairs={{2,5},{5,2},{3,4},{4,3},{6,9},{9,6},{7,8},{8,7},{10,13},{13,10},{1... | collective-permute-start | bytes 147464 | tf_op jit(solution)/shard_map/ppermute | solution.py:731
  44.1 2.1 %collective-permute-start.5 = (f32[48,256]{1,0:T(8,128)S(1)}, f32[48,256]{1,0:T(8,128)S(1)}, u32[]{:S(2)}, u32[]{:S(2)}) collective-permute-start(f32[48,256]{1,0:T(8,128)S(1)} %pad_maximum_fusion.4), channel_id=1, source_target_pairs={{0,3},{3,0},{1,2},{2,1},{4,7},{7,4},{5,6},{6,5},{8,11},{11,8},{9,1... | collective-permute-start | bytes 147464 | tf_op jit(solution)/shard_map/ppermute | solution.py:732
  46.2 2.6 %shard_map.142 = (f32[56,1152]{1,0:T(8,128)S(1)}, f32[56,640]{1,0:T(8,128)S(1)}, f32[96,1152]{1,0:T(8,128)S(1)}, f32[96,256]{1,0:T(8,128)S(1)}) custom-call(f32[56,1152]{1,0:T(8,128)S(1)} %get-tuple-element.122.refs_0_, f32[504,128]{1,0:T(8,128)S(1)} %get-tuple-element.123.refs_1_, bf16[128,128]{1,0:T(8,128)(2,1)S(1)} %get-tuple-element.111.refs_2_.slot_hot, ...), custom_call_target="tpu_custom_call" | custom-call | flops 20000000 | bytes 4204544 | tf_op jit(solution)/shard_map/pallas_call | solution.py:639
  48.9 0.3 collective-permute-done.4.upper
  49.2 0.3 collective-permute-done.5.lower
  49.5 2.1 %shard_map.143 = (f32[504,128]{1,0:T(8,128)S(1)}, f32[40,640]{1,0:T(8,128)S(1)}, f32[96,640]{1,0:T(8,128)S(1)}, f32[72,256]{1,0:T(8,128)S(1)}, f32[24,256]{1,0:T(8,128)S(1)}) custom-call(s32[1]{0:T(128)} %bitcast.place, f32[144,256]{1,0:T(8,128)S(1)} %all_gather.14.near, f32[48,256]{1,0:T(8,128)S(1)} %collective-permute-done.4.upper, ...), custom_call_target="tpu_custom_call" | custom-call | flops 20000000 | bytes 3026948 | tf_op jit(solution)/shard_map/pallas_call | solution.py:639
  51.7 1.9 %all_gather.15.near = f32[144,256]{1,0:T(8,128)S(1)} all-gather(f32[72,256]{1,0:T(8,128)S(1)} %get-tuple-element.129), channel_id=1, replica_groups={{0,1},{2,3},{4,5},{6,7},{8,9},{10,11},{12,13},{14,15},{16,17},{18,19},{..., dimensions={0}, use_global_device_ids=true | all-gather | bytes 221184 | tf_op jit(solution)/shard_map/all_gather | solution.py:725
  53.6 5.6 %collective-permute-start.6 = (f32[48,256]{1,0:T(8,128)S(1)}, f32[48,256]{1,0:T(8,128)S(1)}, u32[]{:S(2)}, u32[]{:S(2)}) collective-permute-start(f32[48,256]{1,0:T(8,128)S(1)} %pad_maximum_fusion.7), channel_id=1, source_target_pairs={{2,5},{5,2},{3,4},{4,3},{6,9},{9,6},{7,8},{8,7},{10,13},{13,10},{1... | collective-permute-start | bytes 147464 | tf_op jit(solution)/shard_map/ppermute | solution.py:731
  59.2 1.9 %collective-permute-start.7 = (f32[48,256]{1,0:T(8,128)S(1)}, f32[48,256]{1,0:T(8,128)S(1)}, u32[]{:S(2)}, u32[]{:S(2)}) collective-permute-start(f32[48,256]{1,0:T(8,128)S(1)} %pad_maximum_fusion.6), channel_id=1, source_target_pairs={{0,3},{3,0},{1,2},{2,1},{4,7},{7,4},{5,6},{6,5},{8,11},{11,8},{9,1... | collective-permute-start | bytes 147464 | tf_op jit(solution)/shard_map/ppermute | solution.py:732
  61.2 2.3 %shard_map.144.state = f32[56,1152]{1,0:T(8,128)S(1)} custom-call(f32[56,1152]{1,0:T(8,128)S(1)} %get-tuple-element.134.refs_0_, f32[504,128]{1,0:T(8,128)S(1)} %get-tuple-element.135.refs_1_, bf16[128,128]{1,0:T(8,128)(2,1)S(1)} %get-tuple-element.111.refs_2_.slot_hot, f32[40,640]{1,0:T(8,128)S(1)} %get-tuple-element.136.refs_3_, ...), custom_call_target="tpu_custom_call" | custom-call | flops 20000000 | bytes 3520512 | tf_op jit(solution)/shard_map/pallas_call | solution.py:639
  63.5 1.0 %collective-permute-done.6.upper = f32[48,256]{1,0:T(8,128)S(1)} collective-permute-done((f32[48,256]{1,0:T(8,128)S(1)}, f32[48,256]{1,0:T(8,128)S(1)}, u32[]{:S(2)}, u32[]{:S(2)}) %collective-permute-start.6) | collective-permute-done | bytes 49184 | tf_op jit(solution)/shard_map/ppermute | solution.py:731
  64.5 0.2 collective-permute-done.7.lower
  64.6 1.4 %shard_map.145 = f32[9,56,128]{2,1,0:T(8,128)} custom-call(s32[1]{0:T(128)} %bitcast.place, f32[144,256]{1,0:T(8,128)S(1)} %all_gather.15.near, f32[48,256]{1,0:T(8,128)S(1)} %collective-permute-done.6.upper, f32[48,256]{1,0:T(8,128)S(1)} %collective-permute-done.7.lower, f32[144,128]{1,0:T(8,128)S(1)} %get-tuple-element.88.slot_flux, ...), custom_call_target="tpu_custom_call" | custom-call | flops 20000000 | bytes 1490948 | tf_op jit(solution)/shard_map/pallas_call | solution.py:639
  (16 shorter events, 0.1 us)
Async XLA Ops:
  5.2 14.1 %collective-permute-start = (f32[48,256]{1,0:T(8,128)S(1)}, f32[48,256]{1,0:T(8,128)S(1)}, u32[]{:S(2)}, u32[]{:S(2)}) collective-permute-start(f32[48,256]{1,0:T(8,128)S(1)} %pad_maximum_fusion.1), channel_id=1, source_target_pairs={{2,5},{5,2},{3,4},{4,3},{6,9},{9,6},{7,8},{8,7},{10,13},{13,10},{1... | collective-permute-start | bytes 147464 | tf_op jit(solution)/shard_map/ppermute | solution.py:731
  13.7 5.6 %collective-permute-start.1 = (f32[48,256]{1,0:T(8,128)S(1)}, f32[48,256]{1,0:T(8,128)S(1)}, u32[]{:S(2)}, u32[]{:S(2)}) collective-permute-start(f32[48,256]{1,0:T(8,128)S(1)} %pad_maximum_fusion), channel_id=1, source_target_pairs={{0,3},{3,0},{1,2},{2,1},{4,7},{7,4},{5,6},{6,5},{8,11},{11,8},{9,1... | collective-permute-start | bytes 147464 | tf_op jit(solution)/shard_map/ppermute | solution.py:732
  23.4 10.9 %collective-permute-start.2 = (f32[48,256]{1,0:T(8,128)S(1)}, f32[48,256]{1,0:T(8,128)S(1)}, u32[]{:S(2)}, u32[]{:S(2)}) collective-permute-start(f32[48,256]{1,0:T(8,128)S(1)} %pad_maximum_fusion.3), channel_id=1, source_target_pairs={{2,5},{5,2},{3,4},{4,3},{6,9},{9,6},{7,8},{8,7},{10,13},{13,10},{1... | collective-permute-start | bytes 147464 | tf_op jit(solution)/shard_map/ppermute | solution.py:731
  28.8 5.4 %collective-permute-start.3 = (f32[48,256]{1,0:T(8,128)S(1)}, f32[48,256]{1,0:T(8,128)S(1)}, u32[]{:S(2)}, u32[]{:S(2)}) collective-permute-start(f32[48,256]{1,0:T(8,128)S(1)} %pad_maximum_fusion.2), channel_id=1, source_target_pairs={{0,3},{3,0},{1,2},{2,1},{4,7},{7,4},{5,6},{6,5},{8,11},{11,8},{9,1... | collective-permute-start | bytes 147464 | tf_op jit(solution)/shard_map/ppermute | solution.py:732
  38.4 10.9 %collective-permute-start.4 = (f32[48,256]{1,0:T(8,128)S(1)}, f32[48,256]{1,0:T(8,128)S(1)}, u32[]{:S(2)}, u32[]{:S(2)}) collective-permute-start(f32[48,256]{1,0:T(8,128)S(1)} %pad_maximum_fusion.5), channel_id=1, source_target_pairs={{2,5},{5,2},{3,4},{4,3},{6,9},{9,6},{7,8},{8,7},{10,13},{13,10},{1... | collective-permute-start | bytes 147464 | tf_op jit(solution)/shard_map/ppermute | solution.py:731
  44.1 5.4 %collective-permute-start.5 = (f32[48,256]{1,0:T(8,128)S(1)}, f32[48,256]{1,0:T(8,128)S(1)}, u32[]{:S(2)}, u32[]{:S(2)}) collective-permute-start(f32[48,256]{1,0:T(8,128)S(1)} %pad_maximum_fusion.4), channel_id=1, source_target_pairs={{0,3},{3,0},{1,2},{2,1},{4,7},{7,4},{5,6},{6,5},{8,11},{11,8},{9,1... | collective-permute-start | bytes 147464 | tf_op jit(solution)/shard_map/ppermute | solution.py:732
  53.6 10.8 %collective-permute-start.6 = (f32[48,256]{1,0:T(8,128)S(1)}, f32[48,256]{1,0:T(8,128)S(1)}, u32[]{:S(2)}, u32[]{:S(2)}) collective-permute-start(f32[48,256]{1,0:T(8,128)S(1)} %pad_maximum_fusion.7), channel_id=1, source_target_pairs={{2,5},{5,2},{3,4},{4,3},{6,9},{9,6},{7,8},{8,7},{10,13},{13,10},{1... | collective-permute-start | bytes 147464 | tf_op jit(solution)/shard_map/ppermute | solution.py:731
  59.2 5.4 %collective-permute-start.7 = (f32[48,256]{1,0:T(8,128)S(1)}, f32[48,256]{1,0:T(8,128)S(1)}, u32[]{:S(2)}, u32[]{:S(2)}) collective-permute-start(f32[48,256]{1,0:T(8,128)S(1)} %pad_maximum_fusion.6), channel_id=1, source_target_pairs={{0,3},{3,0},{1,2},{2,1},{4,7},{7,4},{5,6},{6,5},{8,11},{11,8},{9,1... | collective-permute-start | bytes 147464 | tf_op jit(solution)/shard_map/ppermute | solution.py:732
